TPU v7x, 512 devices: a whole 4x8x8 slice. The times are simulated.
512 devices in a mesh: txt: 16 (over y_hi, z), aud: 32 (over x, y_lo, core).
Axes of the slice: x: 4, y: 8 (y_hi: 2, y_lo: 4; y = y_hi * 4 + y_lo), z: 8, core: 2. Of those that a mesh axis runs over, the one named last changes fastest.
Arguments:
- images: float32 [131072, 1024], P(('txt', 'aud')), may hold values from -2 to 2
- texts: float32 [256, 1024], P('txt'), may hold values from -2 to 2
- audio: float32 [128, 1024], P('aud'), may hold values from -2 to 2
- pos_text: int32 [131072], P(('txt', 'aud')), may hold values from 0 to 255
- pos_audio: int32 [131072], P(('txt', 'aud')), may hold values from 0 to 11
- logit_scale: float32 [1], replicated, may hold values from 1 to 4
- logit_bias: float32 [1], replicated, may hold values from -3 to -1
Outputs:
- grad_images: float32 [131072, 1024], P(('txt', 'aud'))
- grad_texts: float32 [256, 1024], P('txt')
- grad_audio: float32 [128, 1024], P('aud')
All inputs are finite; a program needn't handle non-finite values.
Results may differ from a plain program's by a relative error of at most 0.0044.
Values sent between devices are 32-bit elements; how exact they have to be, the bound alone decides.
No kernel may reach another device: no remote copies, remote signals or barrier semaphores. Data moves between devices by JAX's collectives and lax.ppermute only.
A program may use at most 64 MiB of HBM per device.

v0:
```python
import jax
import jax.numpy as jnp
from jax import lax
from jax.sharding import PartitionSpec as P

HOPS = 2


def from_behind(shard, axis, by):
    size = lax.axis_size(axis)
    return lax.ppermute(shard, axis, [(i, (i + by) % size) for i in range(size)])


def block_terms(image_half, text_piece, window, first_row, pos_text, pos_audio, temper, offset):
    row_count = text_piece.shape[0]
    slot_count = window.shape[0]
    products = (
        (text_piece[:, None, :] * window[None, :, :])
        .reshape(row_count * slot_count, -1)
        .astype(jnp.bfloat16)
    )
    logits = (
        temper
        * lax.dot_general(
            image_half, products, (((1,), (1,)), ((), ())), preferred_element_type=jnp.float32
        )
        + offset
    )
    columns = jnp.arange(row_count * slot_count, dtype=jnp.int32)
    text_of = first_row + columns // slot_count
    slot_of = columns % slot_count
    positive = (text_of[None, :] == pos_text[:, None]) & (slot_of[None, :] == pos_audio[:, None])
    slope = ((jax.nn.sigmoid(logits) - positive.astype(jnp.float32)) * temper).astype(jnp.bfloat16)
    grad_image = jnp.dot(slope, products, preferred_element_type=jnp.float32)
    grad_prod = lax.dot_general(
        slope, image_half, (((0,), (0,)), ((), ())), preferred_element_type=jnp.float32
    )
    grad_prod = grad_prod.reshape(row_count, slot_count, -1)
    grad_piece = jnp.sum(grad_prod * window[None, :, :], axis=1)
    grad_window = jnp.sum(grad_prod * text_piece[:, None, :], axis=0)
    return (grad_image, grad_piece, grad_window)


def send_home(grad_window, block_rows):
    carried = grad_window[HOPS * block_rows :]
    for number in range(HOPS):
        level = HOPS - 1 - number
        carried = (
            from_behind(carried, "aud", 1)
            + grad_window[level * block_rows : (level + 1) * block_rows]
        )
    return carried


def shards(images, texts, audio, pos_text, pos_audio, logit_scale, logit_bias):
    temper = logit_scale[0]
    offset = logit_bias[0]
    block_rows = audio.shape[0]
    text_rows = texts.shape[0]
    pieces = [audio]
    current = audio
    for number in range(HOPS):
        current = from_behind(current, "aud", -1)
        pieces.append(current)
    window = jnp.concatenate(pieces, axis=0)
    image_half = images.astype(jnp.bfloat16)
    cycle_size = lax.axis_size("txt")
    position = lax.axis_index("txt")
    empty_image = jnp.zeros(images.shape, jnp.float32)
    empty_window = jnp.zeros(window.shape, jnp.float32)

    def advance(turn_index, state):
        held_text, held_grad, grad_image, grad_window = state
        owner = (position - turn_index) % cycle_size
        first = owner * text_rows
        more_image, more_piece, more_window = block_terms(
            image_half, held_text, window, first, pos_text, pos_audio, temper, offset
        )
        held_text, held_grad = from_behind((held_text, held_grad + more_piece), "txt", 1)
        return (held_text, held_grad, grad_image + more_image, grad_window + more_window)

    start_state = (texts, jnp.zeros(texts.shape, jnp.float32), empty_image, empty_window)
    final_state = lax.fori_loop(0, cycle_size, advance, start_state)
    grad_local_text = final_state[1]
    grad_images = final_state[2]
    grad_window = final_state[3]
    grad_texts = lax.psum(grad_local_text, "aud")
    summed_window = lax.psum(grad_window, "txt")
    grad_audio = send_home(summed_window, block_rows)
    return (grad_images, grad_texts, grad_audio)


def solution(mesh):
    placed = (
        P(("txt", "aud"), None),
        P("txt", None),
        P("aud", None),
        P(("txt", "aud")),
        P(("txt", "aud")),
        P(),
        P(),
    )
    return jax.shard_map(
        shards,
        mesh=mesh,
        in_specs=placed,
        out_specs=(P(("txt", "aud"), None), P("txt", None), P("aud", None)),
        check_vma=False,
    )
```

profile of v0, /device:TPU:1, one launch (start us, length us, event | category | flops | bytes accessed | tf_op | source)
XLA Modules:
  0.0 683.4 jit_solution(6114707449579966862)
XLA Ops:
  8.7 8.8 %collective-permute-start.2 = (f32[4,1024]{1,0:T(4,128)S(1)}, f32[4,1024]{1,0:T(4,128)S(1)}, u32[]{:S(2)}, u32[]{:S(2)}) collective-permute-start(f32[4,1024]{1,0:T(4,128)S(1)} %copy-done.3), channel_id=1, source_target_pairs={{0,31},{1,0},{2,1},{3,2},{4,3},{5,4},{6,5},{7,6},{8,7},{9,8},{10,9... | collective-permute-start | bytes 49160 | tf_op jit(solution)/shard_map/ppermute | solution.py:11
  18.3 2.5 collective-permute-start.3
  24.1 298.1 %while.23 = (s32[]{:T(128)}, f32[16,1024]{1,0:T(8,128)}, f32[16,1024]{1,0:T(8,128)}, f32[256,1024]{1,0:T(8,128)S(1)}, f32[12,1024]{1,0:T(8,128)}, /*index=5*/f32...) while((s32[]{:T(128)}, f32[16,1024]{1,0:T(8,128)}, ...), condition=%wide.region_3.4_spmd.clone, body=%wide.region_0.3_spmd.clone.sunk | while | flops 304298432 | bytes 14095801 | solution.py:83
  25.0 2.7 collective-permute-start
  31.0 4.0 collective-permute-start.1
  36.1 3.6 collective-permute-done
  39.7 6.6 collective-permute-done.1
  52.5 1.9 collective-permute-start.1
  56.4 2.0 collective-permute-done
  58.4 6.1 collective-permute-done.1
  70.7 1.9 collective-permute-start.1
  74.6 2.6 collective-permute-done
  77.2 5.7 collective-permute-done.1
  89.1 1.9 collective-permute-start.1
  93.0 2.8 collective-permute-done
  95.7 5.7 collective-permute-done.1
  107.6 1.9 collective-permute-start.1
  111.5 3.4 collective-permute-done
  114.8 5.1 collective-permute-done.1
  130.0 3.4 collective-permute-done
  133.3 5.1 collective-permute-done.1
  148.5 3.0 collective-permute-done
  151.5 5.4 collective-permute-done.1
  167.0 2.0 collective-permute-done
  168.9 6.5 collective-permute-done.1
  185.5 2.0 collective-permute-done
  187.5 6.7 collective-permute-done.1
  204.2 2.0 collective-permute-done
  206.1 6.8 collective-permute-done.1
  223.0 2.0 collective-permute-done
  224.9 7.0 %collective-permute-done.1 = f32[16,1024]{1,0:T(8,128)} collective-permute-done((f32[16,1024]{1,0:T(8,128)S(1)}, f32[16,1024]{1,0:T(8,128)}, u32[]{:S(2)}, u32[]{:S(2)}) %collective-permute-start.1) | collective-permute-done | bytes 65568 | tf_op jit(solution)/shard_map/while/body/eval_jaxpr/ppermute | solution.py:11
  242.0 2.7 collective-permute-done
  244.6 6.2 collective-permute-done.1
  260.9 2.7 collective-permute-done
  263.6 4.9 collective-permute-done.1
  278.5 2.0 collective-permute-done
  280.5 5.9 collective-permute-done.1
  296.4 2.0 collective-permute-done
  298.4 6.3 collective-permute-done.1
  310.9 1.9 collective-permute-start.1
  314.8 2.1 collective-permute-done
  316.8 5.3 collective-permute-done.1
  322.2 79.2 %psum.15 = f32[12,1024]{1,0:T(8,128)S(1)} all-reduce(f32[12,1024]{1,0:T(8,128)} %get-tuple-element.335), channel_id=1, replica_groups=mesh['txt'=16,'aud'=32] {'txt'}, use_global_device_ids=true, to_apply=%region_5.6 | all-reduce | flops 12288 | bytes 98304 | tf_op jit(solution)/shard_map/psum | solution.py:88
  401.4 19.2 %collective-permute-start.4 = (f32[4,1024]{1,0:T(4,128)S(1)}, f32[4,1024]{1,0:T(4,128)S(1)}, u32[]{:S(2)}, u32[]{:S(2)}) collective-permute-start(f32[4,1024]{1,0:T(4,128)S(1)} %slice.12), channel_id=1, source_target_pairs={{0,1},{1,2},{2,3},{3,4},{4,5},{5,6},{6,7},{7,8},{8,9},{9,10},{10,1... | collective-permute-start | bytes 49160 | tf_op jit(solution)/shard_map/ppermute | solution.py:11
  420.6 5.4 collective-permute-done.4
  426.0 1.9 collective-permute-start.5
  427.9 7.0 %collective-permute-done.5 = f32[4,1024]{1,0:T(4,128)S(1)} collective-permute-done((f32[4,1024]{1,0:T(4,128)S(1)}, f32[4,1024]{1,0:T(4,128)S(1)}, u32[]{:S(2)}, u32[]{:S(2)}) %collective-permute-start.5) | collective-permute-done | bytes 16416 | tf_op jit(solution)/shard_map/ppermute | solution.py:11
  435.6 239.5 %all-reduce.2.cloned.1.call-done = f32[16,1024]{1,0:T(8,128)} async-done(((f32[16,1024]{1,0:T(8,128)}), f32[16,1024]{1,0:T(8,128)}) %all-reduce.2.cloned.1.call-update) | async-done | bytes 65552 | tf_op jit(solution)/shard_map/psum | solution.py:87
  (287 shorter events, 152.5 us)
Async XLA Ops:
  7.2 667.9 %all-reduce.2.cloned.1.call-start = ((), (), s32[]{:S(2)}) async-start(), calls=%async_computation | async-start | bytes 131072 | tf_op jit(solution)/shard_map/psum | solution.py:87
  8.7 9.6 %collective-permute-start.2 = (f32[4,1024]{1,0:T(4,128)S(1)}, f32[4,1024]{1,0:T(4,128)S(1)}, u32[]{:S(2)}, u32[]{:S(2)}) collective-permute-start(f32[4,1024]{1,0:T(4,128)S(1)} %copy-done.3), channel_id=1, source_target_pairs={{0,31},{1,0},{2,1},{3,2},{4,3},{5,4},{6,5},{7,6},{8,7},{9,8},{10,9... | collective-permute-start | bytes 49160 | tf_op jit(solution)/shard_map/ppermute | solution.py:11
  18.3 5.0 collective-permute-start.3
  25.0 14.7 %collective-permute-start = (f32[16,1024]{1,0:T(8,128)S(1)}, f32[16,1024]{1,0:T(8,128)}, u32[]{:S(2)}, u32[]{:S(2)}) collective-permute-start(f32[16,1024]{1,0:T(8,128)S(1)} %copy.16), channel_id=1, source_target_pairs={{0,32},{32,64},{64,96},{96,128},{128,160},{160,192},{192,224},{224... | collective-permute-start | bytes 196616 | tf_op jit(solution)/shard_map/while/body/eval_jaxpr/ppermute | solution.py:11
  31.0 15.3 %collective-permute-start.1 = (f32[16,1024]{1,0:T(8,128)S(1)}, f32[16,1024]{1,0:T(8,128)}, u32[]{:S(2)}, u32[]{:S(2)}) collective-permute-start(f32[16,1024]{1,0:T(8,128)S(1)} %add.228), channel_id=1, source_target_pairs={{0,32},{32,64},{64,96},{96,128},{128,160},{160,192},{192,224},{224... | collective-permute-start | bytes 196616 | tf_op jit(solution)/shard_map/while/body/eval_jaxpr/ppermute | solution.py:11
  35.0 11.3 %copy-start.2 = (bf16[256,1024]{1,0:T(8,128)(2,1)S(1)}, bf16[256,1024]{1,0:T(8,128)(2,1)}, u32[]{:S(2)}) copy-start(bf16[256,1024]{1,0:T(8,128)(2,1)} %copy-done.1) | copy-start | bytes 1572868 | tf_op jit(solution)/shard_map/while
  47.2 11.2 %collective-permute-start = (f32[16,1024]{1,0:T(8,128)S(1)}, f32[16,1024]{1,0:T(8,128)}, u32[]{:S(2)}, u32[]{:S(2)}) collective-permute-start(f32[16,1024]{1,0:T(8,128)S(1)} %copy.16), channel_id=1, source_target_pairs={{0,32},{32,64},{64,96},{96,128},{128,160},{160,192},{192,224},{224... | collective-permute-start | bytes 196616 | tf_op jit(solution)/shard_map/while/body/eval_jaxpr/ppermute | solution.py:11
  52.5 12.0 %collective-permute-start.1 = (f32[16,1024]{1,0:T(8,128)S(1)}, f32[16,1024]{1,0:T(8,128)}, u32[]{:S(2)}, u32[]{:S(2)}) collective-permute-start(f32[16,1024]{1,0:T(8,128)S(1)} %add.228), channel_id=1, source_target_pairs={{0,32},{32,64},{64,96},{96,128},{128,160},{160,192},{192,224},{224... | collective-permute-start | bytes 196616 | tf_op jit(solution)/shard_map/while/body/eval_jaxpr/ppermute | solution.py:11
  65.4 11.8 %collective-permute-start = (f32[16,1024]{1,0:T(8,128)S(1)}, f32[16,1024]{1,0:T(8,128)}, u32[]{:S(2)}, u32[]{:S(2)}) collective-permute-start(f32[16,1024]{1,0:T(8,128)S(1)} %copy.16), channel_id=1, source_target_pairs={{0,32},{32,64},{64,96},{96,128},{128,160},{160,192},{192,224},{224... | collective-permute-start | bytes 196616 | tf_op jit(solution)/shard_map/while/body/eval_jaxpr/ppermute | solution.py:11
  70.7 12.2 %collective-permute-start.1 = (f32[16,1024]{1,0:T(8,128)S(1)}, f32[16,1024]{1,0:T(8,128)}, u32[]{:S(2)}, u32[]{:S(2)}) collective-permute-start(f32[16,1024]{1,0:T(8,128)S(1)} %add.228), channel_id=1, source_target_pairs={{0,32},{32,64},{64,96},{96,128},{128,160},{160,192},{192,224},{224... | collective-permute-start | bytes 196616 | tf_op jit(solution)/shard_map/while/body/eval_jaxpr/ppermute | solution.py:11
  83.8 11.9 %collective-permute-start = (f32[16,1024]{1,0:T(8,128)S(1)}, f32[16,1024]{1,0:T(8,128)}, u32[]{:S(2)}, u32[]{:S(2)}) collective-permute-start(f32[16,1024]{1,0:T(8,128)S(1)} %copy.16), channel_id=1, source_target_pairs={{0,32},{32,64},{64,96},{96,128},{128,160},{160,192},{192,224},{224... | collective-permute-start | bytes 196616 | tf_op jit(solution)/shard_map/while/body/eval_jaxpr/ppermute | solution.py:11
  89.1 12.3 %collective-permute-start.1 = (f32[16,1024]{1,0:T(8,128)S(1)}, f32[16,1024]{1,0:T(8,128)}, u32[]{:S(2)}, u32[]{:S(2)}) collective-permute-start(f32[16,1024]{1,0:T(8,128)S(1)} %add.228), channel_id=1, source_target_pairs={{0,32},{32,64},{64,96},{96,128},{128,160},{160,192},{192,224},{224... | collective-permute-start | bytes 196616 | tf_op jit(solution)/shard_map/while/body/eval_jaxpr/ppermute | solution.py:11
  91.1 10.4 %copy-start.2 = (bf16[256,1024]{1,0:T(8,128)(2,1)S(1)}, bf16[256,1024]{1,0:T(8,128)(2,1)}, u32[]{:S(2)}) copy-start(bf16[256,1024]{1,0:T(8,128)(2,1)} %copy-done.1) | copy-start | bytes 1572868 | tf_op jit(solution)/shard_map/while
  102.3 12.5 %collective-permute-start = (f32[16,1024]{1,0:T(8,128)S(1)}, f32[16,1024]{1,0:T(8,128)}, u32[]{:S(2)}, u32[]{:S(2)}) collective-permute-start(f32[16,1024]{1,0:T(8,128)S(1)} %copy.16), channel_id=1, source_target_pairs={{0,32},{32,64},{64,96},{96,128},{128,160},{160,192},{192,224},{224... | collective-permute-start | bytes 196616 | tf_op jit(solution)/shard_map/while/body/eval_jaxpr/ppermute | solution.py:11
  107.6 12.3 %collective-permute-start.1 = (f32[16,1024]{1,0:T(8,128)S(1)}, f32[16,1024]{1,0:T(8,128)}, u32[]{:S(2)}, u32[]{:S(2)}) collective-permute-start(f32[16,1024]{1,0:T(8,128)S(1)} %add.228), channel_id=1, source_target_pairs={{0,32},{32,64},{64,96},{96,128},{128,160},{160,192},{192,224},{224... | collective-permute-start | bytes 196616 | tf_op jit(solution)/shard_map/while/body/eval_jaxpr/ppermute | solution.py:11
  109.6 10.3 %copy-start.2 = (bf16[256,1024]{1,0:T(8,128)(2,1)S(1)}, bf16[256,1024]{1,0:T(8,128)(2,1)}, u32[]{:S(2)}) copy-start(bf16[256,1024]{1,0:T(8,128)(2,1)} %copy-done.1) | copy-start | bytes 1572868 | tf_op jit(solution)/shard_map/while
  120.8 12.5 %collective-permute-start = (f32[16,1024]{1,0:T(8,128)S(1)}, f32[16,1024]{1,0:T(8,128)}, u32[]{:S(2)}, u32[]{:S(2)}) collective-permute-start(f32[16,1024]{1,0:T(8,128)S(1)} %copy.16), channel_id=1, source_target_pairs={{0,32},{32,64},{64,96},{96,128},{128,160},{160,192},{192,224},{224... | collective-permute-start | bytes 196616 | tf_op jit(solution)/shard_map/while/body/eval_jaxpr/ppermute | solution.py:11
  126.1 12.3 %collective-permute-start.1 = (f32[16,1024]{1,0:T(8,128)S(1)}, f32[16,1024]{1,0:T(8,128)}, u32[]{:S(2)}, u32[]{:S(2)}) collective-permute-start(f32[16,1024]{1,0:T(8,128)S(1)} %add.228), channel_id=1, source_target_pairs={{0,32},{32,64},{64,96},{96,128},{128,160},{160,192},{192,224},{224... | collective-permute-start | bytes 196616 | tf_op jit(solution)/shard_map/while/body/eval_jaxpr/ppermute | solution.py:11
  128.1 10.4 %copy-start.2 = (bf16[256,1024]{1,0:T(8,128)(2,1)S(1)}, bf16[256,1024]{1,0:T(8,128)(2,1)}, u32[]{:S(2)}) copy-start(bf16[256,1024]{1,0:T(8,128)(2,1)} %copy-done.1) | copy-start | bytes 1572868 | tf_op jit(solution)/shard_map/while
  139.3 12.2 %collective-permute-start = (f32[16,1024]{1,0:T(8,128)S(1)}, f32[16,1024]{1,0:T(8,128)}, u32[]{:S(2)}, u32[]{:S(2)}) collective-permute-start(f32[16,1024]{1,0:T(8,128)S(1)} %copy.16), channel_id=1, source_target_pairs={{0,32},{32,64},{64,96},{96,128},{128,160},{160,192},{192,224},{224... | collective-permute-start | bytes 196616 | tf_op jit(solution)/shard_map/while/body/eval_jaxpr/ppermute | solution.py:11
  144.6 12.3 %collective-permute-start.1 = (f32[16,1024]{1,0:T(8,128)S(1)}, f32[16,1024]{1,0:T(8,128)}, u32[]{:S(2)}, u32[]{:S(2)}) collective-permute-start(f32[16,1024]{1,0:T(8,128)S(1)} %add.228), channel_id=1, source_target_pairs={{0,32},{32,64},{64,96},{96,128},{128,160},{160,192},{192,224},{224... | collective-permute-start | bytes 196616 | tf_op jit(solution)/shard_map/while/body/eval_jaxpr/ppermute | solution.py:11
  146.6 10.3 %copy-start.2 = (bf16[256,1024]{1,0:T(8,128)(2,1)S(1)}, bf16[256,1024]{1,0:T(8,128)(2,1)}, u32[]{:S(2)}) copy-start(bf16[256,1024]{1,0:T(8,128)(2,1)} %copy-done.1) | copy-start | bytes 1572868 | tf_op jit(solution)/shard_map/while
  157.8 11.1 %collective-permute-start = (f32[16,1024]{1,0:T(8,128)S(1)}, f32[16,1024]{1,0:T(8,128)}, u32[]{:S(2)}, u32[]{:S(2)}) collective-permute-start(f32[16,1024]{1,0:T(8,128)S(1)} %copy.16), channel_id=1, source_target_pairs={{0,32},{32,64},{64,96},{96,128},{128,160},{160,192},{192,224},{224... | collective-permute-start | bytes 196616 | tf_op jit(solution)/shard_map/while/body/eval_jaxpr/ppermute | solution.py:11
  163.1 12.3 %collective-permute-start.1 = (f32[16,1024]{1,0:T(8,128)S(1)}, f32[16,1024]{1,0:T(8,128)}, u32[]{:S(2)}, u32[]{:S(2)}) collective-permute-start(f32[16,1024]{1,0:T(8,128)S(1)} %add.228), channel_id=1, source_target_pairs={{0,32},{32,64},{64,96},{96,128},{128,160},{160,192},{192,224},{224... | collective-permute-start | bytes 196616 | tf_op jit(solution)/shard_map/while/body/eval_jaxpr/ppermute | solution.py:11
  165.1 10.4 %copy-start.2 = (bf16[256,1024]{1,0:T(8,128)(2,1)S(1)}, bf16[256,1024]{1,0:T(8,128)(2,1)}, u32[]{:S(2)}) copy-start(bf16[256,1024]{1,0:T(8,128)(2,1)} %copy-done.1) | copy-start | bytes 1572868 | tf_op jit(solution)/shard_map/while
  176.3 11.1 %collective-permute-start = (f32[16,1024]{1,0:T(8,128)S(1)}, f32[16,1024]{1,0:T(8,128)}, u32[]{:S(2)}, u32[]{:S(2)}) collective-permute-start(f32[16,1024]{1,0:T(8,128)S(1)} %copy.16), channel_id=1, source_target_pairs={{0,32},{32,64},{64,96},{96,128},{128,160},{160,192},{192,224},{224... | collective-permute-start | bytes 196616 | tf_op jit(solution)/shard_map/while/body/eval_jaxpr/ppermute | solution.py:11
  181.7 12.5 %collective-permute-start.1 = (f32[16,1024]{1,0:T(8,128)S(1)}, f32[16,1024]{1,0:T(8,128)}, u32[]{:S(2)}, u32[]{:S(2)}) collective-permute-start(f32[16,1024]{1,0:T(8,128)S(1)} %add.228), channel_id=1, source_target_pairs={{0,32},{32,64},{64,96},{96,128},{128,160},{160,192},{192,224},{224... | collective-permute-start | bytes 196616 | tf_op jit(solution)/shard_map/while/body/eval_jaxpr/ppermute | solution.py:11
  183.6 10.5 %copy-start.2 = (bf16[256,1024]{1,0:T(8,128)(2,1)S(1)}, bf16[256,1024]{1,0:T(8,128)(2,1)}, u32[]{:S(2)}) copy-start(bf16[256,1024]{1,0:T(8,128)(2,1)} %copy-done.1) | copy-start | bytes 1572868 | tf_op jit(solution)/shard_map/while
  195.0 11.1 %collective-permute-start = (f32[16,1024]{1,0:T(8,128)S(1)}, f32[16,1024]{1,0:T(8,128)}, u32[]{:S(2)}, u32[]{:S(2)}) collective-permute-start(f32[16,1024]{1,0:T(8,128)S(1)} %copy.16), channel_id=1, source_target_pairs={{0,32},{32,64},{64,96},{96,128},{128,160},{160,192},{192,224},{224... | collective-permute-start | bytes 196616 | tf_op jit(solution)/shard_map/while/body/eval_jaxpr/ppermute | solution.py:11
  200.4 12.6 %collective-permute-start.1 = (f32[16,1024]{1,0:T(8,128)S(1)}, f32[16,1024]{1,0:T(8,128)}, u32[]{:S(2)}, u32[]{:S(2)}) collective-permute-start(f32[16,1024]{1,0:T(8,128)S(1)} %add.228), channel_id=1, source_target_pairs={{0,32},{32,64},{64,96},{96,128},{128,160},{160,192},{192,224},{224... | collective-permute-start | bytes 196616 | tf_op jit(solution)/shard_map/while/body/eval_jaxpr/ppermute | solution.py:11
  202.3 10.6 %copy-start.2 = (bf16[256,1024]{1,0:T(8,128)(2,1)S(1)}, bf16[256,1024]{1,0:T(8,128)(2,1)}, u32[]{:S(2)}) copy-start(bf16[256,1024]{1,0:T(8,128)(2,1)} %copy-done.1) | copy-start | bytes 1572868 | tf_op jit(solution)/shard_map/while
  213.8 11.1 %collective-permute-start = (f32[16,1024]{1,0:T(8,128)S(1)}, f32[16,1024]{1,0:T(8,128)}, u32[]{:S(2)}, u32[]{:S(2)}) collective-permute-start(f32[16,1024]{1,0:T(8,128)S(1)} %copy.16), channel_id=1, source_target_pairs={{0,32},{32,64},{64,96},{96,128},{128,160},{160,192},{192,224},{224... | collective-permute-start | bytes 196616 | tf_op jit(solution)/shard_map/while/body/eval_jaxpr/ppermute | solution.py:11
  219.1 12.8 %collective-permute-start.1 = (f32[16,1024]{1,0:T(8,128)S(1)}, f32[16,1024]{1,0:T(8,128)}, u32[]{:S(2)}, u32[]{:S(2)}) collective-permute-start(f32[16,1024]{1,0:T(8,128)S(1)} %add.228), channel_id=1, source_target_pairs={{0,32},{32,64},{64,96},{96,128},{128,160},{160,192},{192,224},{224... | collective-permute-start | bytes 196616 | tf_op jit(solution)/shard_map/while/body/eval_jaxpr/ppermute | solution.py:11
  221.1 10.8 %copy-start.2 = (bf16[256,1024]{1,0:T(8,128)(2,1)S(1)}, bf16[256,1024]{1,0:T(8,128)(2,1)}, u32[]{:S(2)}) copy-start(bf16[256,1024]{1,0:T(8,128)(2,1)} %copy-done.1) | copy-start | bytes 1572868 | tf_op jit(solution)/shard_map/while
  232.8 11.8 %collective-permute-start = (f32[16,1024]{1,0:T(8,128)S(1)}, f32[16,1024]{1,0:T(8,128)}, u32[]{:S(2)}, u32[]{:S(2)}) collective-permute-start(f32[16,1024]{1,0:T(8,128)S(1)} %copy.16), channel_id=1, source_target_pairs={{0,32},{32,64},{64,96},{96,128},{128,160},{160,192},{192,224},{224... | collective-permute-start | bytes 196616 | tf_op jit(solution)/shard_map/while/body/eval_jaxpr/ppermute | solution.py:11
  238.1 12.7 %collective-permute-start.1 = (f32[16,1024]{1,0:T(8,128)S(1)}, f32[16,1024]{1,0:T(8,128)}, u32[]{:S(2)}, u32[]{:S(2)}) collective-permute-start(f32[16,1024]{1,0:T(8,128)S(1)} %add.228), channel_id=1, source_target_pairs={{0,32},{32,64},{64,96},{96,128},{128,160},{160,192},{192,224},{224... | collective-permute-start | bytes 196616 | tf_op jit(solution)/shard_map/while/body/eval_jaxpr/ppermute | solution.py:11
  240.1 10.8 %copy-start.2 = (bf16[256,1024]{1,0:T(8,128)(2,1)S(1)}, bf16[256,1024]{1,0:T(8,128)(2,1)}, u32[]{:S(2)}) copy-start(bf16[256,1024]{1,0:T(8,128)(2,1)} %copy-done.1) | copy-start | bytes 1572868 | tf_op jit(solution)/shard_map/while
  251.8 11.8 %collective-permute-start = (f32[16,1024]{1,0:T(8,128)S(1)}, f32[16,1024]{1,0:T(8,128)}, u32[]{:S(2)}, u32[]{:S(2)}) collective-permute-start(f32[16,1024]{1,0:T(8,128)S(1)} %copy.16), channel_id=1, source_target_pairs={{0,32},{32,64},{64,96},{96,128},{128,160},{160,192},{192,224},{224... | collective-permute-start | bytes 196616 | tf_op jit(solution)/shard_map/while/body/eval_jaxpr/ppermute | solution.py:11
  257.1 11.3 %collective-permute-start.1 = (f32[16,1024]{1,0:T(8,128)S(1)}, f32[16,1024]{1,0:T(8,128)}, u32[]{:S(2)}, u32[]{:S(2)}) collective-permute-start(f32[16,1024]{1,0:T(8,128)S(1)} %add.228), channel_id=1, source_target_pairs={{0,32},{32,64},{64,96},{96,128},{128,160},{160,192},{192,224},{224... | collective-permute-start | bytes 196616 | tf_op jit(solution)/shard_map/while/body/eval_jaxpr/ppermute | solution.py:11
  269.3 11.1 %collective-permute-start = (f32[16,1024]{1,0:T(8,128)S(1)}, f32[16,1024]{1,0:T(8,128)}, u32[]{:S(2)}, u32[]{:S(2)}) collective-permute-start(f32[16,1024]{1,0:T(8,128)S(1)} %copy.16), channel_id=1, source_target_pairs={{0,32},{32,64},{64,96},{96,128},{128,160},{160,192},{192,224},{224... | collective-permute-start | bytes 196616 | tf_op jit(solution)/shard_map/while/body/eval_jaxpr/ppermute | solution.py:11
  274.7 11.7 %collective-permute-start.1 = (f32[16,1024]{1,0:T(8,128)S(1)}, f32[16,1024]{1,0:T(8,128)}, u32[]{:S(2)}, u32[]{:S(2)}) collective-permute-start(f32[16,1024]{1,0:T(8,128)S(1)} %add.228), channel_id=1, source_target_pairs={{0,32},{32,64},{64,96},{96,128},{128,160},{160,192},{192,224},{224... | collective-permute-start | bytes 196616 | tf_op jit(solution)/shard_map/while/body/eval_jaxpr/ppermute | solution.py:11
  287.2 11.1 %collective-permute-start = (f32[16,1024]{1,0:T(8,128)S(1)}, f32[16,1024]{1,0:T(8,128)}, u32[]{:S(2)}, u32[]{:S(2)}) collective-permute-start(f32[16,1024]{1,0:T(8,128)S(1)} %copy.16), channel_id=1, source_target_pairs={{0,32},{32,64},{64,96},{96,128},{128,160},{160,192},{192,224},{224... | collective-permute-start | bytes 196616 | tf_op jit(solution)/shard_map/while/body/eval_jaxpr/ppermute | solution.py:11
  292.6 12.1 %collective-permute-start.1 = (f32[16,1024]{1,0:T(8,128)S(1)}, f32[16,1024]{1,0:T(8,128)}, u32[]{:S(2)}, u32[]{:S(2)}) collective-permute-start(f32[16,1024]{1,0:T(8,128)S(1)} %add.228), channel_id=1, source_target_pairs={{0,32},{32,64},{64,96},{96,128},{128,160},{160,192},{192,224},{224... | collective-permute-start | bytes 196616 | tf_op jit(solution)/shard_map/while/body/eval_jaxpr/ppermute | solution.py:11
  305.6 11.2 %collective-permute-start = (f32[16,1024]{1,0:T(8,128)S(1)}, f32[16,1024]{1,0:T(8,128)}, u32[]{:S(2)}, u32[]{:S(2)}) collective-permute-start(f32[16,1024]{1,0:T(8,128)S(1)} %copy.16), channel_id=1, source_target_pairs={{0,32},{32,64},{64,96},{96,128},{128,160},{160,192},{192,224},{224... | collective-permute-start | bytes 196616 | tf_op jit(solution)/shard_map/while/body/eval_jaxpr/ppermute | solution.py:11
  310.9 11.2 %collective-permute-start.1 = (f32[16,1024]{1,0:T(8,128)S(1)}, f32[16,1024]{1,0:T(8,128)}, u32[]{:S(2)}, u32[]{:S(2)}) collective-permute-start(f32[16,1024]{1,0:T(8,128)S(1)} %add.228), channel_id=1, source_target_pairs={{0,32},{32,64},{64,96},{96,128},{128,160},{160,192},{192,224},{224... | collective-permute-start | bytes 196616 | tf_op jit(solution)/shard_map/while/body/eval_jaxpr/ppermute | solution.py:11
  322.2 354.4 %copy-start = (f32[256,1024]{1,0:T(8,128)}, f32[256,1024]{1,0:T(8,128)S(1)}, u32[]{:S(2)}) copy-start(f32[256,1024]{1,0:T(8,128)S(1)} %get-tuple-element.535) | copy-start | bytes 3145732
  401.4 24.6 %collective-permute-start.4 = (f32[4,1024]{1,0:T(4,128)S(1)}, f32[4,1024]{1,0:T(4,128)S(1)}, u32[]{:S(2)}, u32[]{:S(2)}) collective-permute-start(f32[4,1024]{1,0:T(4,128)S(1)} %slice.12), channel_id=1, source_target_pairs={{0,1},{1,2},{2,3},{3,4},{4,5},{5,6},{6,7},{7,8},{8,9},{9,10},{10,1... | collective-permute-start | bytes 49160 | tf_op jit(solution)/shard_map/ppermute | solution.py:11
  426.0 9.0 %collective-permute-start.5 = (f32[4,1024]{1,0:T(4,128)S(1)}, f32[4,1024]{1,0:T(4,128)S(1)}, u32[]{:S(2)}, u32[]{:S(2)}) collective-permute-start(f32[4,1024]{1,0:T(4,128)S(1)} %slice_add_fusion.1), channel_id=1, source_target_pairs={{0,1},{1,2},{2,3},{3,4},{4,5},{5,6},{6,7},{7,8},{8,9},{9,10},{10,1... | collective-permute-start | bytes 49160 | tf_op jit(solution)/shard_map/ppermute | solution.py:11
  (25 other events, 137.7 us)
Sparse Core Ops, SparseCore 0:
  428.1 246.9 all-reduce.1
where the time goes:
time: 688 us; the launch traced here: 683 us
  waiting for transfers between devices  389 us (57%)
  starting transfers between devices  96.5 us (14%)
  blocking collectives  79.2 us (12%)
  other arithmetic  44.6 us (6%)
  matrix products  37.2 us (5%)
  local copies, waits for them, and re-layouts  20.8 us (3%)
  between operations  14.1 us (2%)
    psum x1, waiting for transfers between devices, shards(): grad_texts = lax.psum(grad_local_text, 'aud')  239 us
    ppermute x36, waiting for transfers between devices, from_behind(): lax.ppermute(shard, axis, [(i, (i + by) % size) for i in range(size)])  150 us
    ppermute x36, starting transfers between devices, from_behind(): lax.ppermute(shard, axis, [(i, (i + by) % size) for i in range(size)])  96.5 us
    psum x1, blocking collectives, shards(): summed_window = lax.psum(grad_window, 'txt')  79.2 us
    dot_general x16, matrix products, block_terms(): lax.dot_general(image_half, products, (((1,), (1,)), ((), ())), preferred...  26.6 us
    add x16, other arithmetic, advance(): grad_window + more_window  23 us
    while x80, local copies, waits for them, and re-layouts  14.4 us
  transfers between devices with their start and end apart: 37, of which 37 were waited for; matrix products, arithmetic and copies ran while one was open for 12% of the time, Pallas kernels for 0%

commit v1 on v0

v1 whole, which is shorter than its diff:
```python
import jax
import jax.numpy as jnp
from jax import lax
from jax.experimental import pallas as pl
from jax.experimental.pallas import tpu as pltpu
from jax.sharding import PartitionSpec as P

BOTH = ("txt", "aud")
N_TXT, N_AUD = 16, 32
F32, BF16 = jnp.float32, jnp.bfloat16
VMEM = pl.BlockSpec(memory_space=pltpu.VMEM)
SMEM = pl.BlockSpec(memory_space=pltpu.SMEM)
PARAMS = pltpu.CompilerParams(vmem_limit_bytes=56 * 1024 * 1024)


def device(high, z, x, low, core):
    return (high * 8 + z) * N_AUD + (x * 4 + low) * 2 + core


def groups_by(key):
    found = {}
    for high in range(2):
        for z in range(8):
            for x in range(4):
                for low in range(4):
                    for core in range(2):
                        place = (high, z, x, low, core)
                        found.setdefault(key(*place), []).append(device(*place))
    return [found[k] for k in sorted(found)]


TEXT_GROUPS = groups_by(lambda high, z, x, low, core: (x, low if high == 0 else low ^ 2, core))
CHIP_GROUPS = groups_by(lambda high, z, x, low, core: (high, z, core))

OTHER_CORE = [(i, i ^ 1) for i in range(N_AUD)]
FROM_NEXT = [(i, (i - 2) % N_AUD) for i in range(N_AUD)]
FROM_NEXT_OTHER = [(i, ((i - 2) % N_AUD) ^ 1) for i in range(N_AUD)]
TO_NEXT = [(i, (i + 2) % N_AUD) for i in range(N_AUD)]


def prepare_kernel(core_ref, own_ref, other_ref, own_audio, far_audio, next_own, next_far, half_ref, window_ref):
    core = core_ref[0]
    half_ref[pl.ds(pl.multiple_of(core * 256, 256), 256), :] = own_ref[...].astype(BF16)
    half_ref[pl.ds(pl.multiple_of((1 - core) * 256, 256), 256), :] = other_ref[...].astype(BF16)
    first = core == 0
    a, b = own_audio[...], far_audio[0:4, :]
    window_ref[0:4, :] = jnp.where(first, a, b)
    window_ref[4:8, :] = jnp.where(first, b, a)
    a, b = next_own[...], next_far[...]
    window_ref[8:12, :] = jnp.where(first, a, b)
    window_ref[12:16, :] = jnp.where(first, b, a)


BLOCK_COLUMNS = ((0, 256), (0, 512), (0, 512), (256, 512))


def slope_kernel(
    core_ref, scalar_ref, texts, half_ref, window_ref, own_pos, other_pos,
    slope_ref, text_ref, keep_ref, send_ref, products, audio_sum,
):
    core = core_ref[0]
    temper, offset = scalar_ref[0], scalar_ref[1]
    own, other = own_pos[...], other_pos[...]
    positions = jnp.where(
        core == 0,
        jnp.concatenate([own, other], axis=1),
        jnp.concatenate([other, own], axis=1),
    )
    text_pos, slot_pos = positions[0:1, :], positions[1:2, :]
    rest = text_pos & 15
    row = (text_pos >> 4) * 8 + (rest & 7)
    block_of_image = lax.broadcasted_iota(jnp.int32, (1, 512), 1) // 256
    place = (slot_pos + block_of_image * 4) * 128 + row
    place = jnp.where((rest >> 3) == core, place, -1)

    def logits_of(block):
        low, high = BLOCK_COLUMNS[block]
        for w in range(4):
            slot = block * 4 + w
            products[slot * 128 : (slot + 1) * 128, :] = (
                texts[...] * window_ref[slot : slot + 1, :]
            ).astype(BF16)
        return lax.dot_general(
            products[block * 512 : (block + 1) * 512, :],
            half_ref[low:high, :],
            (((1,), (1,)), ((), ())),
            preferred_element_type=F32,
        )

    def slope_of(block, dots):
        low, high = BLOCK_COLUMNS[block]
        rows = lax.broadcasted_iota(jnp.int32, dots.shape, 0) + block * 512
        positive = rows == place[:, low:high]
        value = jax.nn.sigmoid(temper * dots + offset)
        slope = (temper * jnp.where(positive, value - 1.0, value)).astype(BF16)
        slope_ref[block * 512 : (block + 1) * 512, low:high] = slope
        return slope

    def grads_of(block, slope):
        low, high = BLOCK_COLUMNS[block]
        grads = jnp.dot(slope, half_ref[low:high, :], preferred_element_type=F32)
        part = None
        for w in range(4):
            slot = block * 4 + w
            grad = grads[w * 128 : (w + 1) * 128, :]
            more = grad * window_ref[slot : slot + 1, :]
            part = more if part is None else part + more
            audio_sum[slot : slot + 1, :] = jnp.sum(grad * texts[...], axis=0, keepdims=True)
        return part

    dots = logits_of(0)
    total = None
    for block in range(4):
        slope = slope_of(block, dots)
        if block < 3:
            dots = logits_of(block + 1)
        part = grads_of(block, slope)
        total = part if total is None else total + part
    for c in range(8):
        tiles = total[:, c * 128 : (c + 1) * 128].reshape(16, 8, 128)
        text_ref[c * 2] = tiles[:, 0:4, :]
        text_ref[c * 2 + 1] = tiles[:, 4:8, :]
    first = core == 0
    for level in range(2):
        even = audio_sum[level * 8 : level * 8 + 4, :]
        odd = audio_sum[level * 8 + 4 : level * 8 + 8, :]
        keep_ref[level * 4 : level * 4 + 4, :] = jnp.where(first, even, odd)
        send_ref[level * 4 : level * 4 + 4, :] = jnp.where(first, odd, even)


def image_kernel(core_ref, texts, window_ref, slope_ref, own_ref, other_ref, products):
    core = core_ref[0]
    for slot in range(16):
        products[slot * 128 : (slot + 1) * 128, :] = (
            texts[...] * window_ref[slot : slot + 1, :]
        ).astype(BF16)
    grads = [
        lax.dot_general(
            slope_ref[n * 512 : n * 512 + 1536, n * 256 : (n + 1) * 256],
            products[n * 512 : n * 512 + 1536, :],
            (((0,), (0,)), ((), ())),
            preferred_element_type=F32,
        )
        for n in range(2)
    ]
    first = core == 0
    own_ref[...] = jnp.where(first, grads[0], grads[1])
    other_ref[...] = jnp.where(first, grads[1], grads[0])


def second_kernel(parts_ref, own_ref, came_ref, home_ref, out_ref):
    total = parts_ref[0]
    for n in range(1, 16):
        total = total + parts_ref[n]
    audio = own_ref[0:4, :] + came_ref[0:4, :] + home_ref[...]
    for c in range(8):
        rows = audio[:, c * 128 : (c + 1) * 128]
        out_ref[:, c * 4 : c * 4 + 4, :] = jnp.broadcast_to(rows[None], (16, 4, 128))
    out_ref[:, 32:36, :] = total
    out_ref[:, 36:40, :] = jnp.zeros((16, 4, 128), F32)


def third_kernel(parts_ref, audio_ref, piece_ref):
    total = parts_ref[0]
    for n in range(1, 16):
        total = total + parts_ref[n]
    for c in range(8):
        audio_ref[:, c * 128 : (c + 1) * 128] = total[c * 4 : c * 4 + 4, :]
    piece_ref[...] = jnp.broadcast_to(total[32:36, :][None], (32, 4, 128))


def last_kernel(pieces_ref, out_ref):
    for c in range(8):
        for side in range(2):
            for core in range(2):
                row = core * 8 + side * 4
                out_ref[row : row + 4, c * 128 : (c + 1) * 128] = pieces_ref[(c * 2 + side) * 2 + core]


def call(kernel, outs, specs, scratch=(), flops=0, moved=1 << 20):
    return pl.pallas_call(
        kernel,
        out_shape=[jax.ShapeDtypeStruct(shape, kind) for shape, kind in outs],
        in_specs=specs,
        out_specs=[VMEM] * len(outs),
        scratch_shapes=list(scratch),
        compiler_params=PARAMS,
        cost_estimate=pl.CostEstimate(flops=flops, bytes_accessed=moved, transcendentals=0),
    )


def shards(images, texts, audio, pos_text, pos_audio, logit_scale, logit_bias):
    core = (lax.axis_index("aud") % 2).astype(jnp.int32)
    core_arg = core.reshape(1)
    scalars = jnp.concatenate([logit_scale, logit_bias])

    half_block = lax.dynamic_slice_in_dim(texts, core * 8, 8, 0)
    spread = jnp.broadcast_to(half_block[None], (N_TXT, 8, 1024))
    gathered = lax.all_to_all(spread, BOTH, 0, 0, tiled=True, axis_index_groups=TEXT_GROUPS)
    gathered = gathered.reshape(128, 1024)

    positions = jnp.stack([pos_text, pos_audio])
    other_images = lax.ppermute(images, "aud", OTHER_CORE)
    other_positions = lax.ppermute(positions, "aud", OTHER_CORE)
    far_audio = lax.ppermute(audio, "aud", OTHER_CORE)
    next_own = lax.ppermute(audio, "aud", FROM_NEXT)
    next_far = lax.ppermute(audio, "aud", FROM_NEXT_OTHER)

    half, window = call(
        prepare_kernel,
        [((512, 1024), BF16), ((16, 1024), F32)],
        [SMEM] + [VMEM] * 6,
        moved=3 << 20,
    )(core_arg, images, other_images, audio, far_audio, next_own, next_far)

    slope, text_parts, keep, send = call(
        slope_kernel,
        [((2048, 512), BF16), ((16, 16, 4, 128), F32), ((8, 1024), F32), ((8, 1024), F32)],
        [SMEM, SMEM] + [VMEM] * 5,
        [pltpu.VMEM((2048, 1024), BF16), pltpu.VMEM((16, 1024), F32)],
        flops=3_300_000_000,
        moved=4 << 20,
    )(core_arg, scalars, gathered, half, window, positions, other_positions)

    parts = lax.all_to_all(text_parts, BOTH, 0, 0, tiled=True, axis_index_groups=CHIP_GROUPS)

    came = lax.ppermute(send, "aud", OTHER_CORE)
    home = lax.ppermute(keep[4:8] + came[4:8], "aud", TO_NEXT)

    own_grad, other_grad = call(
        image_kernel,
        [((256, 1024), F32), ((256, 1024), F32)],
        [SMEM] + [VMEM] * 3,
        [pltpu.VMEM((2048, 1024), BF16)],
        flops=1_700_000_000,
        moved=5 << 20,
    )(core_arg, gathered, window, slope)
    grad_images = own_grad + lax.ppermute(other_grad, "aud", OTHER_CORE)

    (second,) = call(second_kernel, [((16, 40, 128), F32)], [VMEM] * 4)(parts, keep, came, home)
    second = lax.all_to_all(second, "txt", 0, 0, tiled=True)
    grad_audio, piece = call(
        third_kernel, [((4, 1024), F32), ((32, 4, 128), F32)], [VMEM]
    )(second)
    pieces = lax.all_to_all(piece, "aud", 0, 0, tiled=True)
    (grad_texts,) = call(last_kernel, [((16, 1024), F32)], [VMEM])(pieces)
    return (grad_images, grad_texts, grad_audio)


def solution(mesh):
    placed = (
        P(("txt", "aud"), None),
        P("txt", None),
        P("aud", None),
        P(("txt", "aud")),
        P(("txt", "aud")),
        P(),
        P(),
    )
    return jax.shard_map(
        shards,
        mesh=mesh,
        in_specs=placed,
        out_specs=(P(("txt", "aud"), None), P("txt", None), P("aud", None)),
        check_vma=False,
    )
```

time: 688 us -> 116 us (0.17)
  waiting for transfers between devices: 389 us -> 12.9 us
  blocking collectives: 79.2 us -> 20.7 us
  starting transfers between devices: 96.5 us -> 52.7 us
  other arithmetic: 44.6 us -> 2.47 us
  matrix products: 37.2 us -> 0 us
  Pallas kernels: 0 us -> 19.3 us
  local copies, waits for them, and re-layouts: 20.8 us -> 4.7 us
  between operations: 14.1 us -> 2.18 us
    psum x1 -> x0, waiting for transfers between devices: 239 us -> none  [shards(): grad_texts = lax.psum(grad_local_text, 'aud')]
    ppermute x36 -> x8, waiting for transfers between devices: 150 us -> 6.22 us  [the longest x1 5.03 us: shards(): home = lax.ppermute(keep[4:8] + came[4:8], 'aud', TO_NEXT)]
    psum x1 -> x0, blocking collectives: 79.2 us -> none  [shards(): summed_window = lax.psum(grad_window, 'txt')]
    ppermute x36 -> x8, starting transfers between devices: 96.5 us -> 30.6 us  [the longest x1 8.92 us: shards(): other_images = lax.ppermute(images, 'aud', OTHER_CORE)]
    dot_general x48 -> x0, matrix products: 37.2 us -> none  [the longest x16 26.6 us: block_terms(): lax.dot_general(image_half, products, (((1,), (1,)), ((), ())), preferred...]
    add x34 -> x2, other arithmetic: 37.2 us -> 1.12 us  [the longest x1 1.11 us: shards(): grad_images = own_grad + lax.ppermute(other_grad, 'aud', OTHER_CORE)]
    all_to_all x0 -> x3, starting transfers between devices: none -> 22 us  [the longest x1 8.46 us: shards(): lax.all_to_all(spread, BOTH, 0, 0, tiled=True, axis_index_groups=TEXT_GRO...]
    all_to_all x0 -> x1, blocking collectives: none -> 20.7 us  [shards(): second = lax.all_to_all(second, 'txt', 0, 0, tiled=True)]
  transfers between devices with their start and end apart: 37 -> 11, of which waited for: 37 -> 3; matrix products, arithmetic and copies ran while one was open for 12% -> 3% of each run, Pallas kernels for 0% -> 10%
where the time goes in v1:
time: 116 us; the launch traced here: 115 us
  starting transfers between devices  52.7 us (45%)
  blocking collectives  20.7 us (18%)
  Pallas kernels  19.3 us (17%)
  waiting for transfers between devices  12.9 us (11%)
  local copies, waits for them, and re-layouts  4.7 us (4%)
  other arithmetic  2.47 us (2%)
  between operations  2.18 us (2%)
    all_to_all x1, blocking collectives, shards(): second = lax.all_to_all(second, 'txt', 0, 0, tiled=True)  20.7 us
    ppermute x1, starting transfers between devices, shards(): other_images = lax.ppermute(images, 'aud', OTHER_CORE)  8.92 us
    all_to_all x1, starting transfers between devices, shards(): lax.all_to_all(spread, BOTH, 0, 0, tiled=True, axis_index_groups=TEXT_GRO...  8.46 us
    all_to_all x1, starting transfers between devices, shards(): lax.all_to_all(text_parts, BOTH, 0, 0, tiled=True, axis_index_groups=CHIP...  6.9 us
    pallas_call x1, Pallas kernels, shards(): call(slope_kernel, [((2048, 512), BF16), ((16, 16, 4, 128), F32), ((8, 10...  6.68 us
    all_to_all x1, starting transfers between devices, shards(): pieces = lax.all_to_all(piece, 'aud', 0, 0, tiled=True)  6.66 us
    all_to_all x1, waiting for transfers between devices, shards(): pieces = lax.all_to_all(piece, 'aud', 0, 0, tiled=True)  6.66 us
    ppermute x1, starting transfers between devices, shards(): next_own = lax.ppermute(audio, 'aud', FROM_NEXT)  6.07 us
  transfers between devices with their start and end apart: 11, of which 3 were waited for; matrix products, arithmetic and copies ran while one was open for 3% of the time, Pallas kernels for 10%

profile of v1, /device:TPU:1, one launch (start us, length us, event | category | flops | bytes accessed | tf_op | source)
XLA Modules:
  0.0 114.9 jit_solution(3196677176712866904)
XLA Ops:
  0.6 0.0 copy-start
  0.6 8.9 %collective-permute-start = (f32[256,1024]{1,0:T(8,128)}, f32[256,1024]{1,0:T(8,128)S(1)}, u32[]{:S(2)}, u32[]{:S(2)}) collective-permute-start(f32[256,1024]{1,0:T(8,128)} %own_ref.1), channel_id=1, source_target_pairs={{0,1},{1,0},{2,3},{3,2},{4,5},{5,4},{6,7},{7,6},{8,9},{9,8},{10,11... | collective-permute-start | bytes 3145736 | tf_op jit(solution)/shard_map/ppermute | solution.py:203
  9.6 0.0 copy-done
  9.6 0.9 broadcast_in_dim.2
  10.5 8.5 %all-to-all-start = ((f32[16,8,1024]{2,1,0:T(8,128)}), f32[16,8,1024]{2,1,0:T(8,128)S(1)}, u32[]{:S(2)}, u32[]{:S(2)}) async-start(f32[16,8,1024]{2,1,0:T(8,128)} %broadcast_in_dim.2), calls=%async_computation | async-start | bytes 1048576 | tf_op jit(solution)/shard_map/all_to_all | solution.py:199
  18.9 2.2 %collective-permute-start.1 = (f32[4,1024]{1,0:T(4,128)}, f32[4,1024]{1,0:T(4,128)S(1)}, u32[]{:S(2)}, u32[]{:S(2)}) collective-permute-start(f32[4,1024]{1,0:T(4,128)} %own_audio.1), channel_id=1, source_target_pairs={{0,1},{1,0},{2,3},{3,2},{4,5},{5,4},{6,7},{7,6},{8,9},{9,8},{10,11... | collective-permute-start | bytes 49160 | tf_op jit(solution)/shard_map/ppermute | solution.py:205
  21.2 6.1 %collective-permute-start.2 = (f32[4,1024]{1,0:T(4,128)}, f32[4,1024]{1,0:T(4,128)S(1)}, u32[]{:S(2)}, u32[]{:S(2)}) collective-permute-start(f32[4,1024]{1,0:T(4,128)} %own_audio.1), channel_id=1, source_target_pairs={{0,30},{1,31},{2,0},{3,1},{4,2},{5,3},{6,4},{7,5},{8,6},{9,7},{10,... | collective-permute-start | bytes 49160 | tf_op jit(solution)/shard_map/ppermute | solution.py:206
  27.2 3.4 %collective-permute-start.3 = (f32[4,1024]{1,0:T(4,128)}, f32[4,1024]{1,0:T(4,128)S(1)}, u32[]{:S(2)}, u32[]{:S(2)}) collective-permute-start(f32[4,1024]{1,0:T(4,128)} %own_audio.1), channel_id=1, source_target_pairs={{0,31},{1,30},{2,1},{3,0},{4,3},{5,2},{6,5},{7,4},{8,7},{9,6},{10,... | collective-permute-start | bytes 49160 | tf_op jit(solution)/shard_map/ppermute | solution.py:207
  30.6 0.7 pad_add_fusion.own_pos
  31.3 1.9 %collective-permute-start.4 = (s32[2,256]{1,0:T(2,128)S(1)}, s32[2,256]{1,0:T(2,128)S(1)}, u32[]{:S(2)}, u32[]{:S(2)}) collective-permute-start(s32[2,256]{1,0:T(2,128)S(1)} %pad_add_fusion.own_pos), channel_id=1, source_target_pairs={{0,1},{1,0},{2,3},{3,2},{4,5},{5,4},{6,7},{7,6},{8,9},{9,8},{10,11... | collective-permute-start | bytes 6152 | tf_op jit(solution)/shard_map/ppermute | solution.py:204
  34.5 0.6 pad_maximum_fusion.scalar_ref
  35.2 0.0 collective-permute-done.1.far_audio
  35.2 0.0 collective-permute-done.2.next_own
  35.2 0.0 copy-start.9
  35.2 0.0 collective-permute-done.3.next_far
  35.2 0.0 copy-start.10
  35.2 0.0 collective-permute-done.other_ref
  35.2 0.0 copy-start.3
  35.2 0.5 copy-done.8
  35.8 0.0 copy-done.9
  35.8 0.0 copy-done.10
  35.8 0.4 copy-done.3
  36.2 2.7 %shard_map.94 = (bf16[512,1024]{1,0:T(8,128)(2,1)}, f32[16,1024]{1,0:T(8,128)}) custom-call(s32[1]{0:T(128)} %bitcast.core_ref, f32[256,1024]{1,0:T(8,128)} %own_ref.1, f32[256,1024]{1,0:T(8,128)} %copy-done.3, f32[4,1024]{1,0:T(4,128)} %own_audio.1, f32[4,1024]{1,0:T(4,128)} %copy-done.8, f32[4,1024]{1,0:T(4,128)} %copy-done.9, f32[4,1024]{1,0:T(4,128)} %copy-done.10), custom_call_target="tpu_custom_call" | custom-call | bytes 3145728 | tf_op jit(solution)/shard_map/pallas_call | solution.py:209
  38.9 0.0 collective-permute-done.4.other_pos
  38.9 0.0 all-to-all-done
  38.9 0.0 copy-start.4
  38.9 0.5 copy-done.14
  39.4 0.2 copy-done.4
  39.7 6.7 %shard_map.95 = (bf16[2048,512]{1,0:T(8,128)(2,1)}, f32[16,16,4,128]{3,2,1,0:T(4,128)}, f32[8,1024]{1,0:T(8,128)}, f32[8,1024]{1,0:T(8,128)}) custom-call(s32[1]{0:T(128)} %bitcast.core_ref, f32[2]{0:T(128)} %pad_maximum_fusion.scalar_ref, f32[128,1024]{1,0:T(8,128)} %bitcast.4, bf16[512,1024]{1,0:T(8,128)(2,1)} %get-tuple-element.14.half_ref, ...), custom_call_target="tpu_custom_call" | custom-call | flops 3300000000 | bytes 4194304 | tf_op jit(solution)/shard_map/pallas_call | solution.py:216
  46.4 6.9 %all-to-all-start.1 = ((f32[16,16,4,128]{3,2,1,0:T(4,128)}), f32[16,16,4,128]{3,2,1,0:T(4,128)S(1)}, u32[]{:S(2)}, u32[]{:S(2)}) async-start(f32[16,16,4,128]{3,2,1,0:T(4,128)} %get-tuple-element.18), calls=%async_computation.1 | async-start | bytes 1048576 | tf_op jit(solution)/shard_map/all_to_all | solution.py:225
  53.3 5.0 %shard_map.96 = (f32[256,1024]{1,0:T(8,128)}, f32[256,1024]{1,0:T(8,128)}) custom-call(s32[1]{0:T(128)} %bitcast.core_ref, f32[128,1024]{1,0:T(8,128)} %bitcast.5, f32[16,1024]{1,0:T(8,128)} %get-tuple-element.13.window_ref, bf16[2048,512]{1,0:T(8,128)(2,1)} %get-tuple-element.15.slope_ref), custom_call_target="tpu_custom_call" | custom-call | flops 1700000000 | bytes 5242880 | tf_op jit(solution)/shard_map/pallas_call | solution.py:230
  58.3 2.7 %collective-permute-start.5 = (f32[256,1024]{1,0:T(8,128)}, f32[256,1024]{1,0:T(8,128)S(1)}, u32[]{:S(2)}, u32[]{:S(2)}) collective-permute-start(f32[256,1024]{1,0:T(8,128)} %get-tuple-element.17), channel_id=1, source_target_pairs={{0,1},{1,0},{2,3},{3,2},{4,5},{5,4},{6,7},{7,6},{8,9},{9,8},{10,11... | collective-permute-start | bytes 3145736 | tf_op jit(solution)/shard_map/ppermute | solution.py:238
  61.0 1.9 %collective-permute-start.6 = (f32[8,1024]{1,0:T(8,128)S(1)}, f32[8,1024]{1,0:T(8,128)S(1)}, u32[]{:S(2)}, u32[]{:S(2)}) collective-permute-start(f32[8,1024]{1,0:T(8,128)S(1)} %copy-done.13), channel_id=1, source_target_pairs={{0,1},{1,0},{2,3},{3,2},{4,5},{5,4},{6,7},{7,6},{8,9},{9,8},{10,11... | collective-permute-start | bytes 98312 | tf_op jit(solution)/shard_map/ppermute | solution.py:227
  62.9 1.2 %collective-permute-done.6.came_ref = f32[8,1024]{1,0:T(8,128)S(1)} collective-permute-done((f32[8,1024]{1,0:T(8,128)S(1)}, f32[8,1024]{1,0:T(8,128)S(1)}, u32[]{:S(2)}, u32[]{:S(2)}) %collective-permute-start.6) | collective-permute-done | bytes 32800 | tf_op jit(solution)/shard_map/ppermute | solution.py:227
  64.1 3.6 %collective-permute-start.7 = (f32[4,1024]{1,0:T(4,128)S(1)}, f32[4,1024]{1,0:T(4,128)S(1)}, u32[]{:S(2)}, u32[]{:S(2)}) collective-permute-start(f32[4,1024]{1,0:T(4,128)S(1)} %slice_add_fusion), channel_id=1, source_target_pairs={{0,2},{1,3},{2,4},{3,5},{4,6},{5,7},{6,8},{7,9},{8,10},{9,11},{10,... | collective-permute-start | bytes 49160 | tf_op jit(solution)/shard_map/ppermute | solution.py:228
  67.7 5.0 %collective-permute-done.7.home_ref = f32[4,1024]{1,0:T(4,128)S(1)} collective-permute-done((f32[4,1024]{1,0:T(4,128)S(1)}, f32[4,1024]{1,0:T(4,128)S(1)}, u32[]{:S(2)}, u32[]{:S(2)}) %collective-permute-start.7) | collective-permute-done | bytes 16416 | tf_op jit(solution)/shard_map/ppermute | solution.py:228
  72.7 0.0 all-to-all-done.1.parts_ref
  72.7 0.6 copy-done.11
  73.3 0.8 copy-done.1
  74.1 1.9 %shard_map.97 = f32[16,40,128]{2,1,0:T(8,128)} custom-call(f32[16,16,4,128]{3,2,1,0:T(4,128)} %copy-done.1, f32[8,1024]{1,0:T(8,128)} %get-tuple-element.19.own_ref, f32[8,1024]{1,0:T(8,128)} %copy-done.7, f32[4,1024]{1,0:T(4,128)} %copy-done.11), custom_call_target="tpu_custom_call" | custom-call | bytes 1048576 | tf_op jit(solution)/shard_map/pallas_call | solution.py:240
  76.0 20.7 %all_to_all.20.parts_ref = f32[16,40,128]{2,1,0:T(8,128)} all-to-all(f32[16,40,128]{2,1,0:T(8,128)} %shard_map.97), channel_id=1, replica_groups=mesh['txt'=16,'aud'=32] {'txt'}, dimensions={0} | all-to-all | bytes 655360 | tf_op jit(solution)/shard_map/all_to_all | solution.py:241
  96.7 1.6 %shard_map.98 = (f32[4,1024]{1,0:T(4,128)}, f32[32,4,128]{2,1,0:T(4,128)}) custom-call(f32[16,40,128]{2,1,0:T(8,128)} %all_to_all.20.parts_ref), custom_call_target="tpu_custom_call" | custom-call | bytes 1048576 | tf_op jit(solution)/shard_map/pallas_call | solution.py:242
  98.3 6.7 %all-to-all-start.3 = ((f32[32,4,128]{2,1,0:T(4,128)}), f32[32,4,128]{2,1,0:T(4,128)S(1)}, u32[]{:S(2)}, u32[]{:S(2)}) async-start(f32[32,4,128]{2,1,0:T(4,128)} %get-tuple-element.21), calls=%async_computation.3 | async-start | bytes 131072 | tf_op jit(solution)/shard_map/all_to_all | solution.py:245
  105.0 0.0 collective-permute-done.5
  105.0 1.1 add.15
  106.1 6.7 %all-to-all-done.3.pieces_ref = f32[32,4,128]{2,1,0:T(4,128)S(1)} async-done(((f32[32,4,128]{2,1,0:T(4,128)}), f32[32,4,128]{2,1,0:T(4,128)S(1)}, u32[]{:S(2)}, u32[]{:S(2)}) %all-to-all-start.3) | async-done | bytes 65568 | tf_op jit(solution)/shard_map/all_to_all | solution.py:245
  112.8 0.6 copy-done.5
  113.4 1.5 %shard_map.99 = f32[16,1024]{1,0:T(8,128)} custom-call(f32[32,4,128]{2,1,0:T(4,128)} %copy-done.5), custom_call_target="tpu_custom_call" | custom-call | bytes 1048576 | tf_op jit(solution)/shard_map/pallas_call | solution.py:246
  (17 shorter events, 0.0 us)
Async XLA Ops:
  0.6 9.0 %copy-start = (f32[16,1024]{1,0:T(8,128)S(1)}, f32[16,1024]{1,0:T(8,128)}, u32[]{:S(2)}) copy-start(f32[16,1024]{1,0:T(8,128)} %param.8) | copy-start | bytes 196612
  0.6 34.6 %collective-permute-start = (f32[256,1024]{1,0:T(8,128)}, f32[256,1024]{1,0:T(8,128)S(1)}, u32[]{:S(2)}, u32[]{:S(2)}) collective-permute-start(f32[256,1024]{1,0:T(8,128)} %own_ref.1), channel_id=1, source_target_pairs={{0,1},{1,0},{2,3},{3,2},{4,5},{5,4},{6,7},{7,6},{8,9},{9,8},{10,11... | collective-permute-start | bytes 3145736 | tf_op jit(solution)/shard_map/ppermute | solution.py:203
  10.5 28.4 %all-to-all-start = ((f32[16,8,1024]{2,1,0:T(8,128)}), f32[16,8,1024]{2,1,0:T(8,128)S(1)}, u32[]{:S(2)}, u32[]{:S(2)}) async-start(f32[16,8,1024]{2,1,0:T(8,128)} %broadcast_in_dim.2), calls=%async_computation | async-start | bytes 1048576 | tf_op jit(solution)/shard_map/all_to_all | solution.py:199
  18.9 16.2 %collective-permute-start.1 = (f32[4,1024]{1,0:T(4,128)}, f32[4,1024]{1,0:T(4,128)S(1)}, u32[]{:S(2)}, u32[]{:S(2)}) collective-permute-start(f32[4,1024]{1,0:T(4,128)} %own_audio.1), channel_id=1, source_target_pairs={{0,1},{1,0},{2,3},{3,2},{4,5},{5,4},{6,7},{7,6},{8,9},{9,8},{10,11... | collective-permute-start | bytes 49160 | tf_op jit(solution)/shard_map/ppermute | solution.py:205
  21.2 14.0 %collective-permute-start.2 = (f32[4,1024]{1,0:T(4,128)}, f32[4,1024]{1,0:T(4,128)S(1)}, u32[]{:S(2)}, u32[]{:S(2)}) collective-permute-start(f32[4,1024]{1,0:T(4,128)} %own_audio.1), channel_id=1, source_target_pairs={{0,30},{1,31},{2,0},{3,1},{4,2},{5,3},{6,4},{7,5},{8,6},{9,7},{10,... | collective-permute-start | bytes 49160 | tf_op jit(solution)/shard_map/ppermute | solution.py:206
  27.2 8.0 %collective-permute-start.3 = (f32[4,1024]{1,0:T(4,128)}, f32[4,1024]{1,0:T(4,128)S(1)}, u32[]{:S(2)}, u32[]{:S(2)}) collective-permute-start(f32[4,1024]{1,0:T(4,128)} %own_audio.1), channel_id=1, source_target_pairs={{0,31},{1,30},{2,1},{3,0},{4,3},{5,2},{6,5},{7,4},{8,7},{9,6},{10,... | collective-permute-start | bytes 49160 | tf_op jit(solution)/shard_map/ppermute | solution.py:207
  31.3 7.6 %copy-start.12 = (s32[2,256]{1,0:T(2,128)}, s32[2,256]{1,0:T(2,128)S(1)}, u32[]{:S(2)}) copy-start(s32[2,256]{1,0:T(2,128)S(1)} %pad_add_fusion.own_pos) | copy-start | bytes 6148
  31.3 7.5 %collective-permute-start.4 = (s32[2,256]{1,0:T(2,128)S(1)}, s32[2,256]{1,0:T(2,128)S(1)}, u32[]{:S(2)}, u32[]{:S(2)}) collective-permute-start(s32[2,256]{1,0:T(2,128)S(1)} %pad_add_fusion.own_pos), channel_id=1, source_target_pairs={{0,1},{1,0},{2,3},{3,2},{4,5},{5,4},{6,7},{7,6},{8,9},{9,8},{10,11... | collective-permute-start | bytes 6152 | tf_op jit(solution)/shard_map/ppermute | solution.py:204
  35.2 0.6 copy-start.8
  35.2 0.6 copy-start.9
  35.2 0.6 copy-start.10
  35.2 1.0 copy-start.3
  38.9 0.6 copy-start.14
  38.9 0.8 copy-start.4
  46.4 26.3 %all-to-all-start.1 = ((f32[16,16,4,128]{3,2,1,0:T(4,128)}), f32[16,16,4,128]{3,2,1,0:T(4,128)S(1)}, u32[]{:S(2)}, u32[]{:S(2)}) async-start(f32[16,16,4,128]{3,2,1,0:T(4,128)} %get-tuple-element.18), calls=%async_computation.1 | async-start | bytes 1048576 | tf_op jit(solution)/shard_map/all_to_all | solution.py:225
  53.3 7.7 %copy-start.13 = (f32[8,1024]{1,0:T(8,128)S(1)}, f32[8,1024]{1,0:T(8,128)}, u32[]{:S(2)}) copy-start(f32[8,1024]{1,0:T(8,128)} %get-tuple-element.20) | copy-start | bytes 98308
  53.3 10.8 %copy-start.6 = (f32[8,1024]{1,0:T(8,128)S(1)}, f32[8,1024]{1,0:T(8,128)}, u32[]{:S(2)}) copy-start(f32[8,1024]{1,0:T(8,128)} %get-tuple-element.19.own_ref) | copy-start | bytes 98308
  58.3 46.7 %copy-start.2 = (f32[256,1024]{1,0:T(8,128)S(1)}, f32[256,1024]{1,0:T(8,128)}, u32[]{:S(2)}) copy-start(f32[256,1024]{1,0:T(8,128)} %get-tuple-element.16) | copy-start | bytes 3145732
  58.3 46.7 %collective-permute-start.5 = (f32[256,1024]{1,0:T(8,128)}, f32[256,1024]{1,0:T(8,128)S(1)}, u32[]{:S(2)}, u32[]{:S(2)}) collective-permute-start(f32[256,1024]{1,0:T(8,128)} %get-tuple-element.17), channel_id=1, source_target_pairs={{0,1},{1,0},{2,3},{3,2},{4,5},{5,4},{6,7},{7,6},{8,9},{9,8},{10,11... | collective-permute-start | bytes 3145736 | tf_op jit(solution)/shard_map/ppermute | solution.py:238
  61.0 3.1 %collective-permute-start.6 = (f32[8,1024]{1,0:T(8,128)S(1)}, f32[8,1024]{1,0:T(8,128)S(1)}, u32[]{:S(2)}, u32[]{:S(2)}) collective-permute-start(f32[8,1024]{1,0:T(8,128)S(1)} %copy-done.13), channel_id=1, source_target_pairs={{0,1},{1,0},{2,3},{3,2},{4,5},{5,4},{6,7},{7,6},{8,9},{9,8},{10,11... | collective-permute-start | bytes 98312 | tf_op jit(solution)/shard_map/ppermute | solution.py:227
  64.1 8.6 %copy-start.7 = (f32[8,1024]{1,0:T(8,128)}, f32[8,1024]{1,0:T(8,128)S(1)}, u32[]{:S(2)}) copy-start(f32[8,1024]{1,0:T(8,128)S(1)} %collective-permute-done.6.came_ref) | copy-start | bytes 98308
  64.1 8.6 %collective-permute-start.7 = (f32[4,1024]{1,0:T(4,128)S(1)}, f32[4,1024]{1,0:T(4,128)S(1)}, u32[]{:S(2)}, u32[]{:S(2)}) collective-permute-start(f32[4,1024]{1,0:T(4,128)S(1)} %slice_add_fusion), channel_id=1, source_target_pairs={{0,2},{1,3},{2,4},{3,5},{4,6},{5,7},{6,8},{7,9},{8,10},{9,11},{10,... | collective-permute-start | bytes 49160 | tf_op jit(solution)/shard_map/ppermute | solution.py:228
  72.7 0.6 copy-start.11
  73.3 0.8 copy-start.1
  98.3 14.5 %all-to-all-start.3 = ((f32[32,4,128]{2,1,0:T(4,128)}), f32[32,4,128]{2,1,0:T(4,128)S(1)}, u32[]{:S(2)}, u32[]{:S(2)}) async-start(f32[32,4,128]{2,1,0:T(4,128)} %get-tuple-element.21), calls=%async_computation.3 | async-start | bytes 131072 | tf_op jit(solution)/shard_map/all_to_all | solution.py:245
  112.8 0.6 copy-start.5

commit v2 on v1

v2 whole, which is shorter than its diff:
```python
import jax
import jax.numpy as jnp
from jax import lax
from jax.experimental import pallas as pl
from jax.experimental.pallas import tpu as pltpu
from jax.sharding import PartitionSpec as P

BOTH = ("txt", "aud")
N_TXT, N_AUD = 16, 32
F32, BF16 = jnp.float32, jnp.bfloat16
VMEM = pl.BlockSpec(memory_space=pltpu.VMEM)
SMEM = pl.BlockSpec(memory_space=pltpu.SMEM)


def device(high, z, x, low, core):
    return (high * 8 + z) * N_AUD + (x * 4 + low) * 2 + core


def groups_by(key):
    found = {}
    for high in range(2):
        for z in range(8):
            for x in range(4):
                for low in range(4):
                    for core in range(2):
                        place = (high, z, x, low, core)
                        found.setdefault(key(*place), []).append(device(*place))
    return [found[k] for k in sorted(found)]


TEXT_GROUPS = groups_by(lambda high, z, x, low, core: (x, low if high == 0 else low ^ 2, core))
Y_GROUPS = groups_by(lambda high, z, x, low, core: (z, x, core))
Z_GROUPS = groups_by(lambda high, z, x, low, core: (high, x, low, core))

OTHER_CORE = [(i, i ^ 1) for i in range(N_AUD)]
FROM_NEXT = [(i, (i - 2) % N_AUD) for i in range(N_AUD)]
OTHER_HALF = [(i, i ^ 8) for i in range(N_TXT)]
TO_NEXT = [(i, (i + 2) % N_AUD) for i in range(N_AUD)]


BLOCK_COLUMNS = ((0, 256), (0, 512), (0, 512), (256, 512))


def slope_kernel(
    core_ref, scalar_ref, texts, own_ref, other_a, other_b, own_small, far_small, next_pair,
    slope_out, text_ref, keep_ref, send_ref, window_ref,
    half_ref, slope_ref, products, audio_sum, sems,
):
    core = core_ref[0]
    first = core == 0
    temper, offset = scalar_ref[0], scalar_ref[1]
    for level, (a, b) in enumerate(
        ((own_small[0:4, :], far_small[0:4, :]), (next_pair[0:4, :], next_pair[4:8, :]))
    ):
        window_ref[level * 8 : level * 8 + 4, :] = jnp.where(first, a, b)
        window_ref[level * 8 + 4 : level * 8 + 8, :] = jnp.where(first, b, a)
    half_ref[pl.ds(pl.multiple_of(core * 256, 256), 256), :] = own_ref[...].astype(BF16)
    half_ref[pl.ds(pl.multiple_of((1 - core) * 256, 256), 128), :] = other_a[...].astype(BF16)
    half_ref[pl.ds(pl.multiple_of((1 - core) * 256 + 128, 128), 128), :] = other_b[...].astype(BF16)
    own, far = own_small[4:5, :].astype(jnp.int32), far_small[4:5, :].astype(jnp.int32)
    low, high = jnp.where(first, own, far), jnp.where(first, far, own)
    text_pos = jnp.concatenate([low[:, 0:256], high[:, 0:256]], axis=1)
    slot_pos = jnp.concatenate([low[:, 256:512], high[:, 256:512] + 4], axis=1)
    rest = text_pos & 15
    place = slot_pos * 128 + (text_pos >> 4) * 8 + (rest & 7)
    place = jnp.where((rest >> 3) == core, place, -1)

    def slope_copy(block):
        low, high = BLOCK_COLUMNS[block]
        where = (pl.ds(block * 512, 512), pl.ds(low, high - low))
        return pltpu.make_async_copy(slope_ref.at[where], slope_out.at[where], sems.at[block])

    def logits_of(block):
        low, high = BLOCK_COLUMNS[block]
        for w in range(4):
            slot = block * 4 + w
            products[slot * 128 : (slot + 1) * 128, :] = (
                texts[...] * window_ref[slot : slot + 1, :]
            ).astype(BF16)
        return lax.dot_general(
            products[block * 512 : (block + 1) * 512, :],
            half_ref[low:high, :],
            (((1,), (1,)), ((), ())),
            preferred_element_type=F32,
        )

    def slope_of(block, dots):
        low, high = BLOCK_COLUMNS[block]
        rows = lax.broadcasted_iota(jnp.int32, dots.shape, 0) + block * 512
        positive = rows == place[:, low:high]
        value = jax.nn.sigmoid(temper * dots + offset)
        slope = (temper * jnp.where(positive, value - 1.0, value)).astype(BF16)
        slope_ref[block * 512 : (block + 1) * 512, low:high] = slope
        slope_copy(block).start()
        return slope

    def grads_of(block, slope):
        low, high = BLOCK_COLUMNS[block]
        grads = jnp.dot(slope, half_ref[low:high, :], preferred_element_type=F32)
        part = None
        for w in range(4):
            slot = block * 4 + w
            grad = grads[w * 128 : (w + 1) * 128, :]
            more = grad * window_ref[slot : slot + 1, :]
            part = more if part is None else part + more
            audio_sum[slot : slot + 1, :] = jnp.sum(grad * texts[...], axis=0, keepdims=True)
        return part

    dots = logits_of(0)
    total = None
    for block in range(4):
        slope = slope_of(block, dots)
        if block < 3:
            dots = logits_of(block + 1)
        part = grads_of(block, slope)
        total = part if total is None else total + part
    for c in range(8):
        for high in range(2):
            tiles = total[high * 64 : (high + 1) * 64, c * 128 : (c + 1) * 128].reshape(8, 8, 128)
            text_ref[high * 4 + c // 2, :, (c % 2) * 8 : (c % 2) * 8 + 8, :] = tiles
    for level in range(2):
        even = audio_sum[level * 8 : level * 8 + 4, :]
        odd = audio_sum[level * 8 + 4 : level * 8 + 8, :]
        keep_ref[level * 4 : level * 4 + 4, :] = jnp.where(first, even, odd)
        send_ref[level * 4 : level * 4 + 4, :] = jnp.where(first, odd, even)
    for block in range(4):
        slope_copy(block).wait()


def image_kernel(core_ref, texts, window_ref, slope_ref, own_ref, other_a, other_b, products):
    core = core_ref[0]
    for slot in range(16):
        products[slot * 128 : (slot + 1) * 128, :] = (
            texts[...] * window_ref[slot : slot + 1, :]
        ).astype(BF16)
    grads = [
        lax.dot_general(
            slope_ref[n * 512 : n * 512 + 1536, n * 256 : (n + 1) * 256],
            products[n * 512 : n * 512 + 1536, :],
            (((0,), (0,)), ((), ())),
            preferred_element_type=F32,
        )
        for n in range(2)
    ]
    first = core == 0
    own_ref[...] = jnp.where(first, grads[0], grads[1])
    other_a[...] = jnp.where(first, grads[1][0:128], grads[0][0:128])
    other_b[...] = jnp.where(first, grads[1][128:256], grads[0][128:256])


def second_kernel(parts_ref, own_ref, came_ref, home_ref, out_ref):
    total = parts_ref[0]
    for n in range(1, 8):
        total = total + parts_ref[n]
    out_ref[:, 0:16, :] = total
    audio = own_ref[0:4, :] + came_ref[0:4, :] + home_ref[...]
    for c in range(8):
        rows = audio[:, c * 128 : (c + 1) * 128]
        out_ref[:, 16 + c * 4 : 20 + c * 4, :] = jnp.broadcast_to(rows[None], (8, 4, 128))


def third_kernel(parts_ref, audio_ref, piece_ref):
    total = parts_ref[0]
    for n in range(1, 8):
        total = total + parts_ref[n]
    for c in range(8):
        audio_ref[:, c * 128 : (c + 1) * 128] = total[16 + c * 4 : 20 + c * 4, :]
    piece_ref[...] = jnp.broadcast_to(total[0:16, :][None], (32, 16, 128))


def last_kernel(pieces_ref, mine_ref, fixed_ref, out_ref, audio_ref):
    audio_ref[...] = mine_ref[...] + fixed_ref[...]
    for core in range(2):
        for low in range(4):
            total = pieces_ref[low * 2 + core]
            for x in range(1, 4):
                total = total + pieces_ref[(x * 4 + low) * 2 + core]
            for n in range(2):
                left = (low * 2 + n) * 128
                out_ref[core * 8 : core * 8 + 8, left : left + 128] = total[n * 8 : n * 8 + 8, :]


def call(kernel, outs, specs, scratch=(), flops=0, moved=1 << 20, room=4, out_specs=None):
    return pl.pallas_call(
        kernel,
        out_shape=[o if hasattr(o, "shape") else jax.ShapeDtypeStruct(*o) for o in outs],
        in_specs=specs,
        out_specs=out_specs or [VMEM] * len(outs),
        scratch_shapes=list(scratch),
        compiler_params=pltpu.CompilerParams(vmem_limit_bytes=room << 20),
        cost_estimate=pl.CostEstimate(flops=flops, bytes_accessed=moved, transcendentals=0),
    )


def shards(images, texts, audio, pos_text, pos_audio, logit_scale, logit_bias):
    core = (lax.axis_index("aud") % 2).astype(jnp.int32)
    core_arg = core.reshape(1)
    scalars = jnp.concatenate([logit_scale, logit_bias])

    half_block = lax.dynamic_slice_in_dim(texts, core * 8, 8, 0)
    spread = jnp.broadcast_to(half_block[None], (N_TXT, 8, 1024))
    spread, audio = lax.optimization_barrier((spread, audio))
    gathered = lax.all_to_all(spread, BOTH, 0, 0, tiled=True, axis_index_groups=TEXT_GROUPS)
    gathered = gathered.reshape(128, 1024)

    small = jnp.concatenate(
        [audio, jnp.concatenate([pos_text, pos_audio, jnp.zeros((512,), jnp.int32)]).astype(F32)[None]]
    )
    far_small = lax.ppermute(small, "aud", OTHER_CORE)
    next_pair = lax.ppermute(jnp.concatenate([audio, far_small[0:4]]), "aud", FROM_NEXT)
    other_a = lax.ppermute(images[0:128], "aud", OTHER_CORE)
    other_b = lax.ppermute(images[128:256], "aud", OTHER_CORE)

    slope, text_parts, keep, send, window = call(
        slope_kernel,
        [
            pltpu.HBM((2048, 512), BF16),
            ((8, 8, 16, 128), F32),
            ((8, 1024), F32),
            ((8, 1024), F32),
            ((16, 1024), F32),
        ],
        [SMEM, SMEM] + [VMEM] * 7,
        [
            pltpu.VMEM((512, 1024), BF16),
            pltpu.VMEM((2048, 512), BF16),
            pltpu.VMEM((2048, 1024), BF16),
            pltpu.VMEM((16, 1024), F32),
            pltpu.SemaphoreType.DMA((4,)),
        ],
        flops=3_300_000_000,
        moved=4 << 20,
        room=26,
        out_specs=[pl.BlockSpec(memory_space=pltpu.HBM)] + [VMEM] * 4,
    )(core_arg, scalars, gathered, images, other_a, other_b, small, far_small, next_pair)

    parts = lax.all_to_all(text_parts, BOTH, 0, 0, tiled=True, axis_index_groups=Y_GROUPS)

    came = lax.ppermute(send, "aud", OTHER_CORE)
    leaving = keep[4:8] + came[4:8]
    home = lax.ppermute(leaving, "aud", TO_NEXT)

    (second,) = call(second_kernel, [((8, 48, 128), F32)], [VMEM] * 4)(parts, keep, came, home)
    slope = lax.optimization_barrier((slope, second))[0]
    second = lax.all_to_all(second, BOTH, 0, 0, tiled=True, axis_index_groups=Z_GROUPS)
    own_grad, *other_grads = call(
        image_kernel,
        [((256, 1024), F32), ((128, 1024), F32), ((128, 1024), F32)],
        [SMEM] + [VMEM] * 3,
        [pltpu.VMEM((2048, 1024), BF16)],
        flops=1_700_000_000,
        moved=5 << 20,
        room=24,
    )(core_arg, gathered, window, slope)
    mine, piece = call(
        third_kernel, [((4, 1024), F32), ((32, 16, 128), F32)], [VMEM]
    )(second)
    pieces = lax.all_to_all(piece, "aud", 0, 0, tiled=True)
    fixed = lax.ppermute(mine, "txt", OTHER_HALF)
    came_grads = [lax.ppermute(grad, "aud", OTHER_CORE) for grad in other_grads]
    grad_images = own_grad + jnp.concatenate(came_grads)
    fixed, grad_images = lax.optimization_barrier((fixed, grad_images))
    grad_texts, grad_audio = call(
        last_kernel, [((16, 1024), F32), ((4, 1024), F32)], [VMEM] * 3
    )(pieces, mine, fixed)
    return (grad_images, grad_texts, grad_audio)


def solution(mesh):
    placed = (
        P(("txt", "aud"), None),
        P("txt", None),
        P("aud", None),
        P(("txt", "aud")),
        P(("txt", "aud")),
        P(),
        P(),
    )
    return jax.shard_map(
        shards,
        mesh=mesh,
        in_specs=placed,
        out_specs=(P(("txt", "aud"), None), P("txt", None), P("aud", None)),
        check_vma=False,
    )
```

time: 116 us -> 98.6 us (0.85)
  blocking collectives: 20.7 us -> 0 us
  starting transfers between devices: 52.7 us -> 62.8 us
  Pallas kernels: 19.3 us -> 10.1 us
  waiting for transfers between devices: 12.9 us -> 17.1 us
  local copies, waits for them, and re-layouts: 4.7 us -> 3.32 us
    all_to_all x1 -> x0, blocking collectives: 20.7 us -> none  [shards(): second = lax.all_to_all(second, 'txt', 0, 0, tiled=True)]
    pallas_call x6 -> x5, Pallas kernels: 19.3 us -> 10.1 us  [the longest x1 6.08 us: shards(): call(slope_kernel, [pltpu.HBM((2048, 512), BF16), ((8, 8, 16, 128), F32),...]
    all_to_all x1, starting transfers between devices: 8.46 us -> 14.7 us  [shards(): lax.all_to_all(spread, BOTH, 0, 0, tiled=True, axis_index_groups=TEXT_GRO...]
    all_to_all x1 -> x2, starting transfers between devices: 6.9 us -> 12.1 us  [the longest x1 6.32 us: shards(): lax.all_to_all(text_parts, BOTH, 0, 0, tiled=True, axis_index_groups=Y_GR...]
    ppermute x7 -> x8, waiting for transfers between devices: 5.05 us -> 9.42 us  [the longest x1 5.6 us: shards(): home = lax.ppermute(leaving, 'aud', TO_NEXT)]
    all_to_all x1 -> x2, waiting for transfers between devices: 0.01 us -> 3.9 us  [the longest x1 3.89 us: shards(): lax.all_to_all(text_parts, BOTH, 0, 0, tiled=True, axis_index_groups=Y_GR...]
    all_to_all x1, waiting for transfers between devices: 6.66 us -> 2.94 us  [shards(): pieces = lax.all_to_all(piece, 'aud', 0, 0, tiled=True)]
    ppermute x7 -> x8, starting transfers between devices: 28.7 us -> 25.8 us  [the longest x1 6.07 us: shards(): lax.ppermute(jnp.concatenate([audio, far_small[0:4]]), 'aud', FROM_NEXT)]
  transfers between devices with their start and end apart: 11 -> 13, of which waited for: 3 -> 6; matrix products, arithmetic and copies ran while one was open for 3% -> 2% of each run, Pallas kernels for 10% -> 3%
where the time goes in v2:
time: 98.6 us; the launch traced here: 97.8 us
  starting transfers between devices  62.8 us (64%)
  waiting for transfers between devices  17.1 us (17%)
  Pallas kernels  10.1 us (10%)
  local copies, waits for them, and re-layouts  3.32 us (3%)
  other arithmetic  2.27 us (2%)
  between operations  2.22 us (2%)
    all_to_all x1, starting transfers between devices, shards(): lax.all_to_all(spread, BOTH, 0, 0, tiled=True, axis_index_groups=TEXT_GRO...  14.7 us
    all_to_all x1, starting transfers between devices, shards(): pieces = lax.all_to_all(piece, 'aud', 0, 0, tiled=True)  7.21 us
    all_to_all x1, starting transfers between devices, shards(): lax.all_to_all(text_parts, BOTH, 0, 0, tiled=True, axis_index_groups=Y_GR...  6.32 us
    pallas_call x1, Pallas kernels, shards(): call(slope_kernel, [pltpu.HBM((2048, 512), BF16), ((8, 8, 16, 128), F32),...  6.08 us
    ppermute x1, starting transfers between devices, shards(): lax.ppermute(jnp.concatenate([audio, far_small[0:4]]), 'aud', FROM_NEXT)  6.07 us
    all_to_all x1, starting transfers between devices, shards(): lax.all_to_all(second, BOTH, 0, 0, tiled=True, axis_index_groups=Z_GROUPS)  5.73 us
    ppermute x1, waiting for transfers between devices, shards(): home = lax.ppermute(leaving, 'aud', TO_NEXT)  5.6 us
    ppermute x2, starting transfers between devices, shards(): came_grads = [lax.ppermute(grad, 'aud', OTHER_CORE) for grad in other_grads]  5.29 us
  transfers between devices with their start and end apart: 13, of which 6 were waited for; matrix products, arithmetic and copies ran while one was open for 2% of the time, Pallas kernels for 3%

profile of v2, /device:TPU:1, one launch (start us, length us, event | category | flops | bytes accessed | tf_op | source)
XLA Modules:
  0.0 97.8 jit_solution(16768417701095690770)
XLA Ops:
  0.6 0.0 copy-start
  0.6 0.0 copy-start.3
  0.7 0.0 copy-start.1
  0.7 0.0 copy-start.4
  0.7 0.0 copy-start.5
  0.7 0.8 copy-done
  1.5 0.8 broadcast_in_dim.4
  2.3 14.7 %all-to-all-start = ((f32[16,8,1024]{2,1,0:T(8,128)}), f32[16,8,1024]{2,1,0:T(8,128)S(1)}, u32[]{:S(2)}, u32[]{:S(2)}) async-start(f32[16,8,1024]{2,1,0:T(8,128)} %broadcast_in_dim.4), calls=%async_computation | async-start | bytes 1048576 | tf_op jit(solution)/shard_map/all_to_all | solution.py:203
  17.0 0.0 copy-done.1
  17.0 0.1 fusion
  17.1 2.9 %collective-permute-start.1 = (f32[128,1024]{1,0:T(8,128)S(1)}, f32[128,1024]{1,0:T(8,128)S(1)}, u32[]{:S(2)}, u32[]{:S(2)}) collective-permute-start(f32[128,1024]{1,0:T(8,128)S(1)} %get-tuple-element.37), channel_id=1, source_target_pairs={{0,1},{1,0},{2,3},{3,2},{4,5},{5,4},{6,7},{7,6},{8,9},{9,8},{10,11... | collective-permute-start | bytes 1572872 | tf_op jit(solution)/shard_map/ppermute | solution.py:212
  20.0 1.9 %collective-permute-start = (f32[128,1024]{1,0:T(8,128)S(1)}, f32[128,1024]{1,0:T(8,128)S(1)}, u32[]{:S(2)}, u32[]{:S(2)}) collective-permute-start(f32[128,1024]{1,0:T(8,128)S(1)} %get-tuple-element.38), channel_id=1, source_target_pairs={{0,1},{1,0},{2,3},{3,2},{4,5},{5,4},{6,7},{7,6},{8,9},{9,8},{10,11... | collective-permute-start | bytes 1572872 | tf_op jit(solution)/shard_map/ppermute | solution.py:211
  21.9 0.0 copy-done.4
  21.9 0.0 copy-done.5
  21.9 0.0 copy-done.3
  22.0 2.4 %collective-permute-start.2 = (f32[5,1024]{1,0:T(8,128)S(1)}, f32[5,1024]{1,0:T(8,128)S(1)}, u32[]{:S(2)}, u32[]{:S(2)}) collective-permute-start(f32[5,1024]{1,0:T(8,128)S(1)} %pad_maximum_fusion.own_small), channel_id=1, source_target_pairs={{0,1},{1,0},{2,3},{3,2},{4,5},{5,4},{6,7},{7,6},{8,9},{9,8},{10,11... | collective-permute-start | bytes 61448 | tf_op jit(solution)/shard_map/ppermute | solution.py:209
  25.7 0.0 collective-permute-done.2.far_small
  25.7 6.1 %collective-permute-start.3 = (f32[8,1024]{1,0:T(8,128)S(1)}, f32[8,1024]{1,0:T(8,128)S(1)}, u32[]{:S(2)}, u32[]{:S(2)}) collective-permute-start(f32[8,1024]{1,0:T(8,128)S(1)} %pad_maximum_fusion.1), channel_id=1, source_target_pairs={{0,30},{1,31},{2,0},{3,1},{4,2},{5,3},{6,4},{7,5},{8,6},{9,7},{10,... | collective-permute-start | bytes 98312 | tf_op jit(solution)/shard_map/ppermute | solution.py:210
  31.8 0.1 pad_maximum_fusion.2.scalar_ref
  31.9 0.9 collective-permute-done.3.next_pair
  32.8 0.0 collective-permute-done.1.other_b
  32.8 0.0 collective-permute-done.other_a
  32.8 0.0 all-to-all-done
  32.8 6.1 %shard_map.94 = (bf16[2048,512]{1,0:T(8,128)(2,1)}, f32[8,8,16,128]{3,2,1,0:T(8,128)}, f32[8,1024]{1,0:T(8,128)S(1)}, f32[8,1024]{1,0:T(8,128)S(1)}, f32[16,1024]{1,0:T(8,128)S(1)}) custom-call(s32[1]{0:T(128)} %bitcast.core_ref, f32[2]{0:T(128)S(1)} %pad_maximum_fusion.2.scalar_ref, f32[128,1024]{1,0:T(8,128)S(1)} %bitcast.5, f32[256,1024]{1,0:T(8,128)S(1)} %copy-done.1, ...), custom_call_target="tpu_custom_call" | custom-call | flops 3300000000 | bytes 4194304 | tf_op jit(solution)/shard_map/pallas_call | solution.py:214
  38.9 6.3 %all-to-all-start.1 = ((f32[8,8,16,128]{3,2,1,0:T(8,128)}), f32[8,8,16,128]{3,2,1,0:T(8,128)S(1)}, u32[]{:S(2)}, u32[]{:S(2)}) async-start(f32[8,8,16,128]{3,2,1,0:T(8,128)} %get-tuple-element.22), calls=%async_computation.1 | async-start | bytes 1048576 | tf_op jit(solution)/shard_map/all_to_all | solution.py:237
  45.2 3.1 %collective-permute-start.4 = (f32[8,1024]{1,0:T(8,128)S(1)}, f32[8,1024]{1,0:T(8,128)S(1)}, u32[]{:S(2)}, u32[]{:S(2)}) collective-permute-start(f32[8,1024]{1,0:T(8,128)S(1)} %get-tuple-element.24), channel_id=1, source_target_pairs={{0,1},{1,0},{2,3},{3,2},{4,5},{5,4},{6,7},{7,6},{8,9},{9,8},{10,11... | collective-permute-start | bytes 98312 | tf_op jit(solution)/shard_map/ppermute | solution.py:239
  48.3 0.8 collective-permute-done.4.came_ref
  49.2 3.6 %collective-permute-start.5 = (f32[4,1024]{1,0:T(4,128)S(1)}, f32[4,1024]{1,0:T(4,128)S(1)}, u32[]{:S(2)}, u32[]{:S(2)}) collective-permute-start(f32[4,1024]{1,0:T(4,128)S(1)} %slice_add_fusion), channel_id=1, source_target_pairs={{0,2},{1,3},{2,4},{3,5},{4,6},{5,7},{6,8},{7,9},{8,10},{9,11},{10,... | collective-permute-start | bytes 49160 | tf_op jit(solution)/shard_map/ppermute | solution.py:241
  52.8 5.6 %collective-permute-done.5.home_ref = f32[4,1024]{1,0:T(4,128)S(1)} collective-permute-done((f32[4,1024]{1,0:T(4,128)S(1)}, f32[4,1024]{1,0:T(4,128)S(1)}, u32[]{:S(2)}, u32[]{:S(2)}) %collective-permute-start.5) | collective-permute-done | bytes 16416 | tf_op jit(solution)/shard_map/ppermute | solution.py:241
  58.4 3.9 %all-to-all-done.1.parts_ref = f32[8,8,16,128]{3,2,1,0:T(8,128)S(1)} async-done(((f32[8,8,16,128]{3,2,1,0:T(8,128)}), f32[8,8,16,128]{3,2,1,0:T(8,128)S(1)}, u32[]{:S(2)}, u32[]{:S(2)}) %all-to-all-start.1) | async-done | bytes 524320 | tf_op jit(solution)/shard_map/all_to_all | solution.py:237
  62.3 0.7 shard_map.95
  63.0 5.7 %all-to-all-start.2 = ((f32[8,48,128]{2,1,0:T(8,128)}), f32[8,48,128]{2,1,0:T(8,128)S(1)}, u32[]{:S(2)}, u32[]{:S(2)}) async-start(f32[8,48,128]{2,1,0:T(8,128)} %shard_map.95), calls=%async_computation.2 | async-start | bytes 393216 | tf_op jit(solution)/shard_map/all_to_all | solution.py:245
  68.8 0.0 copy-start.2
  68.8 1.6 %copy-done.2 = bf16[2048,512]{1,0:T(8,128)(2,1)S(1)} copy-done((bf16[2048,512]{1,0:T(8,128)(2,1)S(1)}, bf16[2048,512]{1,0:T(8,128)(2,1)}, u32[]{:S(2)}) %copy-start.2) | copy-done | bytes 2097176
  70.4 1.9 %shard_map.97 = (f32[256,1024]{1,0:T(8,128)S(1)}, f32[128,1024]{1,0:T(8,128)S(1)}, f32[128,1024]{1,0:T(8,128)S(1)}) custom-call(s32[1]{0:T(128)} %bitcast.core_ref, f32[128,1024]{1,0:T(8,128)S(1)} %bitcast.6, f32[16,1024]{1,0:T(8,128)S(1)} %get-tuple-element.26.window_ref, bf16[2048,512]{1,0:T(8,128)(2,1)S(1)} %copy-done.2), custom_call_target="tpu_custom_call" | custom-call | flops 1700000000 | bytes 5242880 | tf_op jit(solution)/shard_map/pallas_call | solution.py:246
  72.2 3.4 %collective-permute-start.7 = (f32[128,1024]{1,0:T(8,128)S(1)}, f32[128,1024]{1,0:T(8,128)S(1)}, u32[]{:S(2)}, u32[]{:S(2)}) collective-permute-start(f32[128,1024]{1,0:T(8,128)S(1)} %get-tuple-element.30), channel_id=1, source_target_pairs={{0,1},{1,0},{2,3},{3,2},{4,5},{5,4},{6,7},{7,6},{8,9},{9,8},{10,11... | collective-permute-start | bytes 1572872 | tf_op jit(solution)/shard_map/ppermute | solution.py:260
  75.6 1.9 %collective-permute-start.8 = (f32[128,1024]{1,0:T(8,128)S(1)}, f32[128,1024]{1,0:T(8,128)}, u32[]{:S(2)}, u32[]{:S(2)}) collective-permute-start(f32[128,1024]{1,0:T(8,128)S(1)} %get-tuple-element.31), channel_id=1, source_target_pairs={{0,1},{1,0},{2,3},{3,2},{4,5},{5,4},{6,7},{7,6},{8,9},{9,8},{10,11... | collective-permute-start | bytes 1572872 | tf_op jit(solution)/shard_map/ppermute | solution.py:260
  77.6 0.0 all-to-all-done.2.parts_ref
  77.6 0.7 shard_map.96
  78.3 7.2 %all-to-all-start.3 = ((f32[32,16,128]{2,1,0:T(8,128)}), f32[32,16,128]{2,1,0:T(8,128)S(1)}, u32[]{:S(2)}, u32[]{:S(2)}) async-start(f32[32,16,128]{2,1,0:T(8,128)} %get-tuple-element.33), calls=%async_computation.3 | async-start | bytes 524288 | tf_op jit(solution)/shard_map/all_to_all | solution.py:258
  85.5 3.6 %collective-permute-start.6 = (f32[4,1024]{1,0:T(4,128)S(1)}, f32[4,1024]{1,0:T(4,128)S(1)}, u32[]{:S(2)}, u32[]{:S(2)}) collective-permute-start(f32[4,1024]{1,0:T(4,128)S(1)} %get-tuple-element.25.mine_ref), channel_id=1, source_target_pairs={{0,256},{32,288},{64,320},{96,352},{128,384},{160,416},{192,448},{... | collective-permute-start | bytes 49160 | tf_op jit(solution)/shard_map/ppermute | solution.py:259
  89.1 0.0 collective-permute-done.7
  89.2 0.0 collective-permute-done.8
  89.2 2.1 %maximum_add_fusion = f32[256,1024]{1,0:T(8,128)} fusion(f32[256,1024]{1,0:T(8,128)S(1)} %get-tuple-element.29, f32[128,1024]{1,0:T(8,128)} %collective-permute-done.8, f32[128,1024]{1,0:T(8,128)S(1)} %collective-permute-done.7), kind=kLoop, calls=%fused_computation | loop fusion | flops 524288 | bytes 3145728 | tf_op jit(solution)/shard_map/add | solution.py:261
  91.3 2.9 %collective-permute-done.6.fixed_ref = f32[4,1024]{1,0:T(4,128)S(1)} collective-permute-done((f32[4,1024]{1,0:T(4,128)S(1)}, f32[4,1024]{1,0:T(4,128)S(1)}, u32[]{:S(2)}, u32[]{:S(2)}) %collective-permute-start.6) | collective-permute-done | bytes 16416 | tf_op jit(solution)/shard_map/ppermute | solution.py:259
  94.2 2.9 %all-to-all-done.3.pieces_ref = f32[32,16,128]{2,1,0:T(8,128)S(1)} async-done(((f32[32,16,128]{2,1,0:T(8,128)}), f32[32,16,128]{2,1,0:T(8,128)S(1)}, u32[]{:S(2)}, u32[]{:S(2)}) %all-to-all-start.3) | async-done | bytes 262176 | tf_op jit(solution)/shard_map/all_to_all | solution.py:258
  97.1 0.7 shard_map.98
  (8 shorter events, 0.1 us)
Async XLA Ops:
  0.6 0.8 copy-start
  0.6 21.3 %copy-start.3 = (f32[4,1024]{1,0:T(4,128)S(1)}, f32[4,1024]{1,0:T(4,128)}, u32[]{:S(2)}) copy-start(f32[4,1024]{1,0:T(4,128)} %param.9) | copy-start | bytes 49156
  0.7 16.3 %copy-start.1 = (f32[256,1024]{1,0:T(8,128)S(1)}, f32[256,1024]{1,0:T(8,128)}, u32[]{:S(2)}) copy-start(f32[256,1024]{1,0:T(8,128)} %own_ref.1) | copy-start | bytes 3145732
  0.7 21.2 %copy-start.4 = (s32[256]{0:T(256)S(1)}, s32[256]{0:T(256)}, u32[]{:S(2)}) copy-start(s32[256]{0:T(256)} %param.11) | copy-start | bytes 3076
  0.7 21.2 %copy-start.5 = (s32[256]{0:T(256)S(1)}, s32[256]{0:T(256)}, u32[]{:S(2)}) copy-start(s32[256]{0:T(256)} %param.10) | copy-start | bytes 3076
  2.3 30.5 %all-to-all-start = ((f32[16,8,1024]{2,1,0:T(8,128)}), f32[16,8,1024]{2,1,0:T(8,128)S(1)}, u32[]{:S(2)}, u32[]{:S(2)}) async-start(f32[16,8,1024]{2,1,0:T(8,128)} %broadcast_in_dim.4), calls=%async_computation | async-start | bytes 1048576 | tf_op jit(solution)/shard_map/all_to_all | solution.py:203
  17.1 15.7 %collective-permute-start.1 = (f32[128,1024]{1,0:T(8,128)S(1)}, f32[128,1024]{1,0:T(8,128)S(1)}, u32[]{:S(2)}, u32[]{:S(2)}) collective-permute-start(f32[128,1024]{1,0:T(8,128)S(1)} %get-tuple-element.37), channel_id=1, source_target_pairs={{0,1},{1,0},{2,3},{3,2},{4,5},{5,4},{6,7},{7,6},{8,9},{9,8},{10,11... | collective-permute-start | bytes 1572872 | tf_op jit(solution)/shard_map/ppermute | solution.py:212
  20.0 12.9 %collective-permute-start = (f32[128,1024]{1,0:T(8,128)S(1)}, f32[128,1024]{1,0:T(8,128)S(1)}, u32[]{:S(2)}, u32[]{:S(2)}) collective-permute-start(f32[128,1024]{1,0:T(8,128)S(1)} %get-tuple-element.38), channel_id=1, source_target_pairs={{0,1},{1,0},{2,3},{3,2},{4,5},{5,4},{6,7},{7,6},{8,9},{9,8},{10,11... | collective-permute-start | bytes 1572872 | tf_op jit(solution)/shard_map/ppermute | solution.py:211
  22.0 3.7 %collective-permute-start.2 = (f32[5,1024]{1,0:T(8,128)S(1)}, f32[5,1024]{1,0:T(8,128)S(1)}, u32[]{:S(2)}, u32[]{:S(2)}) collective-permute-start(f32[5,1024]{1,0:T(8,128)S(1)} %pad_maximum_fusion.own_small), channel_id=1, source_target_pairs={{0,1},{1,0},{2,3},{3,2},{4,5},{5,4},{6,7},{7,6},{8,9},{9,8},{10,11... | collective-permute-start | bytes 61448 | tf_op jit(solution)/shard_map/ppermute | solution.py:209
  25.7 7.1 %collective-permute-start.3 = (f32[8,1024]{1,0:T(8,128)S(1)}, f32[8,1024]{1,0:T(8,128)S(1)}, u32[]{:S(2)}, u32[]{:S(2)}) collective-permute-start(f32[8,1024]{1,0:T(8,128)S(1)} %pad_maximum_fusion.1), channel_id=1, source_target_pairs={{0,30},{1,31},{2,0},{3,1},{4,2},{5,3},{6,4},{7,5},{8,6},{9,7},{10,... | collective-permute-start | bytes 98312 | tf_op jit(solution)/shard_map/ppermute | solution.py:210
  38.9 23.4 %all-to-all-start.1 = ((f32[8,8,16,128]{3,2,1,0:T(8,128)}), f32[8,8,16,128]{3,2,1,0:T(8,128)S(1)}, u32[]{:S(2)}, u32[]{:S(2)}) async-start(f32[8,8,16,128]{3,2,1,0:T(8,128)} %get-tuple-element.22), calls=%async_computation.1 | async-start | bytes 1048576 | tf_op jit(solution)/shard_map/all_to_all | solution.py:237
  45.2 3.9 %collective-permute-start.4 = (f32[8,1024]{1,0:T(8,128)S(1)}, f32[8,1024]{1,0:T(8,128)S(1)}, u32[]{:S(2)}, u32[]{:S(2)}) collective-permute-start(f32[8,1024]{1,0:T(8,128)S(1)} %get-tuple-element.24), channel_id=1, source_target_pairs={{0,1},{1,0},{2,3},{3,2},{4,5},{5,4},{6,7},{7,6},{8,9},{9,8},{10,11... | collective-permute-start | bytes 98312 | tf_op jit(solution)/shard_map/ppermute | solution.py:239
  49.2 9.3 %collective-permute-start.5 = (f32[4,1024]{1,0:T(4,128)S(1)}, f32[4,1024]{1,0:T(4,128)S(1)}, u32[]{:S(2)}, u32[]{:S(2)}) collective-permute-start(f32[4,1024]{1,0:T(4,128)S(1)} %slice_add_fusion), channel_id=1, source_target_pairs={{0,2},{1,3},{2,4},{3,5},{4,6},{5,7},{6,8},{7,9},{8,10},{9,11},{10,... | collective-permute-start | bytes 49160 | tf_op jit(solution)/shard_map/ppermute | solution.py:241
  63.0 14.5 %all-to-all-start.2 = ((f32[8,48,128]{2,1,0:T(8,128)}), f32[8,48,128]{2,1,0:T(8,128)S(1)}, u32[]{:S(2)}, u32[]{:S(2)}) async-start(f32[8,48,128]{2,1,0:T(8,128)} %shard_map.95), calls=%async_computation.2 | async-start | bytes 393216 | tf_op jit(solution)/shard_map/all_to_all | solution.py:245
  68.8 1.6 %copy-start.2 = (bf16[2048,512]{1,0:T(8,128)(2,1)S(1)}, bf16[2048,512]{1,0:T(8,128)(2,1)}, u32[]{:S(2)}) copy-start(bf16[2048,512]{1,0:T(8,128)(2,1)} %get-tuple-element.28.slope_ref) | copy-start | bytes 6291460
  72.2 16.9 %collective-permute-start.7 = (f32[128,1024]{1,0:T(8,128)S(1)}, f32[128,1024]{1,0:T(8,128)S(1)}, u32[]{:S(2)}, u32[]{:S(2)}) collective-permute-start(f32[128,1024]{1,0:T(8,128)S(1)} %get-tuple-element.30), channel_id=1, source_target_pairs={{0,1},{1,0},{2,3},{3,2},{4,5},{5,4},{6,7},{7,6},{8,9},{9,8},{10,11... | collective-permute-start | bytes 1572872 | tf_op jit(solution)/shard_map/ppermute | solution.py:260
  75.6 13.5 %collective-permute-start.8 = (f32[128,1024]{1,0:T(8,128)S(1)}, f32[128,1024]{1,0:T(8,128)}, u32[]{:S(2)}, u32[]{:S(2)}) collective-permute-start(f32[128,1024]{1,0:T(8,128)S(1)} %get-tuple-element.31), channel_id=1, source_target_pairs={{0,1},{1,0},{2,3},{3,2},{4,5},{5,4},{6,7},{7,6},{8,9},{9,8},{10,11... | collective-permute-start | bytes 1572872 | tf_op jit(solution)/shard_map/ppermute | solution.py:260
  78.3 18.9 %all-to-all-start.3 = ((f32[32,16,128]{2,1,0:T(8,128)}), f32[32,16,128]{2,1,0:T(8,128)S(1)}, u32[]{:S(2)}, u32[]{:S(2)}) async-start(f32[32,16,128]{2,1,0:T(8,128)} %get-tuple-element.33), calls=%async_computation.3 | async-start | bytes 524288 | tf_op jit(solution)/shard_map/all_to_all | solution.py:258
  85.5 8.7 %collective-permute-start.6 = (f32[4,1024]{1,0:T(4,128)S(1)}, f32[4,1024]{1,0:T(4,128)S(1)}, u32[]{:S(2)}, u32[]{:S(2)}) collective-permute-start(f32[4,1024]{1,0:T(4,128)S(1)} %get-tuple-element.25.mine_ref), channel_id=1, source_target_pairs={{0,256},{32,288},{64,320},{96,352},{128,384},{160,416},{192,448},{... | collective-permute-start | bytes 49160 | tf_op jit(solution)/shard_map/ppermute | solution.py:259

commit v3 on v2

v3 whole, which is shorter than its diff:
```python
import jax
import jax.numpy as jnp
from jax import lax
from jax.experimental import pallas as pl
from jax.experimental.pallas import tpu as pltpu
from jax.sharding import PartitionSpec as P

BOTH = ("txt", "aud")
N_TXT, N_AUD = 16, 32
SPLIT = 128
F32, BF16 = jnp.float32, jnp.bfloat16
VMEM = pl.BlockSpec(memory_space=pltpu.VMEM)
SMEM = pl.BlockSpec(memory_space=pltpu.SMEM)


def device(high, z, x, low, core):
    return (high * 8 + z) * N_AUD + (x * 4 + low) * 2 + core


def groups_by(key):
    found = {}
    for high in range(2):
        for z in range(8):
            for x in range(4):
                for low in range(4):
                    for core in range(2):
                        place = (high, z, x, low, core)
                        found.setdefault(key(*place), []).append(device(*place))
    return [found[k] for k in sorted(found)]


TEXT_GROUPS = groups_by(lambda high, z, x, low, core: (x, low if high == 0 else low ^ 2, core))
Y_GROUPS = groups_by(lambda high, z, x, low, core: (z, x, core))
Z_GROUPS = groups_by(lambda high, z, x, low, core: (high, x, low, core))

OTHER_CORE = [(i, i ^ 1) for i in range(N_AUD)]
FROM_NEXT = [(i, (i - 2) % N_AUD) for i in range(N_AUD)]
OTHER_HALF = [(i, i ^ 8) for i in range(N_TXT)]
TO_NEXT = [(i, (i + 2) % N_AUD) for i in range(N_AUD)]
TO_NEXT_OTHER = [(i, ((i + 2) % N_AUD) ^ 1) for i in range(N_AUD)]


BLOCK_COLUMNS = ((0, 256), (0, 512), (0, 512), (256, 512))


def pack_kernel(images_ref, audio_ref, text_ref, slot_ref, first_ref, rest_ref):
    first_ref[0:SPLIT, :] = images_ref[0:SPLIT, :]
    rest_ref[...] = images_ref[SPLIT:256, :]
    first_ref[SPLIT : SPLIT + 8, :] = jnp.zeros((8, 1024), F32)
    first_ref[SPLIT : SPLIT + 4, :] = audio_ref[...]
    first_ref[SPLIT + 4 : SPLIT + 5, 0:256] = text_ref[...].astype(F32)
    first_ref[SPLIT + 4 : SPLIT + 5, 256:512] = slot_ref[...].astype(F32)


def pair_kernel(own_ref, far_ref, pair_ref):
    pair_ref[0:4, :] = own_ref[0:4, :]
    pair_ref[4:8, :] = far_ref[0:4, :]


def slope_kernel(
    core_ref, scale_ref, bias_ref, texts, own_a, own_b, other_a, other_b, next_pair,
    slope_out, text_ref, keep_self, keep_next, send_self, send_next, window_ref,
    half_ref, slope_ref, products, audio_sum, total, sems,
):
    core = core_ref[0]
    first = core == 0
    temper, offset = scale_ref[0], bias_ref[0]
    for level, (a, b) in enumerate(
        ((own_a[SPLIT : SPLIT + 4, :], other_a[SPLIT : SPLIT + 4, :]), (next_pair[0:4, :], next_pair[4:8, :]))
    ):
        window_ref[level * 8 : level * 8 + 4, :] = jnp.where(first, a, b)
        window_ref[level * 8 + 4 : level * 8 + 8, :] = jnp.where(first, b, a)
    for which, a, b in ((core, own_a, own_b), (1 - core, other_a, other_b)):
        top = pl.multiple_of(which * 256, 256)
        middle = pl.multiple_of(which * 256 + SPLIT, 32)
        half_ref[pl.ds(top, SPLIT), :] = a[0:SPLIT, :].astype(BF16)
        half_ref[pl.ds(middle, 256 - SPLIT), :] = b[...].astype(BF16)
    own = own_a[SPLIT + 4 : SPLIT + 5, :].astype(jnp.int32)
    far = other_a[SPLIT + 4 : SPLIT + 5, :].astype(jnp.int32)
    low, high = jnp.where(first, own, far), jnp.where(first, far, own)
    text_pos = jnp.concatenate([low[:, 0:256], high[:, 0:256]], axis=1)
    slot_pos = jnp.concatenate([low[:, 256:512], high[:, 256:512] + 4], axis=1)
    rest = text_pos & 15
    place = slot_pos * 128 + (text_pos >> 4) * 8 + (rest & 7)
    place = jnp.where((rest >> 3) == core, place, -1)

    def slope_copy(block):
        low, high = BLOCK_COLUMNS[block]
        where = (pl.ds(block * 512, 512), pl.ds(low, high - low))
        return pltpu.make_async_copy(slope_ref.at[where], slope_out.at[where], sems.at[block])

    def logits_of(block):
        low, high = BLOCK_COLUMNS[block]
        for w in range(4):
            slot = block * 4 + w
            row = window_ref[slot : slot + 1, :]
            for r in range(0, 128, 32):
                products[slot * 128 + r : slot * 128 + r + 32, :] = (
                    texts[r : r + 32, :] * row
                ).astype(BF16)
        return lax.dot_general(
            products[block * 512 : (block + 1) * 512, :],
            half_ref[low:high, :],
            (((1,), (1,)), ((), ())),
            preferred_element_type=F32,
        )

    def slope_of(block, dots):
        low, high = BLOCK_COLUMNS[block]
        place_here = place[:, low:high] - block * 512
        for r in range(0, 512, 32):
            rows = lax.broadcasted_iota(jnp.int32, (32, high - low), 0) + r
            value = jax.nn.sigmoid(temper * dots[r : r + 32, :] + offset)
            value = temper * jnp.where(rows == place_here, value - 1.0, value)
            slope_ref[block * 512 + r : block * 512 + r + 32, low:high] = value.astype(BF16)
        slope_copy(block).start()

    def grads_of(block):
        low, high = BLOCK_COLUMNS[block]
        slope = slope_ref[block * 512 : (block + 1) * 512, low:high]
        for n in range(0, 1024, 256):
            grads = jnp.dot(slope, half_ref[low:high, n : n + 256], preferred_element_type=F32)
            for c in range(n, n + 256, 128):
                part = None if block == 0 else total[:, c : c + 128]
                text = texts[:, c : c + 128]
                for w in range(4):
                    slot = block * 4 + w
                    grad = grads[w * 128 : (w + 1) * 128, c - n : c - n + 128]
                    more = grad * window_ref[slot : slot + 1, c : c + 128]
                    part = more if part is None else part + more
                    audio_sum[slot : slot + 1, c : c + 128] = jnp.sum(grad * text, axis=0, keepdims=True)
                if block < 3:
                    total[:, c : c + 128] = part
                    continue
                for high_half in range(2):
                    top = c // 128 % 2 * 8
                    text_ref[high_half * 4 + c // 256, :, top : top + 8, :] = part[
                        high_half * 64 : (high_half + 1) * 64, :
                    ].reshape(8, 8, 128)

    dots = logits_of(0)
    for block in range(4):
        slope_of(block, dots)
        if block < 3:
            dots = logits_of(block + 1)
        grads_of(block)
    for level, (keep_ref, send_ref) in enumerate(((keep_self, send_self), (keep_next, send_next))):
        even = audio_sum[level * 8 : level * 8 + 4, :]
        odd = audio_sum[level * 8 + 4 : level * 8 + 8, :]
        keep_ref[...] = jnp.where(first, even, odd)
        send_ref[...] = jnp.where(first, odd, even)
    for block in range(4):
        slope_copy(block).wait()


def image_kernel(
    core_ref, texts, window_ref, slope_hbm, own_ref, other_a, other_b, products, slope_ref, sems
):
    core = core_ref[0]

    def slope_copy(n):
        where = (pl.ds(n * 512, 1536), pl.ds(n * 256, 256))
        return pltpu.make_async_copy(slope_hbm.at[where], slope_ref.at[where], sems.at[n])

    slope_copy(0).start()
    slope_copy(1).start()
    for slot in range(16):
        products[slot * 128 : (slot + 1) * 128, :] = (
            texts[...] * window_ref[slot : slot + 1, :]
        ).astype(BF16)
    slope_copy(0).wait()
    slope_copy(1).wait()
    grads = [
        lax.dot_general(
            slope_ref[n * 512 : n * 512 + 1536, n * 256 : (n + 1) * 256],
            products[n * 512 : n * 512 + 1536, :],
            (((0,), (0,)), ((), ())),
            preferred_element_type=F32,
        )
        for n in range(2)
    ]
    first = core == 0
    own_ref[...] = jnp.where(first, grads[0], grads[1])
    other_a[...] = jnp.where(first, grads[1][0:128], grads[0][0:128])
    other_b[...] = jnp.where(first, grads[1][128:256], grads[0][128:256])


def second_kernel(parts_ref, own_ref, next_ref, far_ref, came_ref, out_ref):
    total = parts_ref[0]
    for n in range(1, 8):
        total = total + parts_ref[n]
    out_ref[:, 0:16, :] = total
    audio = (own_ref[...] + came_ref[...]) + (next_ref[...] + far_ref[...])
    for c in range(8):
        rows = audio[:, c * 128 : (c + 1) * 128]
        out_ref[:, 16 + c * 4 : 20 + c * 4, :] = jnp.broadcast_to(rows[None], (8, 4, 128))


def third_kernel(parts_ref, audio_ref, piece_ref):
    total = parts_ref[0]
    for n in range(1, 8):
        total = total + parts_ref[n]
    for c in range(8):
        audio_ref[:, c * 128 : (c + 1) * 128] = total[16 + c * 4 : 20 + c * 4, :]
    piece_ref[...] = jnp.broadcast_to(total[0:16, :][None], (32, 16, 128))


def last_kernel(pieces_ref, mine_ref, fixed_ref, out_ref, audio_ref):
    audio_ref[...] = mine_ref[...] + fixed_ref[...]
    for core in range(2):
        for low in range(4):
            total = pieces_ref[low * 2 + core]
            for x in range(1, 4):
                total = total + pieces_ref[(x * 4 + low) * 2 + core]
            for n in range(2):
                left = (low * 2 + n) * 128
                out_ref[core * 8 : core * 8 + 8, left : left + 128] = total[n * 8 : n * 8 + 8, :]


def call(kernel, outs, specs, scratch=(), flops=0, moved=1 << 20, room=4, out_specs=None):
    return pl.pallas_call(
        kernel,
        out_shape=[o if hasattr(o, "shape") else jax.ShapeDtypeStruct(*o) for o in outs],
        in_specs=specs,
        out_specs=out_specs or [VMEM] * len(outs),
        scratch_shapes=list(scratch),
        compiler_params=pltpu.CompilerParams(vmem_limit_bytes=room << 20),
        cost_estimate=pl.CostEstimate(flops=flops, bytes_accessed=moved, transcendentals=0),
    )


def shards(images, texts, audio, pos_text, pos_audio, logit_scale, logit_bias):
    core = (lax.axis_index("aud") % 2).astype(jnp.int32)
    core_arg = core.reshape(1)

    half_block = lax.dynamic_slice_in_dim(texts, core * 8, 8, 0)
    spread = jnp.broadcast_to(half_block[None], (N_TXT, 8, 1024))
    spread, audio = lax.optimization_barrier((spread, audio))
    gathered = lax.all_to_all(spread, BOTH, 0, 0, tiled=True, axis_index_groups=TEXT_GROUPS)
    gathered = gathered.reshape(128, 1024)

    own_a, own_b = call(
        pack_kernel, [((SPLIT + 8, 1024), F32), ((256 - SPLIT, 1024), F32)], [VMEM] * 4
    )(*(pltpu.with_memory_space_constraint(v, pltpu.HBM) for v in (images, audio, pos_text.reshape(1, 256), pos_audio.reshape(1, 256))))
    other_a = lax.ppermute(own_a, "aud", OTHER_CORE)
    other_b = lax.ppermute(own_b, "aud", OTHER_CORE)
    small = pl.BlockSpec((8, 1024), lambda i: (SPLIT // 8, 0))
    pair = pl.pallas_call(
        pair_kernel,
        out_shape=jax.ShapeDtypeStruct((8, 1024), F32),
        grid=(1,),
        in_specs=[small, small],
        out_specs=pl.BlockSpec((8, 1024), lambda i: (0, 0)),
        compiler_params=pltpu.CompilerParams(vmem_limit_bytes=1 << 20),
    )(own_a, other_a)
    next_pair = lax.ppermute(pair, "aud", FROM_NEXT)

    slope, text_parts, keep_self, keep_next, send_self, send_next, window = call(
        slope_kernel,
        [
            pltpu.HBM((2048, 512), BF16),
            ((8, 8, 16, 128), F32),
            ((4, 1024), F32),
            ((4, 1024), F32),
            ((4, 1024), F32),
            ((4, 1024), F32),
            ((16, 1024), F32),
        ],
        [SMEM] * 3 + [VMEM] * 6,
        [
            pltpu.VMEM((512, 1024), BF16),
            pltpu.VMEM((2048, 512), BF16),
            pltpu.VMEM((2048, 1024), BF16),
            pltpu.VMEM((16, 1024), F32),
            pltpu.VMEM((128, 1024), F32),
            pltpu.SemaphoreType.DMA((4,)),
        ],
        flops=3_300_000_000,
        moved=4 << 20,
        room=26,
        out_specs=[pl.BlockSpec(memory_space=pltpu.HBM)] + [VMEM] * 6,
    )(core_arg, logit_scale, logit_bias, gathered, own_a, own_b, other_a, other_b, next_pair)

    parts = lax.all_to_all(text_parts, BOTH, 0, 0, tiled=True, axis_index_groups=Y_GROUPS)

    home = [
        lax.ppermute(keep_next, "aud", TO_NEXT),
        lax.ppermute(send_next, "aud", TO_NEXT_OTHER),
        lax.ppermute(send_self, "aud", OTHER_CORE),
    ]
    window = lax.optimization_barrier((window, home[2]))[0]

    own_grad, *other_grads = call(
        image_kernel,
        [((256, 1024), F32), ((128, 1024), F32), ((128, 1024), F32)],
        [SMEM, VMEM, VMEM, pl.BlockSpec(memory_space=pltpu.HBM)],
        [
            pltpu.VMEM((2048, 1024), BF16),
            pltpu.VMEM((2048, 512), BF16),
            pltpu.SemaphoreType.DMA((2,)),
        ],
        flops=1_700_000_000,
        moved=5 << 20,
        room=24,
    )(core_arg, gathered, window, pltpu.with_memory_space_constraint(slope, pltpu.HBM))
    keep_self, *other_grads = lax.optimization_barrier((keep_self, *other_grads))
    (second,) = call(second_kernel, [((8, 48, 128), F32)], [VMEM] * 5)(parts, keep_self, *home)
    other_grads = lax.optimization_barrier((*other_grads, second))[:2]
    second = lax.all_to_all(second, BOTH, 0, 0, tiled=True, axis_index_groups=Z_GROUPS)
    mine, piece = call(
        third_kernel, [((4, 1024), F32), ((32, 16, 128), F32)], [VMEM]
    )(second)
    pieces = lax.all_to_all(piece, "aud", 0, 0, tiled=True)
    fixed = lax.ppermute(mine, "txt", OTHER_HALF)
    came_grads = [lax.ppermute(grad, "aud", OTHER_CORE) for grad in other_grads]
    grad_images = own_grad + jnp.concatenate(came_grads)
    fixed, grad_images = lax.optimization_barrier((fixed, grad_images))
    grad_texts, grad_audio = call(
        last_kernel, [((16, 1024), F32), ((4, 1024), F32)], [VMEM] * 3
    )(pieces, mine, fixed)
    return (grad_images, grad_texts, grad_audio)


def solution(mesh):
    placed = (
        P(("txt", "aud"), None),
        P("txt", None),
        P("aud", None),
        P(("txt", "aud")),
        P(("txt", "aud")),
        P(),
        P(),
    )
    return jax.shard_map(
        shards,
        mesh=mesh,
        in_specs=placed,
        out_specs=(P(("txt", "aud"), None), P("txt", None), P("aud", None)),
        check_vma=False,
    )
```

time: 98.6 us -> 97.6 us (0.990)
  waiting for transfers between devices: 17.1 us -> 14.9 us
  Pallas kernels: 10.1 us -> 11.9 us
  local copies, waits for them, and re-layouts: 3.32 us -> 1.67 us
  starting transfers between devices: 62.8 us -> 64 us
    all_to_all x1, waiting for transfers between devices: 3.89 us -> 0.01 us  [shards(): lax.all_to_all(text_parts, BOTH, 0, 0, tiled=True, axis_index_groups=Y_GR...]
    all_to_all x1, waiting for transfers between devices: 0.01 us -> 3.6 us  [shards(): lax.all_to_all(second, BOTH, 0, 0, tiled=True, axis_index_groups=Z_GROUPS)]
    unnamed x12 -> x2, local copies, waits for them, and re-layouts: 2.39 us -> 0.82 us
    pallas_call x1, Pallas kernels: 1.88 us -> 3.23 us  [shards(): call(image_kernel, [((256, 1024), F32), ((128, 1024), F32), ((128, 1024),...]
    pallas_call x1 -> x3, Pallas kernels: 0.72 us -> 2.05 us  [the longest x1 1.32 us: shards(): call(pack_kernel, [((SPLIT + 8, 1024), F32), ((256 - SPLIT, 1024), F32)],...]
    ppermute x6, waiting for transfers between devices: 7.37 us -> 6.18 us  [the longest x1 4.88 us: shards(): lax.ppermute(send_next, 'aud', TO_NEXT_OTHER)]
    all_to_all x1, starting transfers between devices: 6.32 us -> 7.4 us  [shards(): lax.all_to_all(text_parts, BOTH, 0, 0, tiled=True, axis_index_groups=Y_GR...]
  transfers between devices with their start and end apart: 13 -> 13, of which waited for: 6 -> 5; matrix products, arithmetic and copies ran while one was open for 2% -> 2% of each run, Pallas kernels for 3% -> 5%
where the time goes in v3:
time: 97.6 us; the launch traced here: 96.7 us
  starting transfers between devices  64 us (66%)
  waiting for transfers between devices  14.9 us (15%)
  Pallas kernels  11.9 us (12%)
  other arithmetic  2.15 us (2%)
  between operations  2.12 us (2%)
  local copies, waits for them, and re-layouts  1.67 us (2%)
    all_to_all x1, starting transfers between devices, shards(): lax.all_to_all(spread, BOTH, 0, 0, tiled=True, axis_index_groups=TEXT_GRO...  14.7 us
    all_to_all x1, starting transfers between devices, shards(): lax.all_to_all(text_parts, BOTH, 0, 0, tiled=True, axis_index_groups=Y_GR...  7.4 us
    all_to_all x1, starting transfers between devices, shards(): pieces = lax.all_to_all(piece, 'aud', 0, 0, tiled=True)  7.06 us
    ppermute x1, starting transfers between devices, shards(): next_pair = lax.ppermute(pair, 'aud', FROM_NEXT)  6.07 us
    pallas_call x1, Pallas kernels, shards(): call(slope_kernel, [pltpu.HBM((2048, 512), BF16), ((8, 8, 16, 128), F32),...  5.29 us
    ppermute x2, starting transfers between devices, shards(): came_grads = [lax.ppermute(grad, 'aud', OTHER_CORE) for grad in other_grads]  4.99 us
    ppermute x1, waiting for transfers between devices, shards(): lax.ppermute(send_next, 'aud', TO_NEXT_OTHER)  4.88 us
    all_to_all x1, starting transfers between devices, shards(): lax.all_to_all(second, BOTH, 0, 0, tiled=True, axis_index_groups=Z_GROUPS)  4.83 us
  transfers between devices with their start and end apart: 13, of which 5 were waited for; matrix products, arithmetic and copies ran while one was open for 2% of the time, Pallas kernels for 5%

profile of v3, /device:TPU:1, one launch (start us, length us, event | category | flops | bytes accessed | tf_op | source)
XLA Modules:
  0.0 96.7 jit_solution(9475322177818613327)
XLA Ops:
  0.6 0.0 copy-start
  0.7 0.8 copy-done
  1.5 0.8 broadcast_in_dim.2
  2.3 14.7 %all-to-all-start = ((f32[16,8,1024]{2,1,0:T(8,128)}), f32[16,8,1024]{2,1,0:T(8,128)S(1)}, u32[]{:S(2)}, u32[]{:S(2)}) async-start(f32[16,8,1024]{2,1,0:T(8,128)} %broadcast_in_dim.2), calls=%async_computation | async-start | bytes 1048576 | tf_op jit(solution)/shard_map/all_to_all | solution.py:239
  17.0 1.3 %shard_map.94 = (f32[136,1024]{1,0:T(8,128)S(1)}, f32[128,1024]{1,0:T(8,128)S(1)}) custom-call(f32[256,1024]{1,0:T(8,128)} %images_ref.1, f32[4,1024]{1,0:T(4,128)} %audio_ref, s32[1,256]{1,0:T(1,128)} %bitcast.6, s32[1,256]{1,0:T(1,128)} %bitcast.7), custom_call_target="tpu_custom_call" | custom-call | bytes 1048576 | tf_op jit(solution)/shard_map/pallas_call | solution.py:242
  18.3 2.9 %collective-permute-start = (f32[136,1024]{1,0:T(8,128)S(1)}, f32[136,1024]{1,0:T(8,128)S(1)}, u32[]{:S(2)}, u32[]{:S(2)}) collective-permute-start(f32[136,1024]{1,0:T(8,128)S(1)} %get-tuple-element.31.own_ref.own_a), channel_id=1, source_target_pairs={{0,1},{1,0},{2,3},{3,2},{4,5},{5,4},{6,7},{7,6},{8,9},{9,8},{10,11... | collective-permute-start | bytes 1671176 | tf_op jit(solution)/shard_map/ppermute | solution.py:245
  21.2 1.9 %collective-permute-start.1 = (f32[128,1024]{1,0:T(8,128)S(1)}, f32[128,1024]{1,0:T(8,128)S(1)}, u32[]{:S(2)}, u32[]{:S(2)}) collective-permute-start(f32[128,1024]{1,0:T(8,128)S(1)} %get-tuple-element.32.own_b), channel_id=1, source_target_pairs={{0,1},{1,0},{2,3},{3,2},{4,5},{5,4},{6,7},{7,6},{8,9},{9,8},{10,11... | collective-permute-start | bytes 1572872 | tf_op jit(solution)/shard_map/ppermute | solution.py:246
  23.1 0.0 collective-permute-done.far_ref.other_a
  23.1 6.1 %collective-permute-start.2 = (f32[8,1024]{1,0:T(8,128)S(1)}, f32[8,1024]{1,0:T(8,128)S(1)}, u32[]{:S(2)}, u32[]{:S(2)}) collective-permute-start(f32[8,1024]{1,0:T(8,128)S(1)} %shard_map.95), channel_id=1, source_target_pairs={{0,30},{1,31},{2,0},{3,1},{4,2},{5,3},{6,4},{7,5},{8,6},{9,7},{10,... | collective-permute-start | bytes 98312 | tf_op jit(solution)/shard_map/ppermute | solution.py:256
  30.5 0.0 collective-permute-done.1.other_b
  30.5 1.3 %collective-permute-done.2.next_pair = f32[8,1024]{1,0:T(8,128)S(1)} collective-permute-done((f32[8,1024]{1,0:T(8,128)S(1)}, f32[8,1024]{1,0:T(8,128)S(1)}, u32[]{:S(2)}, u32[]{:S(2)}) %collective-permute-start.2) | collective-permute-done | bytes 32800 | tf_op jit(solution)/shard_map/ppermute | solution.py:256
  31.8 0.0 all-to-all-done
  31.8 5.3 %shard_map.96 = (bf16[2048,512]{1,0:T(8,128)(2,1)}, f32[8,8,16,128]{3,2,1,0:T(8,128)}, f32[4,1024]{1,0:T(4,128)S(1)}, f32[4,1024]{1,0:T(4,128)S(1)}, f32[4,1024]...) custom-call(s32[1]{0:T(128)} %bitcast.core_ref, f32[1]{0:T(128)S(6)} %copy.10.scale_ref, ...), custom_call_target="tpu_custom_call" | custom-call | flops 3300000000 | bytes 4194304 | tf_op jit(solution)/shard_map/pallas_call | solution.py:258
  37.1 7.4 %all-to-all-start.1 = ((f32[8,8,16,128]{3,2,1,0:T(8,128)}), f32[8,8,16,128]{3,2,1,0:T(8,128)S(1)}, u32[]{:S(2)}, u32[]{:S(2)}) async-start(f32[8,8,16,128]{3,2,1,0:T(8,128)} %get-tuple-element.33), calls=%async_computation.1 | async-start | bytes 1048576 | tf_op jit(solution)/shard_map/all_to_all | solution.py:284
  44.5 3.1 %collective-permute-start.3 = (f32[4,1024]{1,0:T(4,128)S(1)}, f32[4,1024]{1,0:T(4,128)S(1)}, u32[]{:S(2)}, u32[]{:S(2)}) collective-permute-start(f32[4,1024]{1,0:T(4,128)S(1)} %get-tuple-element.36), channel_id=1, source_target_pairs={{0,1},{1,0},{2,3},{3,2},{4,5},{5,4},{6,7},{7,6},{8,9},{9,8},{10,11... | collective-permute-start | bytes 49160 | tf_op jit(solution)/shard_map/ppermute | solution.py:289
  47.6 3.6 %collective-permute-start.4 = (f32[4,1024]{1,0:T(4,128)S(1)}, f32[4,1024]{1,0:T(4,128)S(1)}, u32[]{:S(2)}, u32[]{:S(2)}) collective-permute-start(f32[4,1024]{1,0:T(4,128)S(1)} %get-tuple-element.42), channel_id=1, source_target_pairs={{0,2},{1,3},{2,4},{3,5},{4,6},{5,7},{6,8},{7,9},{8,10},{9,11},{10,... | collective-permute-start | bytes 49160 | tf_op jit(solution)/shard_map/ppermute | solution.py:287
  51.3 3.3 %collective-permute-start.5 = (f32[4,1024]{1,0:T(4,128)S(1)}, f32[4,1024]{1,0:T(4,128)S(1)}, u32[]{:S(2)}, u32[]{:S(2)}) collective-permute-start(f32[4,1024]{1,0:T(4,128)S(1)} %get-tuple-element.43), channel_id=1, source_target_pairs={{0,3},{1,2},{2,5},{3,4},{4,7},{5,6},{6,9},{7,8},{8,11},{9,10},{10,... | collective-permute-start | bytes 49160 | tf_op jit(solution)/shard_map/ppermute | solution.py:288
  54.5 0.0 collective-permute-done.3.came_ref
  54.6 3.2 %shard_map.97 = (f32[256,1024]{1,0:T(8,128)S(1)}, f32[128,1024]{1,0:T(8,128)S(1)}, f32[128,1024]{1,0:T(8,128)S(1)}) custom-call(s32[1]{0:T(128)} %bitcast.core_ref, f32[128,1024]{1,0:T(8,128)S(1)} %bitcast.5, f32[16,1024]{1,0:T(8,128)S(1)} %get-tuple-element.37.window_ref, bf16[2048,512]{1,0:T(8,128)(2,1)} %get-tuple-element.38.slope_hbm), custom_call_target="tpu_custom_call" | custom-call | flops 1700000000 | bytes 5242880 | tf_op jit(solution)/shard_map/pallas_call | solution.py:293
  57.8 0.0 collective-permute-done.4.next_ref
  57.8 4.9 %collective-permute-done.5.far_ref = f32[4,1024]{1,0:T(4,128)S(1)} collective-permute-done((f32[4,1024]{1,0:T(4,128)S(1)}, f32[4,1024]{1,0:T(4,128)S(1)}, u32[]{:S(2)}, u32[]{:S(2)}) %collective-permute-start.5) | collective-permute-done | bytes 16416 | tf_op jit(solution)/shard_map/ppermute | solution.py:288
  62.7 0.0 all-to-all-done.1.parts_ref
  62.7 0.7 shard_map.98
  63.4 4.8 %all-to-all-start.2 = ((f32[8,48,128]{2,1,0:T(8,128)}), f32[8,48,128]{2,1,0:T(8,128)S(1)}, u32[]{:S(2)}, u32[]{:S(2)}) async-start(f32[8,48,128]{2,1,0:T(8,128)} %shard_map.98), calls=%async_computation.2 | async-start | bytes 393216 | tf_op jit(solution)/shard_map/all_to_all | solution.py:309
  68.2 3.1 %collective-permute-start.7 = (f32[128,1024]{1,0:T(8,128)S(1)}, f32[128,1024]{1,0:T(8,128)S(1)}, u32[]{:S(2)}, u32[]{:S(2)}) collective-permute-start(f32[128,1024]{1,0:T(8,128)S(1)} %get-tuple-element.48), channel_id=1, source_target_pairs={{0,1},{1,0},{2,3},{3,2},{4,5},{5,4},{6,7},{7,6},{8,9},{9,8},{10,11... | collective-permute-start | bytes 1572872 | tf_op jit(solution)/shard_map/ppermute | solution.py:315
  71.3 1.9 %collective-permute-start.8 = (f32[128,1024]{1,0:T(8,128)S(1)}, f32[128,1024]{1,0:T(8,128)}, u32[]{:S(2)}, u32[]{:S(2)}) collective-permute-start(f32[128,1024]{1,0:T(8,128)S(1)} %get-tuple-element.49), channel_id=1, source_target_pairs={{0,1},{1,0},{2,3},{3,2},{4,5},{5,4},{6,7},{7,6},{8,9},{9,8},{10,11... | collective-permute-start | bytes 1572872 | tf_op jit(solution)/shard_map/ppermute | solution.py:315
  73.2 3.6 %all-to-all-done.2.parts_ref = f32[8,48,128]{2,1,0:T(8,128)S(1)} async-done(((f32[8,48,128]{2,1,0:T(8,128)}), f32[8,48,128]{2,1,0:T(8,128)S(1)}, u32[]{:S(2)}, u32[]{:S(2)}) %all-to-all-start.2) | async-done | bytes 196640 | tf_op jit(solution)/shard_map/all_to_all | solution.py:309
  76.8 0.7 shard_map.99
  77.6 7.1 %all-to-all-start.3 = ((f32[32,16,128]{2,1,0:T(8,128)}), f32[32,16,128]{2,1,0:T(8,128)S(1)}, u32[]{:S(2)}, u32[]{:S(2)}) async-start(f32[32,16,128]{2,1,0:T(8,128)} %get-tuple-element.51), calls=%async_computation.3 | async-start | bytes 524288 | tf_op jit(solution)/shard_map/all_to_all | solution.py:313
  84.6 4.2 %collective-permute-start.6 = (f32[4,1024]{1,0:T(4,128)S(1)}, f32[4,1024]{1,0:T(4,128)S(1)}, u32[]{:S(2)}, u32[]{:S(2)}) collective-permute-start(f32[4,1024]{1,0:T(4,128)S(1)} %get-tuple-element.44.mine_ref), channel_id=1, source_target_pairs={{0,256},{32,288},{64,320},{96,352},{128,384},{160,416},{192,448},{... | collective-permute-start | bytes 49160 | tf_op jit(solution)/shard_map/ppermute | solution.py:314
  88.8 0.0 collective-permute-done.7
  88.8 0.0 collective-permute-done.8
  88.9 2.1 %maximum_add_fusion = f32[256,1024]{1,0:T(8,128)} fusion(f32[256,1024]{1,0:T(8,128)S(1)} %get-tuple-element.45, f32[128,1024]{1,0:T(8,128)} %collective-permute-done.8, f32[128,1024]{1,0:T(8,128)S(1)} %collective-permute-done.7), kind=kLoop, calls=%fused_computation | loop fusion | flops 524288 | bytes 3145728 | tf_op jit(solution)/shard_map/add | solution.py:316
  91.0 2.3 %collective-permute-done.6.fixed_ref = f32[4,1024]{1,0:T(4,128)S(1)} collective-permute-done((f32[4,1024]{1,0:T(4,128)S(1)}, f32[4,1024]{1,0:T(4,128)S(1)}, u32[]{:S(2)}, u32[]{:S(2)}) %collective-permute-start.6) | collective-permute-done | bytes 16416 | tf_op jit(solution)/shard_map/ppermute | solution.py:314
  93.3 2.8 %all-to-all-done.3.pieces_ref = f32[32,16,128]{2,1,0:T(8,128)S(1)} async-done(((f32[32,16,128]{2,1,0:T(8,128)}), f32[32,16,128]{2,1,0:T(8,128)S(1)}, u32[]{:S(2)}, u32[]{:S(2)}) %all-to-all-start.3) | async-done | bytes 262176 | tf_op jit(solution)/shard_map/all_to_all | solution.py:313
  96.1 0.7 shard_map.100
  (2 shorter events, 0.0 us)
Async XLA Ops:
  0.6 0.8 copy-start
  2.3 29.5 %all-to-all-start = ((f32[16,8,1024]{2,1,0:T(8,128)}), f32[16,8,1024]{2,1,0:T(8,128)S(1)}, u32[]{:S(2)}, u32[]{:S(2)}) async-start(f32[16,8,1024]{2,1,0:T(8,128)} %broadcast_in_dim.2), calls=%async_computation | async-start | bytes 1048576 | tf_op jit(solution)/shard_map/all_to_all | solution.py:239
  18.3 4.8 %collective-permute-start = (f32[136,1024]{1,0:T(8,128)S(1)}, f32[136,1024]{1,0:T(8,128)S(1)}, u32[]{:S(2)}, u32[]{:S(2)}) collective-permute-start(f32[136,1024]{1,0:T(8,128)S(1)} %get-tuple-element.31.own_ref.own_a), channel_id=1, source_target_pairs={{0,1},{1,0},{2,3},{3,2},{4,5},{5,4},{6,7},{7,6},{8,9},{9,8},{10,11... | collective-permute-start | bytes 1671176 | tf_op jit(solution)/shard_map/ppermute | solution.py:245
  21.2 9.3 %collective-permute-start.1 = (f32[128,1024]{1,0:T(8,128)S(1)}, f32[128,1024]{1,0:T(8,128)S(1)}, u32[]{:S(2)}, u32[]{:S(2)}) collective-permute-start(f32[128,1024]{1,0:T(8,128)S(1)} %get-tuple-element.32.own_b), channel_id=1, source_target_pairs={{0,1},{1,0},{2,3},{3,2},{4,5},{5,4},{6,7},{7,6},{8,9},{9,8},{10,11... | collective-permute-start | bytes 1572872 | tf_op jit(solution)/shard_map/ppermute | solution.py:246
  23.1 8.7 %collective-permute-start.2 = (f32[8,1024]{1,0:T(8,128)S(1)}, f32[8,1024]{1,0:T(8,128)S(1)}, u32[]{:S(2)}, u32[]{:S(2)}) collective-permute-start(f32[8,1024]{1,0:T(8,128)S(1)} %shard_map.95), channel_id=1, source_target_pairs={{0,30},{1,31},{2,0},{3,1},{4,2},{5,3},{6,4},{7,5},{8,6},{9,7},{10,... | collective-permute-start | bytes 98312 | tf_op jit(solution)/shard_map/ppermute | solution.py:256
  37.1 25.6 %all-to-all-start.1 = ((f32[8,8,16,128]{3,2,1,0:T(8,128)}), f32[8,8,16,128]{3,2,1,0:T(8,128)S(1)}, u32[]{:S(2)}, u32[]{:S(2)}) async-start(f32[8,8,16,128]{3,2,1,0:T(8,128)} %get-tuple-element.33), calls=%async_computation.1 | async-start | bytes 1048576 | tf_op jit(solution)/shard_map/all_to_all | solution.py:284
  44.5 10.0 %collective-permute-start.3 = (f32[4,1024]{1,0:T(4,128)S(1)}, f32[4,1024]{1,0:T(4,128)S(1)}, u32[]{:S(2)}, u32[]{:S(2)}) collective-permute-start(f32[4,1024]{1,0:T(4,128)S(1)} %get-tuple-element.36), channel_id=1, source_target_pairs={{0,1},{1,0},{2,3},{3,2},{4,5},{5,4},{6,7},{7,6},{8,9},{9,8},{10,11... | collective-permute-start | bytes 49160 | tf_op jit(solution)/shard_map/ppermute | solution.py:289
  47.6 10.2 %collective-permute-start.4 = (f32[4,1024]{1,0:T(4,128)S(1)}, f32[4,1024]{1,0:T(4,128)S(1)}, u32[]{:S(2)}, u32[]{:S(2)}) collective-permute-start(f32[4,1024]{1,0:T(4,128)S(1)} %get-tuple-element.42), channel_id=1, source_target_pairs={{0,2},{1,3},{2,4},{3,5},{4,6},{5,7},{6,8},{7,9},{8,10},{9,11},{10,... | collective-permute-start | bytes 49160 | tf_op jit(solution)/shard_map/ppermute | solution.py:287
  51.3 11.4 %collective-permute-start.5 = (f32[4,1024]{1,0:T(4,128)S(1)}, f32[4,1024]{1,0:T(4,128)S(1)}, u32[]{:S(2)}, u32[]{:S(2)}) collective-permute-start(f32[4,1024]{1,0:T(4,128)S(1)} %get-tuple-element.43), channel_id=1, source_target_pairs={{0,3},{1,2},{2,5},{3,4},{4,7},{5,6},{6,9},{7,8},{8,11},{9,10},{10,... | collective-permute-start | bytes 49160 | tf_op jit(solution)/shard_map/ppermute | solution.py:288
  63.4 13.4 %all-to-all-start.2 = ((f32[8,48,128]{2,1,0:T(8,128)}), f32[8,48,128]{2,1,0:T(8,128)S(1)}, u32[]{:S(2)}, u32[]{:S(2)}) async-start(f32[8,48,128]{2,1,0:T(8,128)} %shard_map.98), calls=%async_computation.2 | async-start | bytes 393216 | tf_op jit(solution)/shard_map/all_to_all | solution.py:309
  68.2 20.6 %collective-permute-start.7 = (f32[128,1024]{1,0:T(8,128)S(1)}, f32[128,1024]{1,0:T(8,128)S(1)}, u32[]{:S(2)}, u32[]{:S(2)}) collective-permute-start(f32[128,1024]{1,0:T(8,128)S(1)} %get-tuple-element.48), channel_id=1, source_target_pairs={{0,1},{1,0},{2,3},{3,2},{4,5},{5,4},{6,7},{7,6},{8,9},{9,8},{10,11... | collective-permute-start | bytes 1572872 | tf_op jit(solution)/shard_map/ppermute | solution.py:315
  71.3 17.5 %collective-permute-start.8 = (f32[128,1024]{1,0:T(8,128)S(1)}, f32[128,1024]{1,0:T(8,128)}, u32[]{:S(2)}, u32[]{:S(2)}) collective-permute-start(f32[128,1024]{1,0:T(8,128)S(1)} %get-tuple-element.49), channel_id=1, source_target_pairs={{0,1},{1,0},{2,3},{3,2},{4,5},{5,4},{6,7},{7,6},{8,9},{9,8},{10,11... | collective-permute-start | bytes 1572872 | tf_op jit(solution)/shard_map/ppermute | solution.py:315
  77.6 18.5 %all-to-all-start.3 = ((f32[32,16,128]{2,1,0:T(8,128)}), f32[32,16,128]{2,1,0:T(8,128)S(1)}, u32[]{:S(2)}, u32[]{:S(2)}) async-start(f32[32,16,128]{2,1,0:T(8,128)} %get-tuple-element.51), calls=%async_computation.3 | async-start | bytes 524288 | tf_op jit(solution)/shard_map/all_to_all | solution.py:313
  84.6 8.7 %collective-permute-start.6 = (f32[4,1024]{1,0:T(4,128)S(1)}, f32[4,1024]{1,0:T(4,128)S(1)}, u32[]{:S(2)}, u32[]{:S(2)}) collective-permute-start(f32[4,1024]{1,0:T(4,128)S(1)} %get-tuple-element.44.mine_ref), channel_id=1, source_target_pairs={{0,256},{32,288},{64,320},{96,352},{128,384},{160,416},{192,448},{... | collective-permute-start | bytes 49160 | tf_op jit(solution)/shard_map/ppermute | solution.py:314

commit v4 on v3

--- a/solution.py
+++ b/solution.py
@@ -29,7 +29,7 @@
     return [found[k] for k in sorted(found)]
 
 
-TEXT_GROUPS = groups_by(lambda high, z, x, low, core: (x, low if high == 0 else low ^ 2, core))
+TEXT_GROUPS = groups_by(lambda high, z, x, low, core: (x, low if high == 0 else 3 - low, core))
 Y_GROUPS = groups_by(lambda high, z, x, low, core: (z, x, core))
 Z_GROUPS = groups_by(lambda high, z, x, low, core: (high, x, low, core))
 

time: 97.6 us -> 96 us (0.984)
  starting transfers between devices: 64 us -> 61.3 us
  waiting for transfers between devices: 14.9 us -> 16 us
    all_to_all x1, starting transfers between devices: 7.4 us -> 4.76 us  [shards(): lax.all_to_all(text_parts, BOTH, 0, 0, tiled=True, axis_index_groups=Y_GR...]
    all_to_all x1, waiting for transfers between devices: 0.01 us -> 2.44 us  [shards(): lax.all_to_all(spread, BOTH, 0, 0, tiled=True, axis_index_groups=TEXT_GRO...]
    ppermute x1, waiting for transfers between devices: 1.29 us -> 0.01 us  [shards(): next_pair = lax.ppermute(pair, 'aud', FROM_NEXT)]
    all_to_all x1, waiting for transfers between devices: 3.6 us -> 4.85 us  [shards(): lax.all_to_all(second, BOTH, 0, 0, tiled=True, axis_index_groups=Z_GROUPS)]
    all_to_all x1, starting transfers between devices: 7.06 us -> 6.02 us  [shards(): pieces = lax.all_to_all(piece, 'aud', 0, 0, tiled=True)]
    ppermute x1, starting transfers between devices: 3.08 us -> 4.09 us  [shards(): lax.ppermute(send_self, 'aud', OTHER_CORE)]
  transfers between devices with their start and end apart: 13 -> 13, of which waited for: 5 -> 5; matrix products, arithmetic and copies ran while one was open for 2% -> 2% of each run, Pallas kernels for 5% -> 6%
where the time goes in v4:
time: 96 us; the launch traced here: 95.2 us
  starting transfers between devices  61.3 us (64%)
  waiting for transfers between devices  16 us (17%)
  Pallas kernels  12 us (12%)
  other arithmetic  2.15 us (2%)
  between operations  2.12 us (2%)
  local copies, waits for them, and re-layouts  1.67 us (2%)
    all_to_all x1, starting transfers between devices, shards(): lax.all_to_all(spread, BOTH, 0, 0, tiled=True, axis_index_groups=TEXT_GRO...  13.9 us
    ppermute x1, starting transfers between devices, shards(): next_pair = lax.ppermute(pair, 'aud', FROM_NEXT)  6.74 us
    all_to_all x1, starting transfers between devices, shards(): pieces = lax.all_to_all(piece, 'aud', 0, 0, tiled=True)  6.02 us
    pallas_call x1, Pallas kernels, shards(): call(slope_kernel, [pltpu.HBM((2048, 512), BF16), ((8, 8, 16, 128), F32),...  5.3 us
    all_to_all x1, starting transfers between devices, shards(): lax.all_to_all(second, BOTH, 0, 0, tiled=True, axis_index_groups=Z_GROUPS)  5.06 us
    all_to_all x1, waiting for transfers between devices, shards(): lax.all_to_all(second, BOTH, 0, 0, tiled=True, axis_index_groups=Z_GROUPS)  4.85 us
    all_to_all x1, starting transfers between devices, shards(): lax.all_to_all(text_parts, BOTH, 0, 0, tiled=True, axis_index_groups=Y_GR...  4.76 us
    ppermute x2, starting transfers between devices, shards(): came_grads = [lax.ppermute(grad, 'aud', OTHER_CORE) for grad in other_grads]  4.51 us
  transfers between devices with their start and end apart: 13, of which 5 were waited for; matrix products, arithmetic and copies ran while one was open for 2% of the time, Pallas kernels for 6%

profile of v4, /device:TPU:1, one launch (start us, length us, event | category | flops | bytes accessed | tf_op | source)
XLA Modules:
  0.0 95.2 jit_solution(3006246437954511940)
XLA Ops:
  0.6 0.0 copy-start
  0.7 0.8 copy-done
  1.5 0.8 broadcast_in_dim.2
  2.3 13.9 %all-to-all-start = ((f32[16,8,1024]{2,1,0:T(8,128)}), f32[16,8,1024]{2,1,0:T(8,128)S(1)}, u32[]{:S(2)}, u32[]{:S(2)}) async-start(f32[16,8,1024]{2,1,0:T(8,128)} %broadcast_in_dim.2), calls=%async_computation | async-start | bytes 1048576 | tf_op jit(solution)/shard_map/all_to_all | solution.py:239
  16.2 1.3 %shard_map.94 = (f32[136,1024]{1,0:T(8,128)S(1)}, f32[128,1024]{1,0:T(8,128)S(1)}) custom-call(f32[256,1024]{1,0:T(8,128)} %images_ref.1, f32[4,1024]{1,0:T(4,128)} %audio_ref, s32[1,256]{1,0:T(1,128)} %bitcast.6, s32[1,256]{1,0:T(1,128)} %bitcast.7), custom_call_target="tpu_custom_call" | custom-call | bytes 1048576 | tf_op jit(solution)/shard_map/pallas_call | solution.py:242
  17.5 2.9 %collective-permute-start = (f32[136,1024]{1,0:T(8,128)S(1)}, f32[136,1024]{1,0:T(8,128)S(1)}, u32[]{:S(2)}, u32[]{:S(2)}) collective-permute-start(f32[136,1024]{1,0:T(8,128)S(1)} %get-tuple-element.31.own_ref.own_a), channel_id=1, source_target_pairs={{0,1},{1,0},{2,3},{3,2},{4,5},{5,4},{6,7},{7,6},{8,9},{9,8},{10,11... | collective-permute-start | bytes 1671176 | tf_op jit(solution)/shard_map/ppermute | solution.py:245
  20.4 1.9 %collective-permute-start.1 = (f32[128,1024]{1,0:T(8,128)S(1)}, f32[128,1024]{1,0:T(8,128)S(1)}, u32[]{:S(2)}, u32[]{:S(2)}) collective-permute-start(f32[128,1024]{1,0:T(8,128)S(1)} %get-tuple-element.32.own_b), channel_id=1, source_target_pairs={{0,1},{1,0},{2,3},{3,2},{4,5},{5,4},{6,7},{7,6},{8,9},{9,8},{10,11... | collective-permute-start | bytes 1572872 | tf_op jit(solution)/shard_map/ppermute | solution.py:246
  22.3 0.0 collective-permute-done.far_ref.other_a
  22.4 6.7 %collective-permute-start.2 = (f32[8,1024]{1,0:T(8,128)S(1)}, f32[8,1024]{1,0:T(8,128)S(1)}, u32[]{:S(2)}, u32[]{:S(2)}) collective-permute-start(f32[8,1024]{1,0:T(8,128)S(1)} %shard_map.95), channel_id=1, source_target_pairs={{0,30},{1,31},{2,0},{3,1},{4,2},{5,3},{6,4},{7,5},{8,6},{9,7},{10,... | collective-permute-start | bytes 98312 | tf_op jit(solution)/shard_map/ppermute | solution.py:256
  30.4 0.0 collective-permute-done.1.other_b
  30.4 0.0 collective-permute-done.2.next_pair
  30.4 2.4 %all-to-all-done = f32[16,8,1024]{2,1,0:T(8,128)S(1)} async-done(((f32[16,8,1024]{2,1,0:T(8,128)}), f32[16,8,1024]{2,1,0:T(8,128)S(1)}, u32[]{:S(2)}, u32[]{:S(2)}) %all-to-all-start) | async-done | bytes 524320 | tf_op jit(solution)/shard_map/all_to_all | solution.py:239
  32.9 5.3 %shard_map.96 = (bf16[2048,512]{1,0:T(8,128)(2,1)}, f32[8,8,16,128]{3,2,1,0:T(8,128)}, f32[4,1024]{1,0:T(4,128)S(1)}, f32[4,1024]{1,0:T(4,128)S(1)}, f32[4,1024]...) custom-call(s32[1]{0:T(128)} %bitcast.core_ref, f32[1]{0:T(128)S(6)} %copy.10.scale_ref, ...), custom_call_target="tpu_custom_call" | custom-call | flops 3300000000 | bytes 4194304 | tf_op jit(solution)/shard_map/pallas_call | solution.py:258
  38.2 4.8 %all-to-all-start.1 = ((f32[8,8,16,128]{3,2,1,0:T(8,128)}), f32[8,8,16,128]{3,2,1,0:T(8,128)S(1)}, u32[]{:S(2)}, u32[]{:S(2)}) async-start(f32[8,8,16,128]{3,2,1,0:T(8,128)} %get-tuple-element.33), calls=%async_computation.1 | async-start | bytes 1048576 | tf_op jit(solution)/shard_map/all_to_all | solution.py:284
  42.9 4.1 %collective-permute-start.3 = (f32[4,1024]{1,0:T(4,128)S(1)}, f32[4,1024]{1,0:T(4,128)S(1)}, u32[]{:S(2)}, u32[]{:S(2)}) collective-permute-start(f32[4,1024]{1,0:T(4,128)S(1)} %get-tuple-element.36), channel_id=1, source_target_pairs={{0,1},{1,0},{2,3},{3,2},{4,5},{5,4},{6,7},{7,6},{8,9},{9,8},{10,11... | collective-permute-start | bytes 49160 | tf_op jit(solution)/shard_map/ppermute | solution.py:289
  47.0 3.6 %collective-permute-start.4 = (f32[4,1024]{1,0:T(4,128)S(1)}, f32[4,1024]{1,0:T(4,128)S(1)}, u32[]{:S(2)}, u32[]{:S(2)}) collective-permute-start(f32[4,1024]{1,0:T(4,128)S(1)} %get-tuple-element.42), channel_id=1, source_target_pairs={{0,2},{1,3},{2,4},{3,5},{4,6},{5,7},{6,8},{7,9},{8,10},{9,11},{10,... | collective-permute-start | bytes 49160 | tf_op jit(solution)/shard_map/ppermute | solution.py:287
  50.7 3.3 %collective-permute-start.5 = (f32[4,1024]{1,0:T(4,128)S(1)}, f32[4,1024]{1,0:T(4,128)S(1)}, u32[]{:S(2)}, u32[]{:S(2)}) collective-permute-start(f32[4,1024]{1,0:T(4,128)S(1)} %get-tuple-element.43), channel_id=1, source_target_pairs={{0,3},{1,2},{2,5},{3,4},{4,7},{5,6},{6,9},{7,8},{8,11},{9,10},{10,... | collective-permute-start | bytes 49160 | tf_op jit(solution)/shard_map/ppermute | solution.py:288
  54.0 0.0 collective-permute-done.3.came_ref
  54.0 3.2 %shard_map.97 = (f32[256,1024]{1,0:T(8,128)S(1)}, f32[128,1024]{1,0:T(8,128)S(1)}, f32[128,1024]{1,0:T(8,128)S(1)}) custom-call(s32[1]{0:T(128)} %bitcast.core_ref, f32[128,1024]{1,0:T(8,128)S(1)} %bitcast.5, f32[16,1024]{1,0:T(8,128)S(1)} %get-tuple-element.37.window_ref, bf16[2048,512]{1,0:T(8,128)(2,1)} %get-tuple-element.38.slope_hbm), custom_call_target="tpu_custom_call" | custom-call | flops 1700000000 | bytes 5242880 | tf_op jit(solution)/shard_map/pallas_call | solution.py:293
  57.2 0.0 collective-permute-done.4.next_ref
  57.2 3.9 %collective-permute-done.5.far_ref = f32[4,1024]{1,0:T(4,128)S(1)} collective-permute-done((f32[4,1024]{1,0:T(4,128)S(1)}, f32[4,1024]{1,0:T(4,128)S(1)}, u32[]{:S(2)}, u32[]{:S(2)}) %collective-permute-start.5) | collective-permute-done | bytes 16416 | tf_op jit(solution)/shard_map/ppermute | solution.py:288
  61.1 0.0 all-to-all-done.1.parts_ref
  61.1 0.7 shard_map.98
  61.9 5.1 %all-to-all-start.2 = ((f32[8,48,128]{2,1,0:T(8,128)}), f32[8,48,128]{2,1,0:T(8,128)S(1)}, u32[]{:S(2)}, u32[]{:S(2)}) async-start(f32[8,48,128]{2,1,0:T(8,128)} %shard_map.98), calls=%async_computation.2 | async-start | bytes 393216 | tf_op jit(solution)/shard_map/all_to_all | solution.py:309
  66.9 2.6 %collective-permute-start.7 = (f32[128,1024]{1,0:T(8,128)S(1)}, f32[128,1024]{1,0:T(8,128)S(1)}, u32[]{:S(2)}, u32[]{:S(2)}) collective-permute-start(f32[128,1024]{1,0:T(8,128)S(1)} %get-tuple-element.48), channel_id=1, source_target_pairs={{0,1},{1,0},{2,3},{3,2},{4,5},{5,4},{6,7},{7,6},{8,9},{9,8},{10,11... | collective-permute-start | bytes 1572872 | tf_op jit(solution)/shard_map/ppermute | solution.py:315
  69.5 1.9 %collective-permute-start.8 = (f32[128,1024]{1,0:T(8,128)S(1)}, f32[128,1024]{1,0:T(8,128)}, u32[]{:S(2)}, u32[]{:S(2)}) collective-permute-start(f32[128,1024]{1,0:T(8,128)S(1)} %get-tuple-element.49), channel_id=1, source_target_pairs={{0,1},{1,0},{2,3},{3,2},{4,5},{5,4},{6,7},{7,6},{8,9},{9,8},{10,11... | collective-permute-start | bytes 1572872 | tf_op jit(solution)/shard_map/ppermute | solution.py:315
  71.5 4.8 %all-to-all-done.2.parts_ref = f32[8,48,128]{2,1,0:T(8,128)S(1)} async-done(((f32[8,48,128]{2,1,0:T(8,128)}), f32[8,48,128]{2,1,0:T(8,128)S(1)}, u32[]{:S(2)}, u32[]{:S(2)}) %all-to-all-start.2) | async-done | bytes 196640 | tf_op jit(solution)/shard_map/all_to_all | solution.py:309
  76.3 0.7 shard_map.99
  77.0 6.0 %all-to-all-start.3 = ((f32[32,16,128]{2,1,0:T(8,128)}), f32[32,16,128]{2,1,0:T(8,128)S(1)}, u32[]{:S(2)}, u32[]{:S(2)}) async-start(f32[32,16,128]{2,1,0:T(8,128)} %get-tuple-element.51), calls=%async_computation.3 | async-start | bytes 524288 | tf_op jit(solution)/shard_map/all_to_all | solution.py:313
  83.1 4.5 %collective-permute-start.6 = (f32[4,1024]{1,0:T(4,128)S(1)}, f32[4,1024]{1,0:T(4,128)S(1)}, u32[]{:S(2)}, u32[]{:S(2)}) collective-permute-start(f32[4,1024]{1,0:T(4,128)S(1)} %get-tuple-element.44.mine_ref), channel_id=1, source_target_pairs={{0,256},{32,288},{64,320},{96,352},{128,384},{160,416},{192,448},{... | collective-permute-start | bytes 49160 | tf_op jit(solution)/shard_map/ppermute | solution.py:314
  87.6 0.0 collective-permute-done.7
  87.6 0.0 collective-permute-done.8
  87.6 2.1 %maximum_add_fusion = f32[256,1024]{1,0:T(8,128)} fusion(f32[256,1024]{1,0:T(8,128)S(1)} %get-tuple-element.45, f32[128,1024]{1,0:T(8,128)} %collective-permute-done.8, f32[128,1024]{1,0:T(8,128)S(1)} %collective-permute-done.7), kind=kLoop, calls=%fused_computation | loop fusion | flops 524288 | bytes 3145728 | tf_op jit(solution)/shard_map/add | solution.py:316
  89.7 2.0 %collective-permute-done.6.fixed_ref = f32[4,1024]{1,0:T(4,128)S(1)} collective-permute-done((f32[4,1024]{1,0:T(4,128)S(1)}, f32[4,1024]{1,0:T(4,128)S(1)}, u32[]{:S(2)}, u32[]{:S(2)}) %collective-permute-start.6) | collective-permute-done | bytes 16416 | tf_op jit(solution)/shard_map/ppermute | solution.py:314
  91.7 2.8 %all-to-all-done.3.pieces_ref = f32[32,16,128]{2,1,0:T(8,128)S(1)} async-done(((f32[32,16,128]{2,1,0:T(8,128)}), f32[32,16,128]{2,1,0:T(8,128)S(1)}, u32[]{:S(2)}, u32[]{:S(2)}) %all-to-all-start.3) | async-done | bytes 262176 | tf_op jit(solution)/shard_map/all_to_all | solution.py:313
  94.5 0.7 shard_map.100
  (2 shorter events, 0.0 us)
Async XLA Ops:
  0.6 0.8 copy-start
  2.3 30.5 %all-to-all-start = ((f32[16,8,1024]{2,1,0:T(8,128)}), f32[16,8,1024]{2,1,0:T(8,128)S(1)}, u32[]{:S(2)}, u32[]{:S(2)}) async-start(f32[16,8,1024]{2,1,0:T(8,128)} %broadcast_in_dim.2), calls=%async_computation | async-start | bytes 1048576 | tf_op jit(solution)/shard_map/all_to_all | solution.py:239
  17.5 4.8 %collective-permute-start = (f32[136,1024]{1,0:T(8,128)S(1)}, f32[136,1024]{1,0:T(8,128)S(1)}, u32[]{:S(2)}, u32[]{:S(2)}) collective-permute-start(f32[136,1024]{1,0:T(8,128)S(1)} %get-tuple-element.31.own_ref.own_a), channel_id=1, source_target_pairs={{0,1},{1,0},{2,3},{3,2},{4,5},{5,4},{6,7},{7,6},{8,9},{9,8},{10,11... | collective-permute-start | bytes 1671176 | tf_op jit(solution)/shard_map/ppermute | solution.py:245
  20.4 10.0 %collective-permute-start.1 = (f32[128,1024]{1,0:T(8,128)S(1)}, f32[128,1024]{1,0:T(8,128)S(1)}, u32[]{:S(2)}, u32[]{:S(2)}) collective-permute-start(f32[128,1024]{1,0:T(8,128)S(1)} %get-tuple-element.32.own_b), channel_id=1, source_target_pairs={{0,1},{1,0},{2,3},{3,2},{4,5},{5,4},{6,7},{7,6},{8,9},{9,8},{10,11... | collective-permute-start | bytes 1572872 | tf_op jit(solution)/shard_map/ppermute | solution.py:246
  22.4 8.1 %collective-permute-start.2 = (f32[8,1024]{1,0:T(8,128)S(1)}, f32[8,1024]{1,0:T(8,128)S(1)}, u32[]{:S(2)}, u32[]{:S(2)}) collective-permute-start(f32[8,1024]{1,0:T(8,128)S(1)} %shard_map.95), channel_id=1, source_target_pairs={{0,30},{1,31},{2,0},{3,1},{4,2},{5,3},{6,4},{7,5},{8,6},{9,7},{10,... | collective-permute-start | bytes 98312 | tf_op jit(solution)/shard_map/ppermute | solution.py:256
  38.2 23.0 %all-to-all-start.1 = ((f32[8,8,16,128]{3,2,1,0:T(8,128)}), f32[8,8,16,128]{3,2,1,0:T(8,128)S(1)}, u32[]{:S(2)}, u32[]{:S(2)}) async-start(f32[8,8,16,128]{3,2,1,0:T(8,128)} %get-tuple-element.33), calls=%async_computation.1 | async-start | bytes 1048576 | tf_op jit(solution)/shard_map/all_to_all | solution.py:284
  42.9 11.0 %collective-permute-start.3 = (f32[4,1024]{1,0:T(4,128)S(1)}, f32[4,1024]{1,0:T(4,128)S(1)}, u32[]{:S(2)}, u32[]{:S(2)}) collective-permute-start(f32[4,1024]{1,0:T(4,128)S(1)} %get-tuple-element.36), channel_id=1, source_target_pairs={{0,1},{1,0},{2,3},{3,2},{4,5},{5,4},{6,7},{7,6},{8,9},{9,8},{10,11... | collective-permute-start | bytes 49160 | tf_op jit(solution)/shard_map/ppermute | solution.py:289
  47.0 10.2 %collective-permute-start.4 = (f32[4,1024]{1,0:T(4,128)S(1)}, f32[4,1024]{1,0:T(4,128)S(1)}, u32[]{:S(2)}, u32[]{:S(2)}) collective-permute-start(f32[4,1024]{1,0:T(4,128)S(1)} %get-tuple-element.42), channel_id=1, source_target_pairs={{0,2},{1,3},{2,4},{3,5},{4,6},{5,7},{6,8},{7,9},{8,10},{9,11},{10,... | collective-permute-start | bytes 49160 | tf_op jit(solution)/shard_map/ppermute | solution.py:287
  50.7 10.4 %collective-permute-start.5 = (f32[4,1024]{1,0:T(4,128)S(1)}, f32[4,1024]{1,0:T(4,128)S(1)}, u32[]{:S(2)}, u32[]{:S(2)}) collective-permute-start(f32[4,1024]{1,0:T(4,128)S(1)} %get-tuple-element.43), channel_id=1, source_target_pairs={{0,3},{1,2},{2,5},{3,4},{4,7},{5,6},{6,9},{7,8},{8,11},{9,10},{10,... | collective-permute-start | bytes 49160 | tf_op jit(solution)/shard_map/ppermute | solution.py:288
  61.9 14.4 %all-to-all-start.2 = ((f32[8,48,128]{2,1,0:T(8,128)}), f32[8,48,128]{2,1,0:T(8,128)S(1)}, u32[]{:S(2)}, u32[]{:S(2)}) async-start(f32[8,48,128]{2,1,0:T(8,128)} %shard_map.98), calls=%async_computation.2 | async-start | bytes 393216 | tf_op jit(solution)/shard_map/all_to_all | solution.py:309
  66.9 20.6 %collective-permute-start.7 = (f32[128,1024]{1,0:T(8,128)S(1)}, f32[128,1024]{1,0:T(8,128)S(1)}, u32[]{:S(2)}, u32[]{:S(2)}) collective-permute-start(f32[128,1024]{1,0:T(8,128)S(1)} %get-tuple-element.48), channel_id=1, source_target_pairs={{0,1},{1,0},{2,3},{3,2},{4,5},{5,4},{6,7},{7,6},{8,9},{9,8},{10,11... | collective-permute-start | bytes 1572872 | tf_op jit(solution)/shard_map/ppermute | solution.py:315
  69.5 18.0 %collective-permute-start.8 = (f32[128,1024]{1,0:T(8,128)S(1)}, f32[128,1024]{1,0:T(8,128)}, u32[]{:S(2)}, u32[]{:S(2)}) collective-permute-start(f32[128,1024]{1,0:T(8,128)S(1)} %get-tuple-element.49), channel_id=1, source_target_pairs={{0,1},{1,0},{2,3},{3,2},{4,5},{5,4},{6,7},{7,6},{8,9},{9,8},{10,11... | collective-permute-start | bytes 1572872 | tf_op jit(solution)/shard_map/ppermute | solution.py:315
  77.0 17.5 %all-to-all-start.3 = ((f32[32,16,128]{2,1,0:T(8,128)}), f32[32,16,128]{2,1,0:T(8,128)S(1)}, u32[]{:S(2)}, u32[]{:S(2)}) async-start(f32[32,16,128]{2,1,0:T(8,128)} %get-tuple-element.51), calls=%async_computation.3 | async-start | bytes 524288 | tf_op jit(solution)/shard_map/all_to_all | solution.py:313
  83.1 8.7 %collective-permute-start.6 = (f32[4,1024]{1,0:T(4,128)S(1)}, f32[4,1024]{1,0:T(4,128)S(1)}, u32[]{:S(2)}, u32[]{:S(2)}) collective-permute-start(f32[4,1024]{1,0:T(4,128)S(1)} %get-tuple-element.44.mine_ref), channel_id=1, source_target_pairs={{0,256},{32,288},{64,320},{96,352},{128,384},{160,416},{192,448},{... | collective-permute-start | bytes 49160 | tf_op jit(solution)/shard_map/ppermute | solution.py:314

commit v5 on v4

--- a/solution.py
+++ b/solution.py
@@ -29,7 +29,10 @@
     return [found[k] for k in sorted(found)]
 
 
-TEXT_GROUPS = groups_by(lambda high, z, x, low, core: (x, low if high == 0 else 3 - low, core))
+TEXT_GROUPS = [
+    [group[p % 2 * 8 + p // 2] for p in range(N_TXT)]
+    for group in groups_by(lambda high, z, x, low, core: (x, low if high == 0 else 3 - low, core))
+]
 Y_GROUPS = groups_by(lambda high, z, x, low, core: (z, x, core))
 Z_GROUPS = groups_by(lambda high, z, x, low, core: (high, x, low, core))
 
@@ -81,7 +84,8 @@
     text_pos = jnp.concatenate([low[:, 0:256], high[:, 0:256]], axis=1)
     slot_pos = jnp.concatenate([low[:, 256:512], high[:, 256:512] + 4], axis=1)
     rest = text_pos & 15
-    place = slot_pos * 128 + (text_pos >> 4) * 8 + (rest & 7)
+    block = text_pos >> 4
+    place = slot_pos * 128 + ((block & 7) * 2 + (block >> 3)) * 8 + (rest & 7)
     place = jnp.where((rest >> 3) == core, place, -1)
 
     def slope_copy(block):
@@ -132,11 +136,10 @@
                 if block < 3:
                     total[:, c : c + 128] = part
                     continue
-                for high_half in range(2):
-                    top = c // 128 % 2 * 8
-                    text_ref[high_half * 4 + c // 256, :, top : top + 8, :] = part[
-                        high_half * 64 : (high_half + 1) * 64, :
-                    ].reshape(8, 8, 128)
+                tiles = part.reshape(8, 16, 128)
+                top = c // 128 % 2 * 8
+                for half in range(2):
+                    text_ref[half * 4 + c // 256, :, top : top + 8, :] = tiles[:, half * 8 : half * 8 + 8, :]
 
     dots = logits_of(0)
     for block in range(4):

time: 96 us -> 95.7 us (level)
  waiting for transfers between devices: 16 us -> 11.5 us
  starting transfers between devices: 61.3 us -> 65.4 us
    all_to_all x1, starting transfers between devices: 4.76 us -> 8.5 us  [shards(): lax.all_to_all(text_parts, BOTH, 0, 0, tiled=True, axis_index_groups=Y_GR...]
    all_to_all x1, waiting for transfers between devices: 2.44 us -> 0.01 us  [shards(): lax.all_to_all(spread, BOTH, 0, 0, tiled=True, axis_index_groups=TEXT_GRO...]
    all_to_all x1, starting transfers between devices: 5.06 us -> 3.51 us  [shards(): lax.all_to_all(second, BOTH, 0, 0, tiled=True, axis_index_groups=Z_GROUPS)]
    all_to_all x1, waiting for transfers between devices: 4.85 us -> 3.86 us  [shards(): lax.all_to_all(second, BOTH, 0, 0, tiled=True, axis_index_groups=Z_GROUPS)]
  transfers between devices with their start and end apart: 13 -> 13, of which waited for: 5 -> 4; matrix products, arithmetic and copies ran while one was open for 2% -> 2% of each run, Pallas kernels for 6% -> 6%
where the time goes in v5:
time: 95.7 us; the launch traced here: 94.8 us
  starting transfers between devices  65.4 us (68%)
  Pallas kernels  11.9 us (12%)
  waiting for transfers between devices  11.5 us (12%)
  other arithmetic  2.15 us (2%)
  between operations  2.13 us (2%)
  local copies, waits for them, and re-layouts  1.67 us (2%)
    all_to_all x1, starting transfers between devices, shards(): lax.all_to_all(spread, BOTH, 0, 0, tiled=True, axis_index_groups=TEXT_GRO...  13.9 us
    all_to_all x1, starting transfers between devices, shards(): lax.all_to_all(text_parts, BOTH, 0, 0, tiled=True, axis_index_groups=Y_GR...  8.5 us
    ppermute x1, starting transfers between devices, shards(): next_pair = lax.ppermute(pair, 'aud', FROM_NEXT)  6.74 us
    all_to_all x1, starting transfers between devices, shards(): pieces = lax.all_to_all(piece, 'aud', 0, 0, tiled=True)  6.67 us
    pallas_call x1, Pallas kernels, shards(): call(slope_kernel, [pltpu.HBM((2048, 512), BF16), ((8, 8, 16, 128), F32),...  5.29 us
    ppermute x1, starting transfers between devices, shards(): fixed = lax.ppermute(mine, 'txt', OTHER_HALF)  5.14 us
    ppermute x2, starting transfers between devices, shards(): came_grads = [lax.ppermute(grad, 'aud', OTHER_CORE) for grad in other_grads]  4.85 us
    ppermute x1, starting transfers between devices, shards(): lax.ppermute(send_self, 'aud', OTHER_CORE)  4.38 us
  transfers between devices with their start and end apart: 13, of which 4 were waited for; matrix products, arithmetic and copies ran while one was open for 2% of the time, Pallas kernels for 6%

profile of v5, /device:TPU:1, one launch (start us, length us, event | category | flops | bytes accessed | tf_op | source)
XLA Modules:
  0.0 94.8 jit_solution(12665947400654106972)
XLA Ops:
  0.6 0.0 copy-start
  0.7 0.8 copy-done
  1.5 0.8 broadcast_in_dim.2
  2.3 13.9 %all-to-all-start = ((f32[16,8,1024]{2,1,0:T(8,128)}), f32[16,8,1024]{2,1,0:T(8,128)S(1)}, u32[]{:S(2)}, u32[]{:S(2)}) async-start(f32[16,8,1024]{2,1,0:T(8,128)} %broadcast_in_dim.2), calls=%async_computation | async-start | bytes 1048576 | tf_op jit(solution)/shard_map/all_to_all | solution.py:242
  16.2 1.3 %shard_map.94 = (f32[136,1024]{1,0:T(8,128)S(1)}, f32[128,1024]{1,0:T(8,128)S(1)}) custom-call(f32[256,1024]{1,0:T(8,128)} %images_ref.1, f32[4,1024]{1,0:T(4,128)} %audio_ref, s32[1,256]{1,0:T(1,128)} %bitcast.6, s32[1,256]{1,0:T(1,128)} %bitcast.7), custom_call_target="tpu_custom_call" | custom-call | bytes 1048576 | tf_op jit(solution)/shard_map/pallas_call | solution.py:245
  17.5 2.9 %collective-permute-start = (f32[136,1024]{1,0:T(8,128)S(1)}, f32[136,1024]{1,0:T(8,128)S(1)}, u32[]{:S(2)}, u32[]{:S(2)}) collective-permute-start(f32[136,1024]{1,0:T(8,128)S(1)} %get-tuple-element.31.own_ref.own_a), channel_id=1, source_target_pairs={{0,1},{1,0},{2,3},{3,2},{4,5},{5,4},{6,7},{7,6},{8,9},{9,8},{10,11... | collective-permute-start | bytes 1671176 | tf_op jit(solution)/shard_map/ppermute | solution.py:248
  20.4 1.9 %collective-permute-start.1 = (f32[128,1024]{1,0:T(8,128)S(1)}, f32[128,1024]{1,0:T(8,128)S(1)}, u32[]{:S(2)}, u32[]{:S(2)}) collective-permute-start(f32[128,1024]{1,0:T(8,128)S(1)} %get-tuple-element.32.own_b), channel_id=1, source_target_pairs={{0,1},{1,0},{2,3},{3,2},{4,5},{5,4},{6,7},{7,6},{8,9},{9,8},{10,11... | collective-permute-start | bytes 1572872 | tf_op jit(solution)/shard_map/ppermute | solution.py:249
  22.3 0.0 collective-permute-done.far_ref.other_a
  22.4 6.7 %collective-permute-start.2 = (f32[8,1024]{1,0:T(8,128)S(1)}, f32[8,1024]{1,0:T(8,128)S(1)}, u32[]{:S(2)}, u32[]{:S(2)}) collective-permute-start(f32[8,1024]{1,0:T(8,128)S(1)} %shard_map.95), channel_id=1, source_target_pairs={{0,30},{1,31},{2,0},{3,1},{4,2},{5,3},{6,4},{7,5},{8,6},{9,7},{10,... | collective-permute-start | bytes 98312 | tf_op jit(solution)/shard_map/ppermute | solution.py:259
  30.4 0.0 collective-permute-done.1.other_b
  30.4 0.0 collective-permute-done.2.next_pair
  30.4 0.0 all-to-all-done
  30.4 5.3 %shard_map.96 = (bf16[2048,512]{1,0:T(8,128)(2,1)}, f32[8,8,16,128]{3,2,1,0:T(8,128)}, f32[4,1024]{1,0:T(4,128)S(1)}, f32[4,1024]{1,0:T(4,128)S(1)}, f32[4,1024]...) custom-call(s32[1]{0:T(128)} %bitcast.core_ref, f32[1]{0:T(128)S(6)} %copy.10.scale_ref, ...), custom_call_target="tpu_custom_call" | custom-call | flops 3300000000 | bytes 4194304 | tf_op jit(solution)/shard_map/pallas_call | solution.py:261
  35.7 8.5 %all-to-all-start.1 = ((f32[8,8,16,128]{3,2,1,0:T(8,128)}), f32[8,8,16,128]{3,2,1,0:T(8,128)S(1)}, u32[]{:S(2)}, u32[]{:S(2)}) async-start(f32[8,8,16,128]{3,2,1,0:T(8,128)} %get-tuple-element.33), calls=%async_computation.1 | async-start | bytes 1048576 | tf_op jit(solution)/shard_map/all_to_all | solution.py:287
  44.2 4.4 %collective-permute-start.3 = (f32[4,1024]{1,0:T(4,128)S(1)}, f32[4,1024]{1,0:T(4,128)S(1)}, u32[]{:S(2)}, u32[]{:S(2)}) collective-permute-start(f32[4,1024]{1,0:T(4,128)S(1)} %get-tuple-element.36), channel_id=1, source_target_pairs={{0,1},{1,0},{2,3},{3,2},{4,5},{5,4},{6,7},{7,6},{8,9},{9,8},{10,11... | collective-permute-start | bytes 49160 | tf_op jit(solution)/shard_map/ppermute | solution.py:292
  48.6 3.6 %collective-permute-start.4 = (f32[4,1024]{1,0:T(4,128)S(1)}, f32[4,1024]{1,0:T(4,128)S(1)}, u32[]{:S(2)}, u32[]{:S(2)}) collective-permute-start(f32[4,1024]{1,0:T(4,128)S(1)} %get-tuple-element.42), channel_id=1, source_target_pairs={{0,2},{1,3},{2,4},{3,5},{4,6},{5,7},{6,8},{7,9},{8,10},{9,11},{10,... | collective-permute-start | bytes 49160 | tf_op jit(solution)/shard_map/ppermute | solution.py:290
  52.3 3.3 %collective-permute-start.5 = (f32[4,1024]{1,0:T(4,128)S(1)}, f32[4,1024]{1,0:T(4,128)S(1)}, u32[]{:S(2)}, u32[]{:S(2)}) collective-permute-start(f32[4,1024]{1,0:T(4,128)S(1)} %get-tuple-element.43), channel_id=1, source_target_pairs={{0,3},{1,2},{2,5},{3,4},{4,7},{5,6},{6,9},{7,8},{8,11},{9,10},{10,... | collective-permute-start | bytes 49160 | tf_op jit(solution)/shard_map/ppermute | solution.py:291
  55.6 0.0 collective-permute-done.3.came_ref
  55.6 3.2 %shard_map.97 = (f32[256,1024]{1,0:T(8,128)S(1)}, f32[128,1024]{1,0:T(8,128)S(1)}, f32[128,1024]{1,0:T(8,128)S(1)}) custom-call(s32[1]{0:T(128)} %bitcast.core_ref, f32[128,1024]{1,0:T(8,128)S(1)} %bitcast.5, f32[16,1024]{1,0:T(8,128)S(1)} %get-tuple-element.37.window_ref, bf16[2048,512]{1,0:T(8,128)(2,1)} %get-tuple-element.38.slope_hbm), custom_call_target="tpu_custom_call" | custom-call | flops 1700000000 | bytes 5242880 | tf_op jit(solution)/shard_map/pallas_call | solution.py:296
  58.8 0.0 collective-permute-done.4.next_ref
  58.8 3.7 %collective-permute-done.5.far_ref = f32[4,1024]{1,0:T(4,128)S(1)} collective-permute-done((f32[4,1024]{1,0:T(4,128)S(1)}, f32[4,1024]{1,0:T(4,128)S(1)}, u32[]{:S(2)}, u32[]{:S(2)}) %collective-permute-start.5) | collective-permute-done | bytes 16416 | tf_op jit(solution)/shard_map/ppermute | solution.py:291
  62.5 0.0 all-to-all-done.1.parts_ref
  62.5 0.7 shard_map.98
  63.2 3.5 %all-to-all-start.2 = ((f32[8,48,128]{2,1,0:T(8,128)}), f32[8,48,128]{2,1,0:T(8,128)S(1)}, u32[]{:S(2)}, u32[]{:S(2)}) async-start(f32[8,48,128]{2,1,0:T(8,128)} %shard_map.98), calls=%async_computation.2 | async-start | bytes 393216 | tf_op jit(solution)/shard_map/all_to_all | solution.py:312
  66.8 2.9 %collective-permute-start.7 = (f32[128,1024]{1,0:T(8,128)S(1)}, f32[128,1024]{1,0:T(8,128)S(1)}, u32[]{:S(2)}, u32[]{:S(2)}) collective-permute-start(f32[128,1024]{1,0:T(8,128)S(1)} %get-tuple-element.48), channel_id=1, source_target_pairs={{0,1},{1,0},{2,3},{3,2},{4,5},{5,4},{6,7},{7,6},{8,9},{9,8},{10,11... | collective-permute-start | bytes 1572872 | tf_op jit(solution)/shard_map/ppermute | solution.py:318
  69.7 1.9 %collective-permute-start.8 = (f32[128,1024]{1,0:T(8,128)S(1)}, f32[128,1024]{1,0:T(8,128)}, u32[]{:S(2)}, u32[]{:S(2)}) collective-permute-start(f32[128,1024]{1,0:T(8,128)S(1)} %get-tuple-element.49), channel_id=1, source_target_pairs={{0,1},{1,0},{2,3},{3,2},{4,5},{5,4},{6,7},{7,6},{8,9},{9,8},{10,11... | collective-permute-start | bytes 1572872 | tf_op jit(solution)/shard_map/ppermute | solution.py:318
  71.6 3.9 %all-to-all-done.2.parts_ref = f32[8,48,128]{2,1,0:T(8,128)S(1)} async-done(((f32[8,48,128]{2,1,0:T(8,128)}), f32[8,48,128]{2,1,0:T(8,128)S(1)}, u32[]{:S(2)}, u32[]{:S(2)}) %all-to-all-start.2) | async-done | bytes 196640 | tf_op jit(solution)/shard_map/all_to_all | solution.py:312
  75.5 0.7 shard_map.99
  76.2 6.7 %all-to-all-start.3 = ((f32[32,16,128]{2,1,0:T(8,128)}), f32[32,16,128]{2,1,0:T(8,128)S(1)}, u32[]{:S(2)}, u32[]{:S(2)}) async-start(f32[32,16,128]{2,1,0:T(8,128)} %get-tuple-element.51), calls=%async_computation.3 | async-start | bytes 524288 | tf_op jit(solution)/shard_map/all_to_all | solution.py:316
  82.9 5.1 %collective-permute-start.6 = (f32[4,1024]{1,0:T(4,128)S(1)}, f32[4,1024]{1,0:T(4,128)S(1)}, u32[]{:S(2)}, u32[]{:S(2)}) collective-permute-start(f32[4,1024]{1,0:T(4,128)S(1)} %get-tuple-element.44.mine_ref), channel_id=1, source_target_pairs={{0,256},{32,288},{64,320},{96,352},{128,384},{160,416},{192,448},{... | collective-permute-start | bytes 49160 | tf_op jit(solution)/shard_map/ppermute | solution.py:317
  88.0 0.0 collective-permute-done.7
  88.0 0.0 collective-permute-done.8
  88.0 2.1 %maximum_add_fusion = f32[256,1024]{1,0:T(8,128)} fusion(f32[256,1024]{1,0:T(8,128)S(1)} %get-tuple-element.45, f32[128,1024]{1,0:T(8,128)} %collective-permute-done.8, f32[128,1024]{1,0:T(8,128)S(1)} %collective-permute-done.7), kind=kLoop, calls=%fused_computation | loop fusion | flops 524288 | bytes 3145728 | tf_op jit(solution)/shard_map/add | solution.py:319
  90.2 1.6 %collective-permute-done.6.fixed_ref = f32[4,1024]{1,0:T(4,128)S(1)} collective-permute-done((f32[4,1024]{1,0:T(4,128)S(1)}, f32[4,1024]{1,0:T(4,128)S(1)}, u32[]{:S(2)}, u32[]{:S(2)}) %collective-permute-start.6) | collective-permute-done | bytes 16416 | tf_op jit(solution)/shard_map/ppermute | solution.py:317
  91.8 2.4 %all-to-all-done.3.pieces_ref = f32[32,16,128]{2,1,0:T(8,128)S(1)} async-done(((f32[32,16,128]{2,1,0:T(8,128)}), f32[32,16,128]{2,1,0:T(8,128)S(1)}, u32[]{:S(2)}, u32[]{:S(2)}) %all-to-all-start.3) | async-done | bytes 262176 | tf_op jit(solution)/shard_map/all_to_all | solution.py:316
  94.2 0.7 shard_map.100
  (2 shorter events, 0.0 us)
Async XLA Ops:
  0.6 0.8 copy-start
  2.3 28.1 %all-to-all-start = ((f32[16,8,1024]{2,1,0:T(8,128)}), f32[16,8,1024]{2,1,0:T(8,128)S(1)}, u32[]{:S(2)}, u32[]{:S(2)}) async-start(f32[16,8,1024]{2,1,0:T(8,128)} %broadcast_in_dim.2), calls=%async_computation | async-start | bytes 1048576 | tf_op jit(solution)/shard_map/all_to_all | solution.py:242
  17.5 4.8 %collective-permute-start = (f32[136,1024]{1,0:T(8,128)S(1)}, f32[136,1024]{1,0:T(8,128)S(1)}, u32[]{:S(2)}, u32[]{:S(2)}) collective-permute-start(f32[136,1024]{1,0:T(8,128)S(1)} %get-tuple-element.31.own_ref.own_a), channel_id=1, source_target_pairs={{0,1},{1,0},{2,3},{3,2},{4,5},{5,4},{6,7},{7,6},{8,9},{9,8},{10,11... | collective-permute-start | bytes 1671176 | tf_op jit(solution)/shard_map/ppermute | solution.py:248
  20.4 10.0 %collective-permute-start.1 = (f32[128,1024]{1,0:T(8,128)S(1)}, f32[128,1024]{1,0:T(8,128)S(1)}, u32[]{:S(2)}, u32[]{:S(2)}) collective-permute-start(f32[128,1024]{1,0:T(8,128)S(1)} %get-tuple-element.32.own_b), channel_id=1, source_target_pairs={{0,1},{1,0},{2,3},{3,2},{4,5},{5,4},{6,7},{7,6},{8,9},{9,8},{10,11... | collective-permute-start | bytes 1572872 | tf_op jit(solution)/shard_map/ppermute | solution.py:249
  22.4 8.1 %collective-permute-start.2 = (f32[8,1024]{1,0:T(8,128)S(1)}, f32[8,1024]{1,0:T(8,128)S(1)}, u32[]{:S(2)}, u32[]{:S(2)}) collective-permute-start(f32[8,1024]{1,0:T(8,128)S(1)} %shard_map.95), channel_id=1, source_target_pairs={{0,30},{1,31},{2,0},{3,1},{4,2},{5,3},{6,4},{7,5},{8,6},{9,7},{10,... | collective-permute-start | bytes 98312 | tf_op jit(solution)/shard_map/ppermute | solution.py:259
  35.7 26.8 %all-to-all-start.1 = ((f32[8,8,16,128]{3,2,1,0:T(8,128)}), f32[8,8,16,128]{3,2,1,0:T(8,128)S(1)}, u32[]{:S(2)}, u32[]{:S(2)}) async-start(f32[8,8,16,128]{3,2,1,0:T(8,128)} %get-tuple-element.33), calls=%async_computation.1 | async-start | bytes 1048576 | tf_op jit(solution)/shard_map/all_to_all | solution.py:287
  44.2 11.3 %collective-permute-start.3 = (f32[4,1024]{1,0:T(4,128)S(1)}, f32[4,1024]{1,0:T(4,128)S(1)}, u32[]{:S(2)}, u32[]{:S(2)}) collective-permute-start(f32[4,1024]{1,0:T(4,128)S(1)} %get-tuple-element.36), channel_id=1, source_target_pairs={{0,1},{1,0},{2,3},{3,2},{4,5},{5,4},{6,7},{7,6},{8,9},{9,8},{10,11... | collective-permute-start | bytes 49160 | tf_op jit(solution)/shard_map/ppermute | solution.py:292
  48.6 10.2 %collective-permute-start.4 = (f32[4,1024]{1,0:T(4,128)S(1)}, f32[4,1024]{1,0:T(4,128)S(1)}, u32[]{:S(2)}, u32[]{:S(2)}) collective-permute-start(f32[4,1024]{1,0:T(4,128)S(1)} %get-tuple-element.42), channel_id=1, source_target_pairs={{0,2},{1,3},{2,4},{3,5},{4,6},{5,7},{6,8},{7,9},{8,10},{9,11},{10,... | collective-permute-start | bytes 49160 | tf_op jit(solution)/shard_map/ppermute | solution.py:290
  52.3 10.2 %collective-permute-start.5 = (f32[4,1024]{1,0:T(4,128)S(1)}, f32[4,1024]{1,0:T(4,128)S(1)}, u32[]{:S(2)}, u32[]{:S(2)}) collective-permute-start(f32[4,1024]{1,0:T(4,128)S(1)} %get-tuple-element.43), channel_id=1, source_target_pairs={{0,3},{1,2},{2,5},{3,4},{4,7},{5,6},{6,9},{7,8},{8,11},{9,10},{10,... | collective-permute-start | bytes 49160 | tf_op jit(solution)/shard_map/ppermute | solution.py:291
  63.2 12.2 %all-to-all-start.2 = ((f32[8,48,128]{2,1,0:T(8,128)}), f32[8,48,128]{2,1,0:T(8,128)S(1)}, u32[]{:S(2)}, u32[]{:S(2)}) async-start(f32[8,48,128]{2,1,0:T(8,128)} %shard_map.98), calls=%async_computation.2 | async-start | bytes 393216 | tf_op jit(solution)/shard_map/all_to_all | solution.py:312
  66.8 21.3 %collective-permute-start.7 = (f32[128,1024]{1,0:T(8,128)S(1)}, f32[128,1024]{1,0:T(8,128)S(1)}, u32[]{:S(2)}, u32[]{:S(2)}) collective-permute-start(f32[128,1024]{1,0:T(8,128)S(1)} %get-tuple-element.48), channel_id=1, source_target_pairs={{0,1},{1,0},{2,3},{3,2},{4,5},{5,4},{6,7},{7,6},{8,9},{9,8},{10,11... | collective-permute-start | bytes 1572872 | tf_op jit(solution)/shard_map/ppermute | solution.py:318
  69.7 18.3 %collective-permute-start.8 = (f32[128,1024]{1,0:T(8,128)S(1)}, f32[128,1024]{1,0:T(8,128)}, u32[]{:S(2)}, u32[]{:S(2)}) collective-permute-start(f32[128,1024]{1,0:T(8,128)S(1)} %get-tuple-element.49), channel_id=1, source_target_pairs={{0,1},{1,0},{2,3},{3,2},{4,5},{5,4},{6,7},{7,6},{8,9},{9,8},{10,11... | collective-permute-start | bytes 1572872 | tf_op jit(solution)/shard_map/ppermute | solution.py:318
  76.2 18.0 %all-to-all-start.3 = ((f32[32,16,128]{2,1,0:T(8,128)}), f32[32,16,128]{2,1,0:T(8,128)S(1)}, u32[]{:S(2)}, u32[]{:S(2)}) async-start(f32[32,16,128]{2,1,0:T(8,128)} %get-tuple-element.51), calls=%async_computation.3 | async-start | bytes 524288 | tf_op jit(solution)/shard_map/all_to_all | solution.py:316
  82.9 8.9 %collective-permute-start.6 = (f32[4,1024]{1,0:T(4,128)S(1)}, f32[4,1024]{1,0:T(4,128)S(1)}, u32[]{:S(2)}, u32[]{:S(2)}) collective-permute-start(f32[4,1024]{1,0:T(4,128)S(1)} %get-tuple-element.44.mine_ref), channel_id=1, source_target_pairs={{0,256},{32,288},{64,320},{96,352},{128,384},{160,416},{192,448},{... | collective-permute-start | bytes 49160 | tf_op jit(solution)/shard_map/ppermute | solution.py:317

commit v6 on v5

--- a/solution.py
+++ b/solution.py
@@ -291,7 +291,6 @@
         lax.ppermute(send_next, "aud", TO_NEXT_OTHER),
         lax.ppermute(send_self, "aud", OTHER_CORE),
     ]
-    window = lax.optimization_barrier((window, home[2]))[0]
 
     own_grad, *other_grads = call(
         image_kernel,

time: 95.7 us -> 95.9 us (level)
    ppermute x1, starting transfers between devices: 3.27 us -> 6.02 us  [shards(): lax.ppermute(send_next, 'aud', TO_NEXT_OTHER)]
    ppermute x1, starting transfers between devices: 4.38 us -> 1.92 us  [shards(): lax.ppermute(send_self, 'aud', OTHER_CORE)]
where the time goes in v6:
time: 95.9 us; the launch traced here: 95 us
  starting transfers between devices  66 us (69%)
  Pallas kernels  11.9 us (12%)
  waiting for transfers between devices  11.1 us (12%)
  other arithmetic  2.15 us (2%)
  between operations  2.12 us (2%)
  local copies, waits for them, and re-layouts  1.67 us (2%)
    all_to_all x1, starting transfers between devices, shards(): lax.all_to_all(spread, BOTH, 0, 0, tiled=True, axis_index_groups=TEXT_GRO...  13.9 us
    all_to_all x1, starting transfers between devices, shards(): lax.all_to_all(text_parts, BOTH, 0, 0, tiled=True, axis_index_groups=Y_GR...  8.5 us
    all_to_all x1, starting transfers between devices, shards(): pieces = lax.all_to_all(piece, 'aud', 0, 0, tiled=True)  6.88 us
    ppermute x1, starting transfers between devices, shards(): next_pair = lax.ppermute(pair, 'aud', FROM_NEXT)  6.74 us
    ppermute x1, starting transfers between devices, shards(): lax.ppermute(send_next, 'aud', TO_NEXT_OTHER)  6.02 us
    pallas_call x1, Pallas kernels, shards(): call(slope_kernel, [pltpu.HBM((2048, 512), BF16), ((8, 8, 16, 128), F32),...  5.29 us
    ppermute x1, starting transfers between devices, shards(): fixed = lax.ppermute(mine, 'txt', OTHER_HALF)  4.92 us
    ppermute x2, starting transfers between devices, shards(): came_grads = [lax.ppermute(grad, 'aud', OTHER_CORE) for grad in other_grads]  4.85 us
  transfers between devices with their start and end apart: 13, of which 4 were waited for; matrix products, arithmetic and copies ran while one was open for 2% of the time, Pallas kernels for 6%

profile of v6, /device:TPU:1, one launch (start us, length us, event | category | flops | bytes accessed | tf_op | source)
XLA Modules:
  0.0 95.0 jit_solution(1763952419459465280)
XLA Ops:
  0.6 0.0 copy-start
  0.7 0.8 copy-done
  1.5 0.8 broadcast_in_dim.2
  2.3 13.9 %all-to-all-start = ((f32[16,8,1024]{2,1,0:T(8,128)}), f32[16,8,1024]{2,1,0:T(8,128)S(1)}, u32[]{:S(2)}, u32[]{:S(2)}) async-start(f32[16,8,1024]{2,1,0:T(8,128)} %broadcast_in_dim.2), calls=%async_computation | async-start | bytes 1048576 | tf_op jit(solution)/shard_map/all_to_all | solution.py:242
  16.2 1.3 %shard_map.94 = (f32[136,1024]{1,0:T(8,128)S(1)}, f32[128,1024]{1,0:T(8,128)S(1)}) custom-call(f32[256,1024]{1,0:T(8,128)} %images_ref.1, f32[4,1024]{1,0:T(4,128)} %audio_ref, s32[1,256]{1,0:T(1,128)} %bitcast.6, s32[1,256]{1,0:T(1,128)} %bitcast.7), custom_call_target="tpu_custom_call" | custom-call | bytes 1048576 | tf_op jit(solution)/shard_map/pallas_call | solution.py:245
  17.5 2.9 %collective-permute-start = (f32[136,1024]{1,0:T(8,128)S(1)}, f32[136,1024]{1,0:T(8,128)S(1)}, u32[]{:S(2)}, u32[]{:S(2)}) collective-permute-start(f32[136,1024]{1,0:T(8,128)S(1)} %get-tuple-element.30.own_ref.own_a), channel_id=1, source_target_pairs={{0,1},{1,0},{2,3},{3,2},{4,5},{5,4},{6,7},{7,6},{8,9},{9,8},{10,11... | collective-permute-start | bytes 1671176 | tf_op jit(solution)/shard_map/ppermute | solution.py:248
  20.4 1.9 %collective-permute-start.1 = (f32[128,1024]{1,0:T(8,128)S(1)}, f32[128,1024]{1,0:T(8,128)S(1)}, u32[]{:S(2)}, u32[]{:S(2)}) collective-permute-start(f32[128,1024]{1,0:T(8,128)S(1)} %get-tuple-element.31.own_b), channel_id=1, source_target_pairs={{0,1},{1,0},{2,3},{3,2},{4,5},{5,4},{6,7},{7,6},{8,9},{9,8},{10,11... | collective-permute-start | bytes 1572872 | tf_op jit(solution)/shard_map/ppermute | solution.py:249
  22.3 0.0 collective-permute-done.far_ref.other_a
  22.4 6.7 %collective-permute-start.2 = (f32[8,1024]{1,0:T(8,128)S(1)}, f32[8,1024]{1,0:T(8,128)S(1)}, u32[]{:S(2)}, u32[]{:S(2)}) collective-permute-start(f32[8,1024]{1,0:T(8,128)S(1)} %shard_map.95), channel_id=1, source_target_pairs={{0,30},{1,31},{2,0},{3,1},{4,2},{5,3},{6,4},{7,5},{8,6},{9,7},{10,... | collective-permute-start | bytes 98312 | tf_op jit(solution)/shard_map/ppermute | solution.py:259
  30.4 0.0 collective-permute-done.1.other_b
  30.4 0.0 collective-permute-done.2.next_pair
  30.4 0.0 all-to-all-done
  30.4 5.3 %shard_map.96 = (bf16[2048,512]{1,0:T(8,128)(2,1)}, f32[8,8,16,128]{3,2,1,0:T(8,128)}, f32[4,1024]{1,0:T(4,128)S(1)}, f32[4,1024]{1,0:T(4,128)S(1)}, f32[4,1024]...) custom-call(s32[1]{0:T(128)} %bitcast.core_ref, f32[1]{0:T(128)S(6)} %copy.10.scale_ref, ...), custom_call_target="tpu_custom_call" | custom-call | flops 3300000000 | bytes 4194304 | tf_op jit(solution)/shard_map/pallas_call | solution.py:261
  35.7 8.5 %all-to-all-start.1 = ((f32[8,8,16,128]{3,2,1,0:T(8,128)}), f32[8,8,16,128]{3,2,1,0:T(8,128)S(1)}, u32[]{:S(2)}, u32[]{:S(2)}) async-start(f32[8,8,16,128]{3,2,1,0:T(8,128)} %get-tuple-element.32), calls=%async_computation.1 | async-start | bytes 1048576 | tf_op jit(solution)/shard_map/all_to_all | solution.py:287
  44.2 3.4 %collective-permute-start.3 = (f32[4,1024]{1,0:T(4,128)S(1)}, f32[4,1024]{1,0:T(4,128)S(1)}, u32[]{:S(2)}, u32[]{:S(2)}) collective-permute-start(f32[4,1024]{1,0:T(4,128)S(1)} %get-tuple-element.39), channel_id=1, source_target_pairs={{0,2},{1,3},{2,4},{3,5},{4,6},{5,7},{6,8},{7,9},{8,10},{9,11},{10,... | collective-permute-start | bytes 49160 | tf_op jit(solution)/shard_map/ppermute | solution.py:290
  47.6 6.0 %collective-permute-start.4 = (f32[4,1024]{1,0:T(4,128)S(1)}, f32[4,1024]{1,0:T(4,128)S(1)}, u32[]{:S(2)}, u32[]{:S(2)}) collective-permute-start(f32[4,1024]{1,0:T(4,128)S(1)} %get-tuple-element.40), channel_id=1, source_target_pairs={{0,3},{1,2},{2,5},{3,4},{4,7},{5,6},{6,9},{7,8},{8,11},{9,10},{10,... | collective-permute-start | bytes 49160 | tf_op jit(solution)/shard_map/ppermute | solution.py:291
  53.6 1.9 %collective-permute-start.5 = (f32[4,1024]{1,0:T(4,128)S(1)}, f32[4,1024]{1,0:T(4,128)S(1)}, u32[]{:S(2)}, u32[]{:S(2)}) collective-permute-start(f32[4,1024]{1,0:T(4,128)S(1)} %get-tuple-element.41), channel_id=1, source_target_pairs={{0,1},{1,0},{2,3},{3,2},{4,5},{5,4},{6,7},{7,6},{8,9},{9,8},{10,11... | collective-permute-start | bytes 49160 | tf_op jit(solution)/shard_map/ppermute | solution.py:292
  55.6 3.2 %shard_map.97 = (f32[256,1024]{1,0:T(8,128)S(1)}, f32[128,1024]{1,0:T(8,128)S(1)}, f32[128,1024]{1,0:T(8,128)S(1)}) custom-call(s32[1]{0:T(128)} %bitcast.core_ref, f32[128,1024]{1,0:T(8,128)S(1)} %bitcast.5, f32[16,1024]{1,0:T(8,128)S(1)} %get-tuple-element.34.window_ref, bf16[2048,512]{1,0:T(8,128)(2,1)} %get-tuple-element.35.slope_hbm), custom_call_target="tpu_custom_call" | custom-call | flops 1700000000 | bytes 5242880 | tf_op jit(solution)/shard_map/pallas_call | solution.py:295
  58.8 0.0 collective-permute-done.3.next_ref
  58.8 3.0 %collective-permute-done.4.far_ref = f32[4,1024]{1,0:T(4,128)S(1)} collective-permute-done((f32[4,1024]{1,0:T(4,128)S(1)}, f32[4,1024]{1,0:T(4,128)S(1)}, u32[]{:S(2)}, u32[]{:S(2)}) %collective-permute-start.4) | collective-permute-done | bytes 16416 | tf_op jit(solution)/shard_map/ppermute | solution.py:291
  61.8 0.0 collective-permute-done.5.came_ref
  61.9 0.0 all-to-all-done.1.parts_ref
  61.9 0.7 shard_map.98
  62.6 4.2 %all-to-all-start.2 = ((f32[8,48,128]{2,1,0:T(8,128)}), f32[8,48,128]{2,1,0:T(8,128)S(1)}, u32[]{:S(2)}, u32[]{:S(2)}) async-start(f32[8,48,128]{2,1,0:T(8,128)} %shard_map.98), calls=%async_computation.2 | async-start | bytes 393216 | tf_op jit(solution)/shard_map/all_to_all | solution.py:311
  66.8 2.9 %collective-permute-start.7 = (f32[128,1024]{1,0:T(8,128)S(1)}, f32[128,1024]{1,0:T(8,128)S(1)}, u32[]{:S(2)}, u32[]{:S(2)}) collective-permute-start(f32[128,1024]{1,0:T(8,128)S(1)} %get-tuple-element.46), channel_id=1, source_target_pairs={{0,1},{1,0},{2,3},{3,2},{4,5},{5,4},{6,7},{7,6},{8,9},{9,8},{10,11... | collective-permute-start | bytes 1572872 | tf_op jit(solution)/shard_map/ppermute | solution.py:317
  69.7 1.9 %collective-permute-start.8 = (f32[128,1024]{1,0:T(8,128)S(1)}, f32[128,1024]{1,0:T(8,128)}, u32[]{:S(2)}, u32[]{:S(2)}) collective-permute-start(f32[128,1024]{1,0:T(8,128)S(1)} %get-tuple-element.47), channel_id=1, source_target_pairs={{0,1},{1,0},{2,3},{3,2},{4,5},{5,4},{6,7},{7,6},{8,9},{9,8},{10,11... | collective-permute-start | bytes 1572872 | tf_op jit(solution)/shard_map/ppermute | solution.py:317
  71.6 3.9 %all-to-all-done.2.parts_ref = f32[8,48,128]{2,1,0:T(8,128)S(1)} async-done(((f32[8,48,128]{2,1,0:T(8,128)}), f32[8,48,128]{2,1,0:T(8,128)S(1)}, u32[]{:S(2)}, u32[]{:S(2)}) %all-to-all-start.2) | async-done | bytes 196640 | tf_op jit(solution)/shard_map/all_to_all | solution.py:311
  75.5 0.7 shard_map.99
  76.2 6.9 %all-to-all-start.3 = ((f32[32,16,128]{2,1,0:T(8,128)}), f32[32,16,128]{2,1,0:T(8,128)S(1)}, u32[]{:S(2)}, u32[]{:S(2)}) async-start(f32[32,16,128]{2,1,0:T(8,128)} %get-tuple-element.49), calls=%async_computation.3 | async-start | bytes 524288 | tf_op jit(solution)/shard_map/all_to_all | solution.py:315
  83.1 4.9 %collective-permute-start.6 = (f32[4,1024]{1,0:T(4,128)S(1)}, f32[4,1024]{1,0:T(4,128)S(1)}, u32[]{:S(2)}, u32[]{:S(2)}) collective-permute-start(f32[4,1024]{1,0:T(4,128)S(1)} %get-tuple-element.42.mine_ref), channel_id=1, source_target_pairs={{0,256},{32,288},{64,320},{96,352},{128,384},{160,416},{192,448},{... | collective-permute-start | bytes 49160 | tf_op jit(solution)/shard_map/ppermute | solution.py:316
  88.0 0.0 collective-permute-done.7
  88.0 0.0 collective-permute-done.8
  88.0 2.1 %maximum_add_fusion = f32[256,1024]{1,0:T(8,128)} fusion(f32[256,1024]{1,0:T(8,128)S(1)} %get-tuple-element.43, f32[128,1024]{1,0:T(8,128)} %collective-permute-done.8, f32[128,1024]{1,0:T(8,128)S(1)} %collective-permute-done.7), kind=kLoop, calls=%fused_computation | loop fusion | flops 524288 | bytes 3145728 | tf_op jit(solution)/shard_map/add | solution.py:318
  90.2 1.6 %collective-permute-done.6.fixed_ref = f32[4,1024]{1,0:T(4,128)S(1)} collective-permute-done((f32[4,1024]{1,0:T(4,128)S(1)}, f32[4,1024]{1,0:T(4,128)S(1)}, u32[]{:S(2)}, u32[]{:S(2)}) %collective-permute-start.6) | collective-permute-done | bytes 16416 | tf_op jit(solution)/shard_map/ppermute | solution.py:316
  91.8 2.5 %all-to-all-done.3.pieces_ref = f32[32,16,128]{2,1,0:T(8,128)S(1)} async-done(((f32[32,16,128]{2,1,0:T(8,128)}), f32[32,16,128]{2,1,0:T(8,128)S(1)}, u32[]{:S(2)}, u32[]{:S(2)}) %all-to-all-start.3) | async-done | bytes 262176 | tf_op jit(solution)/shard_map/all_to_all | solution.py:315
  94.4 0.7 shard_map.100
  (2 shorter events, 0.0 us)
Async XLA Ops:
  0.6 0.8 copy-start
  2.3 28.1 %all-to-all-start = ((f32[16,8,1024]{2,1,0:T(8,128)}), f32[16,8,1024]{2,1,0:T(8,128)S(1)}, u32[]{:S(2)}, u32[]{:S(2)}) async-start(f32[16,8,1024]{2,1,0:T(8,128)} %broadcast_in_dim.2), calls=%async_computation | async-start | bytes 1048576 | tf_op jit(solution)/shard_map/all_to_all | solution.py:242
  17.5 4.8 %collective-permute-start = (f32[136,1024]{1,0:T(8,128)S(1)}, f32[136,1024]{1,0:T(8,128)S(1)}, u32[]{:S(2)}, u32[]{:S(2)}) collective-permute-start(f32[136,1024]{1,0:T(8,128)S(1)} %get-tuple-element.30.own_ref.own_a), channel_id=1, source_target_pairs={{0,1},{1,0},{2,3},{3,2},{4,5},{5,4},{6,7},{7,6},{8,9},{9,8},{10,11... | collective-permute-start | bytes 1671176 | tf_op jit(solution)/shard_map/ppermute | solution.py:248
  20.4 10.0 %collective-permute-start.1 = (f32[128,1024]{1,0:T(8,128)S(1)}, f32[128,1024]{1,0:T(8,128)S(1)}, u32[]{:S(2)}, u32[]{:S(2)}) collective-permute-start(f32[128,1024]{1,0:T(8,128)S(1)} %get-tuple-element.31.own_b), channel_id=1, source_target_pairs={{0,1},{1,0},{2,3},{3,2},{4,5},{5,4},{6,7},{7,6},{8,9},{9,8},{10,11... | collective-permute-start | bytes 1572872 | tf_op jit(solution)/shard_map/ppermute | solution.py:249
  22.4 8.1 %collective-permute-start.2 = (f32[8,1024]{1,0:T(8,128)S(1)}, f32[8,1024]{1,0:T(8,128)S(1)}, u32[]{:S(2)}, u32[]{:S(2)}) collective-permute-start(f32[8,1024]{1,0:T(8,128)S(1)} %shard_map.95), channel_id=1, source_target_pairs={{0,30},{1,31},{2,0},{3,1},{4,2},{5,3},{6,4},{7,5},{8,6},{9,7},{10,... | collective-permute-start | bytes 98312 | tf_op jit(solution)/shard_map/ppermute | solution.py:259
  35.7 26.1 %all-to-all-start.1 = ((f32[8,8,16,128]{3,2,1,0:T(8,128)}), f32[8,8,16,128]{3,2,1,0:T(8,128)S(1)}, u32[]{:S(2)}, u32[]{:S(2)}) async-start(f32[8,8,16,128]{3,2,1,0:T(8,128)} %get-tuple-element.32), calls=%async_computation.1 | async-start | bytes 1048576 | tf_op jit(solution)/shard_map/all_to_all | solution.py:287
  44.2 14.6 %collective-permute-start.3 = (f32[4,1024]{1,0:T(4,128)S(1)}, f32[4,1024]{1,0:T(4,128)S(1)}, u32[]{:S(2)}, u32[]{:S(2)}) collective-permute-start(f32[4,1024]{1,0:T(4,128)S(1)} %get-tuple-element.39), channel_id=1, source_target_pairs={{0,2},{1,3},{2,4},{3,5},{4,6},{5,7},{6,8},{7,9},{8,10},{9,11},{10,... | collective-permute-start | bytes 49160 | tf_op jit(solution)/shard_map/ppermute | solution.py:290
  47.6 14.2 %collective-permute-start.4 = (f32[4,1024]{1,0:T(4,128)S(1)}, f32[4,1024]{1,0:T(4,128)S(1)}, u32[]{:S(2)}, u32[]{:S(2)}) collective-permute-start(f32[4,1024]{1,0:T(4,128)S(1)} %get-tuple-element.40), channel_id=1, source_target_pairs={{0,3},{1,2},{2,5},{3,4},{4,7},{5,6},{6,9},{7,8},{8,11},{9,10},{10,... | collective-permute-start | bytes 49160 | tf_op jit(solution)/shard_map/ppermute | solution.py:291
  53.6 8.2 %collective-permute-start.5 = (f32[4,1024]{1,0:T(4,128)S(1)}, f32[4,1024]{1,0:T(4,128)S(1)}, u32[]{:S(2)}, u32[]{:S(2)}) collective-permute-start(f32[4,1024]{1,0:T(4,128)S(1)} %get-tuple-element.41), channel_id=1, source_target_pairs={{0,1},{1,0},{2,3},{3,2},{4,5},{5,4},{6,7},{7,6},{8,9},{9,8},{10,11... | collective-permute-start | bytes 49160 | tf_op jit(solution)/shard_map/ppermute | solution.py:292
  62.6 12.9 %all-to-all-start.2 = ((f32[8,48,128]{2,1,0:T(8,128)}), f32[8,48,128]{2,1,0:T(8,128)S(1)}, u32[]{:S(2)}, u32[]{:S(2)}) async-start(f32[8,48,128]{2,1,0:T(8,128)} %shard_map.98), calls=%async_computation.2 | async-start | bytes 393216 | tf_op jit(solution)/shard_map/all_to_all | solution.py:311
  66.8 21.3 %collective-permute-start.7 = (f32[128,1024]{1,0:T(8,128)S(1)}, f32[128,1024]{1,0:T(8,128)S(1)}, u32[]{:S(2)}, u32[]{:S(2)}) collective-permute-start(f32[128,1024]{1,0:T(8,128)S(1)} %get-tuple-element.46), channel_id=1, source_target_pairs={{0,1},{1,0},{2,3},{3,2},{4,5},{5,4},{6,7},{7,6},{8,9},{9,8},{10,11... | collective-permute-start | bytes 1572872 | tf_op jit(solution)/shard_map/ppermute | solution.py:317
  69.7 18.3 %collective-permute-start.8 = (f32[128,1024]{1,0:T(8,128)S(1)}, f32[128,1024]{1,0:T(8,128)}, u32[]{:S(2)}, u32[]{:S(2)}) collective-permute-start(f32[128,1024]{1,0:T(8,128)S(1)} %get-tuple-element.47), channel_id=1, source_target_pairs={{0,1},{1,0},{2,3},{3,2},{4,5},{5,4},{6,7},{7,6},{8,9},{9,8},{10,11... | collective-permute-start | bytes 1572872 | tf_op jit(solution)/shard_map/ppermute | solution.py:317
  76.2 18.2 %all-to-all-start.3 = ((f32[32,16,128]{2,1,0:T(8,128)}), f32[32,16,128]{2,1,0:T(8,128)S(1)}, u32[]{:S(2)}, u32[]{:S(2)}) async-start(f32[32,16,128]{2,1,0:T(8,128)} %get-tuple-element.49), calls=%async_computation.3 | async-start | bytes 524288 | tf_op jit(solution)/shard_map/all_to_all | solution.py:315
  83.1 8.7 %collective-permute-start.6 = (f32[4,1024]{1,0:T(4,128)S(1)}, f32[4,1024]{1,0:T(4,128)S(1)}, u32[]{:S(2)}, u32[]{:S(2)}) collective-permute-start(f32[4,1024]{1,0:T(4,128)S(1)} %get-tuple-element.42.mine_ref), channel_id=1, source_target_pairs={{0,256},{32,288},{64,320},{96,352},{128,384},{160,416},{192,448},{... | collective-permute-start | bytes 49160 | tf_op jit(solution)/shard_map/ppermute | solution.py:316
